TPU v7x, 32 devices: a whole 2x2x4 slice. The times are simulated.
32 devices in a mesh: dp: 4 (over y, core), section: 2 (over x), ctx: 4 (over z).
Axes of the slice: x: 2, y: 2, z: 4, core: 2. Of those that a mesh axis runs over, the one named last changes fastest.
Arguments:
- queries: bfloat16 [2, 4, 512, 4096], P('section', 'dp', 'ctx'), may hold values from -30 to 30
- keys_values: bfloat16 [2, 4, 512, 1024], P('section', 'dp', 'ctx'), may hold values from -30 to 30
- random_blocks: int32 [4, 4, 4, 4], P('dp'), may hold values from 0 to 3, as said below
- global_blocks: int32 [4, 2], P('dp'), may hold values from 0 to 3
- doc_lengths: int32 [4, 4], P('dp'), may hold values from 1 to 256, 512 in all within a row
- cotangent: bfloat16 [2, 4, 512, 4096], P('section', 'dp', 'ctx'), may hold values from -1.5 to 1.5
Outputs:
- stream: bfloat16 [2, 4, 512, 4096], P('section', 'dp', 'ctx')
- gain_grad: float32 [2, 4096], P('section')
Inputs may be any that keep to these rules, and one draw needn't show every extreme that they name: `random_blocks`: for each query block, its 4 x 4 entries over all key heads name every block of the sequence exactly 4 times.
All inputs are finite; a program needn't handle non-finite values.
Results may differ from a plain program's by a relative error of at most 0.0062.
Values may be sent and summed in bfloat16 or wider, within the bound.
No kernel may reach another device: no remote copies, remote signals or barrier semaphores. Data moves between devices by JAX's collectives and lax.ppermute only.
A program may use at most 64 MiB of HBM per device.

v0:
```python
import math

import jax
import jax.numpy as jnp
from jax import lax
from jax.sharding import PartitionSpec as P

HEADS = 32
KVH = 4
HD = 128
RAND = 4
GLOBALS = 2
GROUP = 8


def passed_along(value, axis, steps):
    count = lax.axis_size(axis)
    initial, last = (max(0, -steps), min(count, count - steps))
    return lax.ppermute(value, axis, [(source, source + steps) for source in range(initial, last)])


def by_heads(row_block):
    row_count = row_block.shape[0]
    split_rows = row_block.reshape(row_count, 2, KVH, HD)
    return jnp.transpose(split_rows, (2, 0, 1, 3)).reshape(KVH, row_count, 2 * HD)


def doc_index(doc_ends, positions):
    return jnp.sum((doc_ends <= positions[..., None]).astype(jnp.int32), axis=-1)


def attend_head(operands):
    query_rows, key_rows, value_rows, allowed = operands
    scores = jnp.einsum(
        "qgd,kd->gqk", query_rows, key_rows, preferred_element_type=jnp.float32
    ) / math.sqrt(HD)
    scores = jnp.where(allowed[None], scores, -1e30)
    row_max = jnp.max(scores, axis=-1, keepdims=True)
    weights = jnp.where(allowed[None], jnp.exp(scores - row_max), 0.0)
    weight_sum = jnp.sum(weights, axis=-1)
    product = jnp.einsum(
        "gqk,kd->qgd", weights.astype(jnp.bfloat16), value_rows, preferred_element_type=jnp.float32
    )
    return product / jnp.transpose(weight_sum)[:, :, None]


def per_device(queries, keys_values, random_blocks, global_blocks, doc_lengths, cotangent):
    ctx_count = lax.axis_size("ctx")
    ctx_place = lax.axis_index("ctx")
    local_kv = keys_values[0, 0]
    block_rows = local_kv.shape[0]
    seq_len = ctx_count * block_rows
    block_table = random_blocks[0]
    own_lists = lax.dynamic_index_in_dim(block_table, ctx_place, 0, keepdims=False)
    globals_ids = global_blocks[0]
    whole_kv = lax.all_gather(local_kv, "ctx", axis=0, tiled=True)
    padded = jnp.pad(whole_kv, ((block_rows, block_rows), (0, 0)))
    window_kv = lax.dynamic_slice_in_dim(padded, ctx_place * block_rows, 3 * block_rows, 0)
    global_kv = jnp.concatenate(
        [
            lax.dynamic_slice_in_dim(whole_kv, globals_ids[global_slot] * block_rows, block_rows, 0)
            for global_slot in range(GLOBALS)
        ],
        axis=0,
    )
    blocked = whole_kv.reshape(ctx_count, block_rows, 2, KVH, HD)
    head_index = jnp.arange(KVH, dtype=jnp.int32)
    random_kv = blocked[own_lists, :, :, head_index[:, None]].reshape(
        KVH, RAND * block_rows, 2 * HD
    )
    shared_kv = by_heads(jnp.concatenate([window_kv, global_kv], axis=0))
    all_kv = jnp.concatenate([shared_kv, random_kv], axis=1)
    row_steps = jnp.arange(block_rows, dtype=jnp.int32)
    window_pos = (ctx_place - 1) * block_rows + jnp.arange(3 * block_rows, dtype=jnp.int32)
    global_pos = (globals_ids[:, None] * block_rows + row_steps[None, :]).reshape(-1)
    shared_pos = jnp.concatenate([window_pos, global_pos])
    random_pos = (own_lists[:, :, None] * block_rows + row_steps).reshape(KVH, -1)
    doc_ends = jnp.cumsum(doc_lengths[0])
    query_doc = doc_index(doc_ends, ctx_place * block_rows + row_steps)
    shared_ok = (shared_pos >= 0) & (shared_pos < seq_len)
    shared_ok = shared_ok[None, :] & (
        doc_index(doc_ends, shared_pos)[None, :] == query_doc[:, None]
    )
    random_ok = doc_index(doc_ends, random_pos)[:, None, :] == query_doc[None, :, None]
    allowed = jnp.concatenate(
        [jnp.broadcast_to(shared_ok[None], (KVH,) + shared_ok.shape), random_ok], axis=2
    )
    query_heads = jnp.transpose(queries[0, 0].reshape(block_rows, KVH, GROUP, HD), (1, 0, 2, 3))
    attention = lax.map(attend_head, (query_heads, all_kv[:, :, :HD], all_kv[:, :, HD:], allowed))
    attention = jnp.transpose(attention, (1, 0, 2, 3)).reshape(block_rows, HEADS * HD)
    rounded_out = attention.astype(jnp.bfloat16)
    section_place = lax.axis_index("section")
    section_count = lax.axis_size("section")
    handed = rounded_out
    for section_step in range(1, section_count):
        arrived = passed_along(handed, "section", 1)
        updated = (arrived.astype(jnp.float32) + rounded_out.astype(jnp.float32)).astype(
            jnp.bfloat16
        )
        handed = jnp.where(section_place == section_step, updated, handed)
    widened = handed.astype(jnp.float32)
    inverse = lax.rsqrt(jnp.mean(widened * widened, axis=-1, keepdims=True) + 1e-06)
    gradient_term = jnp.sum(
        cotangent[0, 0].astype(jnp.float32) * widened * inverse, axis=0
    ) / lax.axis_size("dp")
    gain_grad = lax.psum(gradient_term, ("dp", "ctx"))
    return (handed[None, None], gain_grad[None])


def solution(mesh):
    in_specs = (
        P("section", "dp", "ctx", None),
        P("section", "dp", "ctx", None),
        P("dp", None, None, None),
        P("dp", None),
        P("dp", None),
        P("section", "dp", "ctx", None),
    )
    out_specs = (P("section", "dp", "ctx", None), P("section", None))
    return jax.shard_map(
        per_device, mesh=mesh, in_specs=in_specs, out_specs=out_specs, check_vma=False
    )
```

profile of v0, /device:TPU:0, one launch (start us, length us, event | category | flops | bytes accessed | tf_op | source)
XLA Modules:
  0.0 189.9 jit_solution(18233723689298900807)
XLA Ops:
  13.6 2.3 %copy.30 = bf16[1,1,128,4096]{2,3,1,0:T(8,128)(2,1)} copy(bf16[1,1,128,4096]{3,2,1,0:T(8,128)(2,1)} %param.8) | data formatting | bytes 2097152 | tf_op args[0]
  17.8 22.5 %all-gather.3.cloned.1.call-done = bf16[1,1,512,1024]{3,2,1,0:T(8,128)(2,1)} async-done(((bf16[1,1,128,1024]{3,2,1,0:T(8,128)(2,1)}), bf16[1,1,512,1024]{3,2,1,0:T(8,128)(2,1)}) %all-gather.3.cloned.1.call-update) | async-done | bytes 1048592 | tf_op jit(solution)/shard_map/all_gather | solution.py:56
  41.8 1.8 reshape.210
  43.6 2.3 %copy.41 = bf16[640,2,4,128]{3,1,0,2:T(2,128)(2,1)S(1)} copy(bf16[640,2,4,128]{3,2,1,0:T(4,128)(2,1)} %reshape.210) | data formatting | bytes 2621440 | tf_op jit(solution)/shard_map/reshape | solution.py:24
  45.9 1.7 reshape.211
  49.0 1.6 reshape.212
  52.1 1.7 gather_fusion
  53.7 3.3 %copy.29 = bf16[16,128,2,128]{3,2,1,0:T(2,128)(2,1)} copy(bf16[16,128,2,128]{3,1,2,0:T(8,128)(2,1)} %gather_fusion) | data formatting | bytes 2097152 | tf_op jit(solution)/shard_map/gather | solution.py:68
  57.1 1.7 reshape.213
  58.9 1.8 fusion.70
  60.7 33.2 %while.10 = (s32[]{:T(128)}, bf16[4,128,8,128]{1,3,2,0:T(8,128)(2,1)}, bf16[4,1152,128]{2,1,0:T(8,128)(2,1)}, pred[4,128,1152]{1,2,0:T(8,128)(4,1)}, bf16[4,1152...) while((s32[]{:T(128)}, bf16[4,128,8,128]{1,3,2,0:T(8,128)(2,1)}, ...), condition=%wide.region_7.8_spmd, body=%wide.region_4.7_spmd.sunk | while | flops 917900544 | bytes 11218057 | solution.py:89
  61.7 3.1 %fusion.86 = f32[8,128]{1,0:T(8,128)S(1)} fusion(pred[128,1152]{0,1:T(8,128)(4,1)S(1)} %dynamic-slice_bitcast_fusion.4, bf16[4,1152,128]{2,1,0:T(8,128)(2,1)} %get-tuple-element.134, s32[]{:T(128)} %get-tuple-element.123, bf16[4,128,8,128]{1,3,2,0:T(8,128)(2,1)} %get-tuple-element.135), kind=kOutput, calls=%fused_computation.71.clone.1 | convolution fusion | flops 307889280 | bytes 857088 | tf_op jit(solution)/shard_map/while/body/eval_jaxpr/sub | solution.py:39
  64.8 3.2 %fusion.87 = bf16[4,128,8,128]{1,3,2,0:T(8,128)(2,1)S(1)} fusion(bf16[4,128,8,128]{1,3,2,0:T(8,128)(2,1)S(1)} %copy-done.3, s32[]{:T(128)} %get-tuple-element.123, bf16[4,1152,128]{2,1,0:T(8,128)(2,1)} %get-tuple-element.132, f32[128,8]{0,1:T(8,128)S(1)} %bitcast.134, pred[128,1152]{0,1:T(8,128)(4,1)S(1)} %dynamic-slice_bitcast_fusion.4, ...), kind=kOutput, calls=%fused_computation.14.clone.1 | convolution fusion | flops 610011264 | bytes 1677312 | tf_op jit(solution)/shard_map/while/body/eval_jaxpr/gqk,kd->qgd/dot_general | solution.py:41
  70.0 3.1 %fusion.86 = f32[8,128]{1,0:T(8,128)S(1)} fusion(pred[128,1152]{0,1:T(8,128)(4,1)S(1)} %dynamic-slice_bitcast_fusion.4, bf16[4,1152,128]{2,1,0:T(8,128)(2,1)} %get-tuple-element.134, s32[]{:T(128)} %get-tuple-element.123, bf16[4,128,8,128]{1,3,2,0:T(8,128)(2,1)} %get-tuple-element.135), kind=kOutput, calls=%fused_computation.71.clone.1 | convolution fusion | flops 307889280 | bytes 857088 | tf_op jit(solution)/shard_map/while/body/eval_jaxpr/sub | solution.py:39
  73.1 3.2 %fusion.87 = bf16[4,128,8,128]{1,3,2,0:T(8,128)(2,1)S(1)} fusion(bf16[4,128,8,128]{1,3,2,0:T(8,128)(2,1)S(1)} %copy-done.3, s32[]{:T(128)} %get-tuple-element.123, bf16[4,1152,128]{2,1,0:T(8,128)(2,1)} %get-tuple-element.132, f32[128,8]{0,1:T(8,128)S(1)} %bitcast.134, pred[128,1152]{0,1:T(8,128)(4,1)S(1)} %dynamic-slice_bitcast_fusion.4, ...), kind=kOutput, calls=%fused_computation.14.clone.1 | convolution fusion | flops 610011264 | bytes 1677312 | tf_op jit(solution)/shard_map/while/body/eval_jaxpr/gqk,kd->qgd/dot_general | solution.py:41
  78.3 3.1 %fusion.86 = f32[8,128]{1,0:T(8,128)S(1)} fusion(pred[128,1152]{0,1:T(8,128)(4,1)S(1)} %dynamic-slice_bitcast_fusion.4, bf16[4,1152,128]{2,1,0:T(8,128)(2,1)} %get-tuple-element.134, s32[]{:T(128)} %get-tuple-element.123, bf16[4,128,8,128]{1,3,2,0:T(8,128)(2,1)} %get-tuple-element.135), kind=kOutput, calls=%fused_computation.71.clone.1 | convolution fusion | flops 307889280 | bytes 857088 | tf_op jit(solution)/shard_map/while/body/eval_jaxpr/sub | solution.py:39
  81.4 3.2 %fusion.87 = bf16[4,128,8,128]{1,3,2,0:T(8,128)(2,1)S(1)} fusion(bf16[4,128,8,128]{1,3,2,0:T(8,128)(2,1)S(1)} %copy-done.3, s32[]{:T(128)} %get-tuple-element.123, bf16[4,1152,128]{2,1,0:T(8,128)(2,1)} %get-tuple-element.132, f32[128,8]{0,1:T(8,128)S(1)} %bitcast.134, pred[128,1152]{0,1:T(8,128)(4,1)S(1)} %dynamic-slice_bitcast_fusion.4, ...), kind=kOutput, calls=%fused_computation.14.clone.1 | convolution fusion | flops 610011264 | bytes 1677312 | tf_op jit(solution)/shard_map/while/body/eval_jaxpr/gqk,kd->qgd/dot_general | solution.py:41
  86.6 3.1 %fusion.86 = f32[8,128]{1,0:T(8,128)S(1)} fusion(pred[128,1152]{0,1:T(8,128)(4,1)S(1)} %dynamic-slice_bitcast_fusion.4, bf16[4,1152,128]{2,1,0:T(8,128)(2,1)} %get-tuple-element.134, s32[]{:T(128)} %get-tuple-element.123, bf16[4,128,8,128]{1,3,2,0:T(8,128)(2,1)} %get-tuple-element.135), kind=kOutput, calls=%fused_computation.71.clone.1 | convolution fusion | flops 307889280 | bytes 857088 | tf_op jit(solution)/shard_map/while/body/eval_jaxpr/sub | solution.py:39
  89.7 3.2 %fusion.87 = bf16[4,128,8,128]{1,3,2,0:T(8,128)(2,1)S(1)} fusion(bf16[4,128,8,128]{1,3,2,0:T(8,128)(2,1)S(1)} %copy-done.3, s32[]{:T(128)} %get-tuple-element.123, bf16[4,1152,128]{2,1,0:T(8,128)(2,1)} %get-tuple-element.132, f32[128,8]{0,1:T(8,128)S(1)} %bitcast.134, pred[128,1152]{0,1:T(8,128)(4,1)S(1)} %dynamic-slice_bitcast_fusion.4, ...), kind=kOutput, calls=%fused_computation.14.clone.1 | convolution fusion | flops 610011264 | bytes 1677312 | tf_op jit(solution)/shard_map/while/body/eval_jaxpr/gqk,kd->qgd/dot_general | solution.py:41
  93.9 1.5 copy.35
  95.4 4.5 %collective-permute-start = (bf16[128,4096]{1,0:T(8,128)(2,1)S(1)}, bf16[128,4096]{1,0:T(8,128)(2,1)}, u32[]{:S(2)}, u32[]{:S(2)}) collective-permute-start(bf16[128,4096]{1,0:T(8,128)(2,1)S(1)} %copy.35), channel_id=1, source_target_pairs={{0,4},{1,5},{2,6},{3,7},{8,12},{9,13},{10,14},{11,15},{16,20},{17,... | collective-permute-start | bytes 3145736 | tf_op jit(solution)/shard_map/ppermute | solution.py:19
  99.9 21.3 %collective-permute-done = bf16[128,4096]{1,0:T(8,128)(2,1)} collective-permute-done((bf16[128,4096]{1,0:T(8,128)(2,1)S(1)}, bf16[128,4096]{1,0:T(8,128)(2,1)}, u32[]{:S(2)}, u32[]{:S(2)}) %collective-permute-start) | collective-permute-done | bytes 1048608 | tf_op jit(solution)/shard_map/ppermute | solution.py:19
  121.2 1.7 fusion.59
  123.4 59.7 %psum.7 = f32[1,4096]{1,0:T(1,128)} all-reduce(f32[1,4096]{1,0:T(1,128)S(1)} %bitcast.129), channel_id=1, replica_groups=mesh['dp'=4,'section'=2,'ctx'=4] {'dp','ctx'}, use_global_device_ids=true, to_apply=%region_10.11 | all-reduce | flops 4096 | bytes 32768 | tf_op jit(solution)/shard_map/psum | solution.py:106
  (59 shorter events, 19.4 us)
Async XLA Ops:
  7.2 33.1 %all-gather.3.cloned.1.call-start = ((), (), s32[]{:S(2)}) async-start(), calls=%async_computation | async-start | bytes 1310720 | tf_op jit(solution)/shard_map/all_gather | solution.py:56
  40.2 1.4 copy-start
  61.7 3.2 %copy-start.3 = (bf16[4,128,8,128]{1,3,2,0:T(8,128)(2,1)S(1)}, bf16[4,128,8,128]{1,3,2,0:T(8,128)(2,1)}, u32[]{:S(2)}) copy-start(bf16[4,128,8,128]{1,3,2,0:T(8,128)(2,1)} %get-tuple-element.124) | copy-start | bytes 3145732 | tf_op jit(solution)/shard_map/while
  68.1 1.0 copy-start.4
  70.0 3.2 %copy-start.3 = (bf16[4,128,8,128]{1,3,2,0:T(8,128)(2,1)S(1)}, bf16[4,128,8,128]{1,3,2,0:T(8,128)(2,1)}, u32[]{:S(2)}) copy-start(bf16[4,128,8,128]{1,3,2,0:T(8,128)(2,1)} %get-tuple-element.124) | copy-start | bytes 3145732 | tf_op jit(solution)/shard_map/while
  76.4 1.0 copy-start.4
  78.3 3.2 %copy-start.3 = (bf16[4,128,8,128]{1,3,2,0:T(8,128)(2,1)S(1)}, bf16[4,128,8,128]{1,3,2,0:T(8,128)(2,1)}, u32[]{:S(2)}) copy-start(bf16[4,128,8,128]{1,3,2,0:T(8,128)(2,1)} %get-tuple-element.124) | copy-start | bytes 3145732 | tf_op jit(solution)/shard_map/while
  84.7 1.0 copy-start.4
  86.6 3.2 %copy-start.3 = (bf16[4,128,8,128]{1,3,2,0:T(8,128)(2,1)S(1)}, bf16[4,128,8,128]{1,3,2,0:T(8,128)(2,1)}, u32[]{:S(2)}) copy-start(bf16[4,128,8,128]{1,3,2,0:T(8,128)(2,1)} %get-tuple-element.124) | copy-start | bytes 3145732 | tf_op jit(solution)/shard_map/while
  93.0 1.0 copy-start.4
  95.4 27.6 %copy-start.2 = (bf16[1,1,128,4096]{3,2,1,0:T(8,128)(2,1)S(1)}, bf16[1,1,128,4096]{3,2,1,0:T(8,128)(2,1)}, u32[]{:S(2)}) copy-start(bf16[1,1,128,4096]{3,2,1,0:T(8,128)(2,1)} %param.13) | copy-start | bytes 3145732
  95.4 25.8 %collective-permute-start = (bf16[128,4096]{1,0:T(8,128)(2,1)S(1)}, bf16[128,4096]{1,0:T(8,128)(2,1)}, u32[]{:S(2)}, u32[]{:S(2)}) collective-permute-start(bf16[128,4096]{1,0:T(8,128)(2,1)S(1)} %copy.35), channel_id=1, source_target_pairs={{0,4},{1,5},{2,6},{3,7},{8,12},{9,13},{10,14},{11,15},{16,20},{17,... | collective-permute-start | bytes 3145736 | tf_op jit(solution)/shard_map/ppermute | solution.py:19
  123.0 60.1 %copy-start.1 = (bf16[128,4096]{1,0:T(8,128)(2,1)}, bf16[128,4096]{1,0:T(8,128)(2,1)S(1)}, u32[]{:S(2)}) copy-start(bf16[128,4096]{1,0:T(8,128)(2,1)S(1)} %get-tuple-element.72) | copy-start | bytes 3145732
Sparse Core Ops, SparseCore 0:
  9.6 30.6 all-gather.2
where the time goes:
time: 191 us; the launch traced here: 190 us
  blocking collectives  59.7 us (31%)
  waiting for transfers between devices  44.4 us (23%)
  local copies, waits for them, and re-layouts  33.3 us (17%)
  matrix products  25.5 us (13%)
  between operations  15.5 us (8%)
  other arithmetic  6.9 us (4%)
  starting transfers between devices  4.55 us (2%)
    psum x1, blocking collectives, per_device(): gain_grad = lax.psum(gradient_term, ('dp', 'ctx'))  59.7 us
    all_gather x1, waiting for transfers between devices, per_device(): whole_kv = lax.all_gather(local_kv, 'ctx', axis=0, tiled=True)  22.5 us
    ppermute x1, waiting for transfers between devices, passed_along(): lax.ppermute(value, axis, [(source, source + steps) for source in range(i...  21.3 us
    dot_general x4, matrix products, attend_head(): jnp.einsum('gqk,kd->qgd', weights.astype(jnp.bfloat16), value_rows, prefe...  12.9 us
    sub x4, matrix products, attend_head(): weights = jnp.where(allowed[None], jnp.exp(scores - row_max), 0.0)  12.6 us
    gather x2, local copies, waits for them, and re-layouts, per_device(): blocked[own_lists, :, :, head_index[:, None]]  5.02 us
    ppermute x1, starting transfers between devices, passed_along(): lax.ppermute(value, axis, [(source, source + steps) for source in range(i...  4.52 us
    reshape x2, local copies, waits for them, and re-layouts, by_heads(): split_rows = row_block.reshape(row_count, 2, KVH, HD)  4.13 us
  transfers between devices with their start and end apart: 2, of which 2 were waited for; matrix products, arithmetic and copies ran while one was open for 4% of the time, Pallas kernels for 0%

commit v1 on v0

v1 whole, which is shorter than its diff:
```python
import functools
import math

import jax
import jax.numpy as jnp
from jax import lax
from jax.experimental import pallas as pl
from jax.experimental.pallas import tpu as pltpu
from jax.sharding import PartitionSpec as P

HEADS = 32
KVH = 4
HD = 128
RAND = 4
GLOBALS = 2
GROUP = 8
PART = 2
PARTS = KVH // PART
NEVER = -1e30
SCALE = math.log2(math.e) / math.sqrt(HD)
VMEM = pl.BlockSpec(memory_space=pltpu.VMEM)
SMEM = pl.BlockSpec(memory_space=pltpu.SMEM)


def count_docs(doc_ends, positions):
    found = jnp.zeros(positions.shape, jnp.int32)
    for end in doc_ends:
        found += (positions >= end).astype(jnp.int32)
    return found


def attend_kernel(part, place_ref, lists_ref, globals_ref, docs_ref, q_ref, *refs):
    kv_refs, out_ref = refs[:-1], refs[-1]
    rows = q_ref.shape[0]
    place = place_ref[0]
    doc_ends, end = [], 0
    for doc in range(docs_ref.shape[1]):
        end = end + docs_ref[0, doc]
        doc_ends.append(end)
    query_doc = count_docs(doc_ends, place * rows + lax.broadcasted_iota(jnp.int32, (rows, 1), 0))
    blocks, same = [], []
    for slot in range(len(kv_refs)):
        block = place ^ slot
        key_doc = count_docs(doc_ends, block * rows + lax.broadcasted_iota(jnp.int32, (1, rows), 1))
        blocks.append(block)
        same.append(query_doc == key_doc)
    for index in range(PART):
        head = part * PART + index
        biases = []
        for block, same_doc in zip(blocks, same):
            times = (jnp.abs(block - place) <= 1).astype(jnp.int32)
            for slot in range(GLOBALS):
                times += (globals_ref[0, slot] == block).astype(jnp.int32)
            for slot in range(RAND):
                times += (lists_ref[0, place, head, slot] == block).astype(jnp.int32)
            level = jnp.log2(jnp.full((1, rows), times, jnp.int32).astype(jnp.float32))
            biases.append(jnp.where(same_doc & (times > 0), level, NEVER))
        bias = jnp.concatenate(biases, axis=1)
        bias = jnp.concatenate([bias, bias], axis=0)
        keys = jnp.concatenate([ref[:, pl.ds(index * HD, HD)] for ref in kv_refs], axis=0)
        values = jnp.concatenate([ref[:, pl.ds((PART + index) * HD, HD)] for ref in kv_refs], axis=0)
        values = jnp.concatenate([values, jnp.ones_like(values)], axis=1)
        for pair in range(GROUP // 2):
            first = (index * GROUP + 2 * pair) * HD
            query = jnp.concatenate(
                [q_ref[:, pl.ds(first, HD)], q_ref[:, pl.ds(first + HD, HD)]], axis=0
            )
            scores = lax.dot_general(
                query, keys, (((1,), (1,)), ((), ())), preferred_element_type=jnp.float32
            )
            scores = scores * SCALE + bias
            weights = jnp.exp2(scores - jnp.max(scores, axis=1, keepdims=True))
            product = jnp.dot(
                weights.astype(jnp.bfloat16), values, preferred_element_type=jnp.float32
            )
            result = (product[:, :HD] / product[:, HD:]).astype(jnp.bfloat16)
            out_ref[:, pl.ds(first, HD)] = result[:rows]
            out_ref[:, pl.ds(first + HD, HD)] = result[rows:]


def attend(part, scalars, queries, kv_slots):
    rows = queries.shape[0]
    width = PART * GROUP * HD
    keys = rows * len(kv_slots)
    return pl.pallas_call(
        functools.partial(attend_kernel, part),
        out_shape=jax.ShapeDtypeStruct((rows, width), jnp.bfloat16),
        grid=(1,),
        in_specs=[SMEM] * 4
        + [pl.BlockSpec((rows, width), lambda step: (0, part))]
        + [VMEM] * len(kv_slots),
        out_specs=VMEM,
        compiler_params=pltpu.CompilerParams(vmem_limit_bytes=40 << 20),
        cost_estimate=pl.CostEstimate(
            flops=4 * rows * width * keys,
            bytes_accessed=4 * rows * width + 4 * keys * PART * HD,
            transcendentals=rows * PART * GROUP * keys,
        ),
        name="attend",
    )(*scalars, queries, *kv_slots)


def finish_kernel(scale, last_ref, cotangent_ref, *refs):
    arrived_refs, handed_refs = refs[:PARTS], refs[PARTS : 2 * PARTS]
    stream_ref, share_ref = refs[2 * PARTS :]
    rows, width = handed_refs[0].shape
    is_last = last_ref[0] == 1
    squares = jnp.zeros((rows, HD), jnp.float32)
    for part in range(PARTS):
        for column in range(0, width, HD):
            handed = handed_refs[part][:, pl.ds(column, HD)].astype(jnp.float32)
            arrived = arrived_refs[part][:, pl.ds(column, HD)].astype(jnp.float32)
            total = jnp.where(is_last, handed + arrived, handed).astype(jnp.bfloat16)
            stream_ref[:, pl.ds(part * width + column, HD)] = total
            widened = total.astype(jnp.float32)
            squares += widened * widened
    mean = jnp.sum(squares, axis=1, keepdims=True) / (PARTS * width)
    inverse = lax.rsqrt(mean + 1e-06) * scale
    for tile in range(PARTS * width // HD):
        columns = pl.ds(tile * HD, HD)
        term = cotangent_ref[:, columns].astype(jnp.float32) * stream_ref[:, columns].astype(jnp.float32)
        share_ref[pl.ds(tile, 1), :] = jnp.sum(term * inverse, axis=0, keepdims=True)


def finish(is_last, cotangent, arrived, handed, scale):
    rows, features = cotangent.shape
    return pl.pallas_call(
        functools.partial(finish_kernel, scale),
        out_shape=(
            jax.ShapeDtypeStruct((rows, features), jnp.bfloat16),
            jax.ShapeDtypeStruct((features // HD, HD), jnp.float32),
        ),
        in_specs=[SMEM] + [VMEM] * (1 + 2 * PARTS),
        out_specs=(VMEM, VMEM),
        compiler_params=pltpu.CompilerParams(vmem_limit_bytes=40 << 20),
        cost_estimate=pl.CostEstimate(
            flops=10 * rows * features, bytes_accessed=8 * rows * features, transcendentals=rows
        ),
        name="finish",
    )(is_last, cotangent, *arrived, *handed)


def swapped_sum(value, axis):
    count = lax.axis_size(axis)
    distance = 1
    while distance < count:
        value = value + lax.ppermute(value, axis, [(place, place ^ distance) for place in range(count)])
        distance *= 2
    return value


def gather_slots(value):
    count = lax.axis_size("ctx")
    slots = [value]
    for slot in range(1, count):
        pairs = [
            (place, place ^ slot)
            for place in range(count)
            if abs(place - (place ^ slot)) <= count // 2
        ]
        slots.append(lax.ppermute(value, "ctx", pairs))
    return slots


def per_device(queries, keys_values, random_blocks, global_blocks, doc_lengths, cotangent):
    queries, keys_values, cotangent = queries[0, 0], keys_values[0, 0], cotangent[0, 0]
    place = lax.axis_index("ctx").astype(jnp.int32).reshape(1)
    scalars = (place, random_blocks, global_blocks, doc_lengths)
    section_count = lax.axis_size("section")
    section_place = lax.axis_index("section")
    half = KVH * HD
    step_width = PART * HD
    slots = []
    for part in range(PARTS):
        first = part * step_width
        kv = jnp.concatenate(
            [
                keys_values[:, first : first + step_width],
                keys_values[:, half + first : half + first + step_width],
            ],
            axis=1,
        )
        slots.append(gather_slots(kv))
    handed, arrived = [], []
    for part in range(PARTS):
        handed.append(attend(part, scalars, queries, slots[part]))
        arrived.append(lax.ppermute(handed[part], "section", [(0, 1), (1, 0)]))
    for step in range(2, section_count):
        on_step = section_place == step - 1
        for part in range(PARTS):
            total = handed[part].astype(jnp.float32) + arrived[part].astype(jnp.float32)
            handed[part] = jnp.where(on_step, total.astype(jnp.bfloat16), handed[part])
            arrived[part] = lax.ppermute(handed[part], "section", [(step - 1, step), (step, step - 1)])
    is_last = (section_place == section_count - 1).astype(jnp.int32).reshape(1)
    stream, share = finish(is_last, cotangent, arrived, handed, 1.0 / lax.axis_size("dp"))
    gain_grad = swapped_sum(swapped_sum(share, "dp"), "ctx")
    return (stream[None, None], gain_grad.reshape(1, HEADS * HD))


def solution(mesh):
    in_specs = (
        P("section", "dp", "ctx", None),
        P("section", "dp", "ctx", None),
        P("dp", None, None, None),
        P("dp", None),
        P("dp", None),
        P("section", "dp", "ctx", None),
    )
    out_specs = (P("section", "dp", "ctx", None), P("section", None))
    return jax.shard_map(
        per_device, mesh=mesh, in_specs=in_specs, out_specs=out_specs, check_vma=False
    )
```

time: 191 us -> 61.2 us (0.32)
  blocking collectives: 59.7 us -> 0 us
  local copies, waits for them, and re-layouts: 33.3 us -> 1.72 us
  matrix products: 25.5 us -> 0 us
  starting transfers between devices: 4.55 us -> 22 us
  waiting for transfers between devices: 44.4 us -> 28.3 us
  between operations: 15.5 us -> 0.73 us
  Pallas kernels: 0 us -> 7.52 us
  other arithmetic: 6.9 us -> 0.64 us
    psum x1 -> x0, blocking collectives: 59.7 us -> none  [per_device(): gain_grad = lax.psum(gradient_term, ('dp', 'ctx'))]
    all_gather x1 -> x0, waiting for transfers between devices: 22.5 us -> none  [per_device(): whole_kv = lax.all_gather(local_kv, 'ctx', axis=0, tiled=True)]
    ppermute x1 -> x12, starting transfers between devices: 4.52 us -> 22 us  [the longest x6 14.1 us: gather_slots(): slots.append(lax.ppermute(value, 'ctx', pairs))]
    dot_general x4 -> x0, matrix products: 12.9 us -> none  [attend_head(): jnp.einsum('gqk,kd->qgd', weights.astype(jnp.bfloat16), value_rows, prefe...]
    sub x4 -> x0, matrix products: 12.6 us -> none  [attend_head(): weights = jnp.where(allowed[None], jnp.exp(scores - row_max), 0.0)]
    reshape x6 -> x0, local copies, waits for them, and re-layouts: 10.6 us -> none  [the longest x2 4.13 us: by_heads(): split_rows = row_block.reshape(row_count, 2, KVH, HD)]
    pallas_call x0 -> x3, Pallas kernels: none -> 7.52 us  [the longest x2 4.81 us: attend(): pl.pallas_call(functools.partial(attend_kernel, part), out_shape=jax.Shap...]
    ppermute x1 -> x12, waiting for transfers between devices: 21.3 us -> 28.3 us  [the longest x2 14.9 us: per_device(): arrived.append(lax.ppermute(handed[part], 'section', [(0, 1), (1, 0)]))]
  transfers between devices with their start and end apart: 2 -> 12, of which waited for: 2 -> 7; matrix products, arithmetic and copies ran while one was open for 4% -> 0% of each run, Pallas kernels for 0% -> 8%
where the time goes in v1:
time: 61.2 us; the launch traced here: 61 us
  waiting for transfers between devices  28.3 us (46%)
  starting transfers between devices  22 us (36%)
  Pallas kernels  7.52 us (12%)
  local copies, waits for them, and re-layouts  1.72 us (3%)
  between operations  0.73 us (1%)
  other arithmetic  0.64 us (1%)
    ppermute x2, waiting for transfers between devices, per_device(): arrived.append(lax.ppermute(handed[part], 'section', [(0, 1), (1, 0)]))  14.9 us
    ppermute x6, starting transfers between devices, gather_slots(): slots.append(lax.ppermute(value, 'ctx', pairs))  14.1 us
    ppermute x4, waiting for transfers between devices, swapped_sum(): lax.ppermute(value, axis, [(place, place ^ distance) for place in range(c...  8.4 us
    ppermute x6, waiting for transfers between devices, gather_slots(): slots.append(lax.ppermute(value, 'ctx', pairs))  5.07 us
    ppermute x4, starting transfers between devices, swapped_sum(): lax.ppermute(value, axis, [(place, place ^ distance) for place in range(c...  4.9 us
    pallas_call x2, Pallas kernels, attend(): pl.pallas_call(functools.partial(attend_kernel, part), out_shape=jax.Shap...  4.81 us
    ppermute x2, starting transfers between devices, per_device(): arrived.append(lax.ppermute(handed[part], 'section', [(0, 1), (1, 0)]))  3.05 us
    pallas_call x1, Pallas kernels, finish(): pl.pallas_call(functools.partial(finish_kernel, scale), out_shape=(jax.Sh...  2.71 us
  transfers between devices with their start and end apart: 12, of which 7 were waited for; matrix products, arithmetic and copies ran while one was open for 0% of the time, Pallas kernels for 8%

profile of v1, /device:TPU:0, one launch (start us, length us, event | category | flops | bytes accessed | tf_op | source)
XLA Modules:
  0.0 61.0 jit_solution(12993412232355880957)
XLA Ops:
  0.6 1.0 %fusion = (bf16[128,256]{1,0:T(8,128)(2,1)S(1)}, bf16[128,256]{1,0:T(8,128)(2,1)S(1)}, bf16[128,256]{1,0:T(8,128)(2,1)S(1)}, bf16[128,256]{1,0:T(8,128)(2,1)S(1)}) fusion(bf16[128,1024]{1,0:T(8,128)(2,1)} %bitcast.10), kind=kLoop, calls=%fused_computation.2 | loop fusion | bytes 524288 | tf_op jit(solution)/shard_map/slice | solution.py:178
  1.7 0.7 %collective-permute-start.6 = (bf16[128,512]{1,0:T(8,128)(2,1)S(1)}, bf16[128,512]{1,0:T(8,128)(2,1)S(1)}, u32[]{:S(2)}, u32[]{:S(2)}) collective-permute-start(bf16[128,512]{1,0:T(8,128)(2,1)S(1)} %pad_maximum_fusion.1.refs_0_), channel_id=1, source_target_pairs={{1,2},{2,1},{5,6},{6,5},{9,10},{10,9},{13,14},{14,13},{17,18},{18,... | collective-permute-start | bytes 393224 | tf_op jit(solution)/shard_map/ppermute | solution.py:161
  2.4 5.8 %collective-permute-start.5 = (bf16[128,512]{1,0:T(8,128)(2,1)S(1)}, bf16[128,512]{1,0:T(8,128)(2,1)S(1)}, u32[]{:S(2)}, u32[]{:S(2)}) collective-permute-start(bf16[128,512]{1,0:T(8,128)(2,1)S(1)} %pad_maximum_fusion.1.refs_0_), channel_id=1, source_target_pairs={{0,2},{1,3},{2,0},{3,1},{4,6},{5,7},{6,4},{7,5},{8,10},{9,11},{10,... | collective-permute-start | bytes 393224 | tf_op jit(solution)/shard_map/ppermute | solution.py:161
  8.2 0.2 collective-permute-start.4
  8.4 0.7 %collective-permute-start.2 = (bf16[128,512]{1,0:T(8,128)(2,1)S(1)}, bf16[128,512]{1,0:T(8,128)(2,1)S(1)}, u32[]{:S(2)}, u32[]{:S(2)}) collective-permute-start(bf16[128,512]{1,0:T(8,128)(2,1)S(1)} %pad_maximum_fusion.refs_0_), channel_id=1, source_target_pairs={{1,2},{2,1},{5,6},{6,5},{9,10},{10,9},{13,14},{14,13},{17,18},{18,... | collective-permute-start | bytes 393224 | tf_op jit(solution)/shard_map/ppermute | solution.py:161
  9.1 4.6 %collective-permute-start.1 = (bf16[128,512]{1,0:T(8,128)(2,1)S(1)}, bf16[128,512]{1,0:T(8,128)(2,1)S(1)}, u32[]{:S(2)}, u32[]{:S(2)}) collective-permute-start(bf16[128,512]{1,0:T(8,128)(2,1)S(1)} %pad_maximum_fusion.refs_0_), channel_id=1, source_target_pairs={{0,2},{1,3},{2,0},{3,1},{4,6},{5,7},{6,4},{7,5},{8,10},{9,11},{10,... | collective-permute-start | bytes 393224 | tf_op jit(solution)/shard_map/ppermute | solution.py:161
  13.7 2.1 %collective-permute-start = (bf16[128,512]{1,0:T(8,128)(2,1)S(1)}, bf16[128,512]{1,0:T(8,128)(2,1)}, u32[]{:S(2)}, u32[]{:S(2)}) collective-permute-start(bf16[128,512]{1,0:T(8,128)(2,1)S(1)} %pad_maximum_fusion.refs_0_), channel_id=1, source_target_pairs={{0,1},{1,0},{2,3},{3,2},{4,5},{5,4},{6,7},{7,6},{8,9},{9,8},{10,11... | collective-permute-start | bytes 393224 | tf_op jit(solution)/shard_map/ppermute | solution.py:161
  15.8 5.1 %collective-permute-done.5.refs_2_ = bf16[128,512]{1,0:T(8,128)(2,1)S(1)} collective-permute-done((bf16[128,512]{1,0:T(8,128)(2,1)S(1)}, bf16[128,512]{1,0:T(8,128)(2,1)S(1)}, u32[]{:S(2)}, u32[]{:S(2)}) %collective-permute-start.5) | collective-permute-done | bytes 131104 | tf_op jit(solution)/shard_map/ppermute | solution.py:161
  20.9 0.6 %copy-done.3 = s32[1,2]{1,0:T(1,128)S(1)} copy-done((s32[1,2]{1,0:T(1,128)S(1)}, s32[1,2]{1,0:T(1,128)}, u32[]{:S(2)}) %copy-start.3) | copy-done | bytes 32
  21.5 2.3 %attend.3.refs_3_ = bf16[128,2048]{1,0:T(8,128)(2,1)S(1)} custom-call(s32[1]{0:T(128)} %bitcast.2.place_ref, s32[1,4,4,4]{3,2,1,0:T(4,128)S(1)} %copy-done.2, s32[1,2]{1,0:T(1,128)S(1)} %copy-done.3, s32[1,4]{1,0:T(1,128)S(1)} %copy-done.4, bf16[128,4096]{1,0:T(8,128)(2,1)S(1)} %bitcast.7, bf16[128,512]{1,0:T(8,128)(2,1)S(1)} %pad_maximum_fusion.1.refs_0_, ...), custom_call_target="tpu_custom_call" | custom-call | flops 536870912 | bytes 1572864 | tf_op jit(solution)/shard_map/attend/pallas_call | solution.py:85
  23.8 1.6 %collective-permute-start.7 = (bf16[128,2048]{1,0:T(8,128)(2,1)S(1)}, bf16[128,2048]{1,0:T(8,128)(2,1)}, u32[]{:S(2)}, u32[]{:S(2)}) collective-permute-start(bf16[128,2048]{1,0:T(8,128)(2,1)S(1)} %attend.3.refs_3_), channel_id=1, source_target_pairs={{0,4},{4,0},{1,5},{5,1},{2,6},{6,2},{3,7},{7,3},{8,12},{12,8},{9,1... | collective-permute-start | bytes 1572872 | tf_op jit(solution)/shard_map/ppermute | solution.py:187
  25.4 2.5 %attend.2.refs_2_ = bf16[128,2048]{1,0:T(8,128)(2,1)S(1)} custom-call(s32[1]{0:T(128)} %bitcast.2.place_ref, s32[1,4,4,4]{3,2,1,0:T(4,128)S(1)} %copy-done.2, s32[1,2]{1,0:T(1,128)S(1)} %copy-done.3, s32[1,4]{1,0:T(1,128)S(1)} %copy-done.4, bf16[128,4096]{1,0:T(8,128)(2,1)S(1)} %bitcast.8, bf16[128,512]{1,0:T(8,128)(2,1)S(1)} %pad_maximum_fusion.refs_0_, ...), custom_call_target="tpu_custom_call" | custom-call | flops 536870912 | bytes 1572864 | tf_op jit(solution)/shard_map/attend/pallas_call | solution.py:85
  27.9 1.5 %collective-permute-start.3 = (bf16[128,2048]{1,0:T(8,128)(2,1)S(1)}, bf16[128,2048]{1,0:T(8,128)(2,1)S(1)}, u32[]{:S(2)}, u32[]{:S(2)}) collective-permute-start(bf16[128,2048]{1,0:T(8,128)(2,1)S(1)} %attend.2.refs_2_), channel_id=1, source_target_pairs={{0,4},{4,0},{1,5},{5,1},{2,6},{6,2},{3,7},{7,3},{8,12},{12,8},{9,1... | collective-permute-start | bytes 1572872 | tf_op jit(solution)/shard_map/ppermute | solution.py:187
  29.4 7.2 %collective-permute-done.7.refs_1_ = bf16[128,2048]{1,0:T(8,128)(2,1)} collective-permute-done((bf16[128,2048]{1,0:T(8,128)(2,1)S(1)}, bf16[128,2048]{1,0:T(8,128)(2,1)}, u32[]{:S(2)}, u32[]{:S(2)}) %collective-permute-start.7) | collective-permute-done | bytes 524320 | tf_op jit(solution)/shard_map/ppermute | solution.py:187
  36.7 7.6 %collective-permute-done.3.refs_0_ = bf16[128,2048]{1,0:T(8,128)(2,1)S(1)} collective-permute-done((bf16[128,2048]{1,0:T(8,128)(2,1)S(1)}, bf16[128,2048]{1,0:T(8,128)(2,1)S(1)}, u32[]{:S(2)}, u32[]{:S(2)}) %collective-permute-start.3) | collective-permute-done | bytes 524320 | tf_op jit(solution)/shard_map/ppermute | solution.py:187
  44.3 2.7 %finish.1 = (bf16[128,4096]{1,0:T(8,128)(2,1)}, f32[32,128]{1,0:T(8,128)S(1)}) custom-call(s32[1]{0:T(128)} %bitcast.last_ref, bf16[128,4096]{1,0:T(8,128)(2,1)S(1)} %bitcast.9, bf16[128,2048]{1,0:T(8,128)(2,1)S(1)} %collective-permute-done.3.refs_0_, bf16[128,2048]{1,0:T(8,128)(2,1)} %collective-permute-done.7.refs_1_, ...), custom_call_target="tpu_custom_call" | custom-call | flops 5242880 | bytes 4194304 | tf_op jit(solution)/shard_map/finish/pallas_call | solution.py:127
  47.0 1.2 %collective-permute-done.8 = f32[32,128]{1,0:T(8,128)S(1)} collective-permute-done((f32[32,128]{1,0:T(8,128)S(1)}, f32[32,128]{1,0:T(8,128)S(1)}, u32[]{:S(2)}, u32[]{:S(2)}) %collective-permute-start.8) | collective-permute-done | bytes 16416 | tf_op jit(solution)/shard_map/ppermute | solution.py:147
  48.2 1.5 %collective-permute-start.9 = (f32[32,128]{1,0:T(8,128)S(1)}, f32[32,128]{1,0:T(8,128)S(1)}, u32[]{:S(2)}, u32[]{:S(2)}) collective-permute-start(f32[32,128]{1,0:T(8,128)S(1)} %add.12), channel_id=1, source_target_pairs={{0,16},{8,24},{16,0},{24,8},{1,17},{9,25},{17,1},{25,9},{2,18},{10... | collective-permute-start | bytes 49160 | tf_op jit(solution)/shard_map/ppermute | solution.py:147
  49.7 2.2 %collective-permute-done.9 = f32[32,128]{1,0:T(8,128)S(1)} collective-permute-done((f32[32,128]{1,0:T(8,128)S(1)}, f32[32,128]{1,0:T(8,128)S(1)}, u32[]{:S(2)}, u32[]{:S(2)}) %collective-permute-start.9) | collective-permute-done | bytes 16416 | tf_op jit(solution)/shard_map/ppermute | solution.py:147
  52.0 0.8 %collective-permute-start.10 = (f32[32,128]{1,0:T(8,128)S(1)}, f32[32,128]{1,0:T(8,128)S(1)}, u32[]{:S(2)}, u32[]{:S(2)}) collective-permute-start(f32[32,128]{1,0:T(8,128)S(1)} %add.13), channel_id=1, source_target_pairs={{0,1},{1,0},{2,3},{3,2},{4,5},{5,4},{6,7},{7,6},{8,9},{9,8},{10,11... | collective-permute-start | bytes 49160 | tf_op jit(solution)/shard_map/ppermute | solution.py:147
  52.7 3.0 %collective-permute-done.10 = f32[32,128]{1,0:T(8,128)S(1)} collective-permute-done((f32[32,128]{1,0:T(8,128)S(1)}, f32[32,128]{1,0:T(8,128)S(1)}, u32[]{:S(2)}, u32[]{:S(2)}) %collective-permute-start.10) | collective-permute-done | bytes 16416 | tf_op jit(solution)/shard_map/ppermute | solution.py:147
  55.7 2.6 %collective-permute-start.11 = (f32[32,128]{1,0:T(8,128)S(1)}, f32[32,128]{1,0:T(8,128)S(1)}, u32[]{:S(2)}, u32[]{:S(2)}) collective-permute-start(f32[32,128]{1,0:T(8,128)S(1)} %add.14), channel_id=1, source_target_pairs={{0,2},{1,3},{2,0},{3,1},{4,6},{5,7},{6,4},{7,5},{8,10},{9,11},{10,... | collective-permute-start | bytes 49160 | tf_op jit(solution)/shard_map/ppermute | solution.py:147
  58.3 2.0 %collective-permute-done.11 = f32[32,128]{1,0:T(8,128)S(1)} collective-permute-done((f32[32,128]{1,0:T(8,128)S(1)}, f32[32,128]{1,0:T(8,128)S(1)}, u32[]{:S(2)}, u32[]{:S(2)}) %collective-permute-start.11) | collective-permute-done | bytes 16416 | tf_op jit(solution)/shard_map/ppermute | solution.py:147
  60.4 0.6 add.15
  (20 shorter events, 0.1 us)
Async XLA Ops:
  0.6 20.3 %copy-start = (bf16[1,1,128,4096]{3,2,1,0:T(8,128)(2,1)S(1)}, bf16[1,1,128,4096]{3,2,1,0:T(8,128)(2,1)}, u32[]{:S(2)}) copy-start(bf16[1,1,128,4096]{3,2,1,0:T(8,128)(2,1)} %param.6) | copy-start | bytes 3145732
  1.7 12.0 %collective-permute-start.6 = (bf16[128,512]{1,0:T(8,128)(2,1)S(1)}, bf16[128,512]{1,0:T(8,128)(2,1)S(1)}, u32[]{:S(2)}, u32[]{:S(2)}) collective-permute-start(bf16[128,512]{1,0:T(8,128)(2,1)S(1)} %pad_maximum_fusion.1.refs_0_), channel_id=1, source_target_pairs={{1,2},{2,1},{5,6},{6,5},{9,10},{10,9},{13,14},{14,13},{17,18},{18,... | collective-permute-start | bytes 393224 | tf_op jit(solution)/shard_map/ppermute | solution.py:161
  2.4 18.5 %collective-permute-start.5 = (bf16[128,512]{1,0:T(8,128)(2,1)S(1)}, bf16[128,512]{1,0:T(8,128)(2,1)S(1)}, u32[]{:S(2)}, u32[]{:S(2)}) collective-permute-start(bf16[128,512]{1,0:T(8,128)(2,1)S(1)} %pad_maximum_fusion.1.refs_0_), channel_id=1, source_target_pairs={{0,2},{1,3},{2,0},{3,1},{4,6},{5,7},{6,4},{7,5},{8,10},{9,11},{10,... | collective-permute-start | bytes 393224 | tf_op jit(solution)/shard_map/ppermute | solution.py:161
  8.2 12.7 %collective-permute-start.4 = (bf16[128,512]{1,0:T(8,128)(2,1)S(1)}, bf16[128,512]{1,0:T(8,128)(2,1)S(1)}, u32[]{:S(2)}, u32[]{:S(2)}) collective-permute-start(bf16[128,512]{1,0:T(8,128)(2,1)S(1)} %pad_maximum_fusion.1.refs_0_), channel_id=1, source_target_pairs={{0,1},{1,0},{2,3},{3,2},{4,5},{5,4},{6,7},{7,6},{8,9},{9,8},{10,11... | collective-permute-start | bytes 393224 | tf_op jit(solution)/shard_map/ppermute | solution.py:161
  8.4 12.5 %copy-start.2 = (s32[1,4,4,4]{3,2,1,0:T(4,128)S(1)}, s32[1,4,4,4]{3,2,1,0:T(4,128)}, u32[]{:S(2)}) copy-start(s32[1,4,4,4]{3,2,1,0:T(4,128)} %lists_ref.3) | copy-start | bytes 772
  8.4 17.0 %collective-permute-start.2 = (bf16[128,512]{1,0:T(8,128)(2,1)S(1)}, bf16[128,512]{1,0:T(8,128)(2,1)S(1)}, u32[]{:S(2)}, u32[]{:S(2)}) collective-permute-start(bf16[128,512]{1,0:T(8,128)(2,1)S(1)} %pad_maximum_fusion.refs_0_), channel_id=1, source_target_pairs={{1,2},{2,1},{5,6},{6,5},{9,10},{10,9},{13,14},{14,13},{17,18},{18,... | collective-permute-start | bytes 393224 | tf_op jit(solution)/shard_map/ppermute | solution.py:161
  9.1 16.3 %collective-permute-start.1 = (bf16[128,512]{1,0:T(8,128)(2,1)S(1)}, bf16[128,512]{1,0:T(8,128)(2,1)S(1)}, u32[]{:S(2)}, u32[]{:S(2)}) collective-permute-start(bf16[128,512]{1,0:T(8,128)(2,1)S(1)} %pad_maximum_fusion.refs_0_), channel_id=1, source_target_pairs={{0,2},{1,3},{2,0},{3,1},{4,6},{5,7},{6,4},{7,5},{8,10},{9,11},{10,... | collective-permute-start | bytes 393224 | tf_op jit(solution)/shard_map/ppermute | solution.py:161
  13.7 11.7 %collective-permute-start = (bf16[128,512]{1,0:T(8,128)(2,1)S(1)}, bf16[128,512]{1,0:T(8,128)(2,1)}, u32[]{:S(2)}, u32[]{:S(2)}) collective-permute-start(bf16[128,512]{1,0:T(8,128)(2,1)S(1)} %pad_maximum_fusion.refs_0_), channel_id=1, source_target_pairs={{0,1},{1,0},{2,3},{3,2},{4,5},{5,4},{6,7},{7,6},{8,9},{9,8},{10,11... | collective-permute-start | bytes 393224 | tf_op jit(solution)/shard_map/ppermute | solution.py:161
  20.9 0.7 %copy-start.3 = (s32[1,2]{1,0:T(1,128)S(1)}, s32[1,2]{1,0:T(1,128)}, u32[]{:S(2)}) copy-start(s32[1,2]{1,0:T(1,128)} %globals_ref.3) | copy-start | bytes 28
  20.9 0.7 %copy-start.4 = (s32[1,4]{1,0:T(1,128)S(1)}, s32[1,4]{1,0:T(1,128)}, u32[]{:S(2)}) copy-start(s32[1,4]{1,0:T(1,128)} %docs_ref.3) | copy-start | bytes 52
  23.8 20.5 %copy-start.1 = (bf16[1,1,128,4096]{3,2,1,0:T(8,128)(2,1)S(1)}, bf16[1,1,128,4096]{3,2,1,0:T(8,128)(2,1)}, u32[]{:S(2)}) copy-start(bf16[1,1,128,4096]{3,2,1,0:T(8,128)(2,1)} %param.11) | copy-start | bytes 3145732
  23.8 12.9 %collective-permute-start.7 = (bf16[128,2048]{1,0:T(8,128)(2,1)S(1)}, bf16[128,2048]{1,0:T(8,128)(2,1)}, u32[]{:S(2)}, u32[]{:S(2)}) collective-permute-start(bf16[128,2048]{1,0:T(8,128)(2,1)S(1)} %attend.3.refs_3_), channel_id=1, source_target_pairs={{0,4},{4,0},{1,5},{5,1},{2,6},{6,2},{3,7},{7,3},{8,12},{12,8},{9,1... | collective-permute-start | bytes 1572872 | tf_op jit(solution)/shard_map/ppermute | solution.py:187
  27.9 16.4 %collective-permute-start.3 = (bf16[128,2048]{1,0:T(8,128)(2,1)S(1)}, bf16[128,2048]{1,0:T(8,128)(2,1)S(1)}, u32[]{:S(2)}, u32[]{:S(2)}) collective-permute-start(bf16[128,2048]{1,0:T(8,128)(2,1)S(1)} %attend.2.refs_2_), channel_id=1, source_target_pairs={{0,4},{4,0},{1,5},{5,1},{2,6},{6,2},{3,7},{7,3},{8,12},{12,8},{9,1... | collective-permute-start | bytes 1572872 | tf_op jit(solution)/shard_map/ppermute | solution.py:187
  47.0 1.2 %collective-permute-start.8 = (f32[32,128]{1,0:T(8,128)S(1)}, f32[32,128]{1,0:T(8,128)S(1)}, u32[]{:S(2)}, u32[]{:S(2)}) collective-permute-start(f32[32,128]{1,0:T(8,128)S(1)} %get-tuple-element.5), channel_id=1, source_target_pairs={{0,8},{8,0},{16,24},{24,16},{1,9},{9,1},{17,25},{25,17},{2,10},{10... | collective-permute-start | bytes 49160 | tf_op jit(solution)/shard_map/ppermute | solution.py:147
  48.2 3.7 %collective-permute-start.9 = (f32[32,128]{1,0:T(8,128)S(1)}, f32[32,128]{1,0:T(8,128)S(1)}, u32[]{:S(2)}, u32[]{:S(2)}) collective-permute-start(f32[32,128]{1,0:T(8,128)S(1)} %add.12), channel_id=1, source_target_pairs={{0,16},{8,24},{16,0},{24,8},{1,17},{9,25},{17,1},{25,9},{2,18},{10... | collective-permute-start | bytes 49160 | tf_op jit(solution)/shard_map/ppermute | solution.py:147
  52.0 3.7 %collective-permute-start.10 = (f32[32,128]{1,0:T(8,128)S(1)}, f32[32,128]{1,0:T(8,128)S(1)}, u32[]{:S(2)}, u32[]{:S(2)}) collective-permute-start(f32[32,128]{1,0:T(8,128)S(1)} %add.13), channel_id=1, source_target_pairs={{0,1},{1,0},{2,3},{3,2},{4,5},{5,4},{6,7},{7,6},{8,9},{9,8},{10,11... | collective-permute-start | bytes 49160 | tf_op jit(solution)/shard_map/ppermute | solution.py:147
  55.7 4.6 %collective-permute-start.11 = (f32[32,128]{1,0:T(8,128)S(1)}, f32[32,128]{1,0:T(8,128)S(1)}, u32[]{:S(2)}, u32[]{:S(2)}) collective-permute-start(f32[32,128]{1,0:T(8,128)S(1)} %add.14), channel_id=1, source_target_pairs={{0,2},{1,3},{2,0},{3,1},{4,6},{5,7},{6,4},{7,5},{8,10},{9,11},{10,... | collective-permute-start | bytes 49160 | tf_op jit(solution)/shard_map/ppermute | solution.py:147

commit v2 on v1

--- a/solution.py
+++ b/solution.py
@@ -29,7 +29,7 @@
     return found
 
 
-def attend_kernel(part, place_ref, lists_ref, globals_ref, docs_ref, q_ref, *refs):
+def attend_kernel(part, base, place_ref, lists_ref, globals_ref, docs_ref, q_ref, *refs):
     kv_refs, out_ref = refs[:-1], refs[-1]
     rows = q_ref.shape[0]
     place = place_ref[0]
@@ -57,8 +57,8 @@
             biases.append(jnp.where(same_doc & (times > 0), level, NEVER))
         bias = jnp.concatenate(biases, axis=1)
         bias = jnp.concatenate([bias, bias], axis=0)
-        keys = jnp.concatenate([ref[:, pl.ds(index * HD, HD)] for ref in kv_refs], axis=0)
-        values = jnp.concatenate([ref[:, pl.ds((PART + index) * HD, HD)] for ref in kv_refs], axis=0)
+        keys = jnp.concatenate([ref[:, pl.ds(base + index * HD, HD)] for ref in kv_refs], axis=0)
+        values = jnp.concatenate([ref[:, pl.ds(base + (PART + index) * HD, HD)] for ref in kv_refs], axis=0)
         values = jnp.concatenate([values, jnp.ones_like(values)], axis=1)
         for pair in range(GROUP // 2):
             first = (index * GROUP + 2 * pair) * HD
@@ -78,21 +78,45 @@
             out_ref[:, pl.ds(first + HD, HD)] = result[rows:]
 
 
-def attend(part, scalars, queries, kv_slots):
+def prepare_kernel(queries_ref, kv_ref, *refs):
+    for part in range(PARTS):
+        width = PART * HD
+        for side in range(2):
+            source = pl.ds(side * KVH * HD + part * width, width)
+            refs[part][:, pl.ds(side * width, width)] = kv_ref[:, source]
+    refs[PARTS][...] = queries_ref[...]
+
+
+def prepare(queries, keys_values):
+    rows = queries.shape[0]
+    width = PART * GROUP * HD
+    outs = pl.pallas_call(
+        prepare_kernel,
+        grid=(1,),
+        out_shape=[jax.ShapeDtypeStruct((rows, 2 * PART * HD), jnp.bfloat16)] * PARTS
+        + [jax.ShapeDtypeStruct((rows, width), jnp.bfloat16)],
+        in_specs=[pl.BlockSpec((rows, width), lambda step: (0, 0)), VMEM],
+        out_specs=[VMEM] * (PARTS + 1),
+        name="prepare",
+    )(queries, keys_values)
+    return outs[:PARTS], outs[PARTS]
+
+
+def attend(part, scalars, queries, query_part, kv_slots, base):
     rows = queries.shape[0]
     width = PART * GROUP * HD
     keys = rows * len(kv_slots)
     return pl.pallas_call(
-        functools.partial(attend_kernel, part),
+        functools.partial(attend_kernel, part, base),
         out_shape=jax.ShapeDtypeStruct((rows, width), jnp.bfloat16),
         grid=(1,),
         in_specs=[SMEM] * 4
-        + [pl.BlockSpec((rows, width), lambda step: (0, part))]
+        + [pl.BlockSpec((rows, width), lambda step: (0, query_part))]
         + [VMEM] * len(kv_slots),
         out_specs=VMEM,
         compiler_params=pltpu.CompilerParams(vmem_limit_bytes=40 << 20),
         cost_estimate=pl.CostEstimate(
-            flops=4 * rows * width * keys,
+            flops=120 * rows * width * keys,
             bytes_accessed=4 * rows * width + 4 * keys * PART * HD,
             transcendentals=rows * PART * GROUP * keys,
         ),
@@ -149,16 +173,17 @@
     return value
 
 
-def gather_slots(value):
+def gather_slots(value, sections):
     count = lax.axis_size("ctx")
     slots = [value]
     for slot in range(1, count):
         pairs = [
-            (place, place ^ slot)
+            (section * count + place, section * count + (place ^ slot))
+            for section in sections
             for place in range(count)
             if abs(place - (place ^ slot)) <= count // 2
         ]
-        slots.append(lax.ppermute(value, "ctx", pairs))
+        slots.append(lax.ppermute(value, ("section", "ctx"), pairs))
     return slots
 
 
@@ -168,23 +193,20 @@
     scalars = (place, random_blocks, global_blocks, doc_lengths)
     section_count = lax.axis_size("section")
     section_place = lax.axis_index("section")
-    half = KVH * HD
-    step_width = PART * HD
-    slots = []
-    for part in range(PARTS):
-        first = part * step_width
-        kv = jnp.concatenate(
-            [
-                keys_values[:, first : first + step_width],
-                keys_values[:, half + first : half + first + step_width],
-            ],
-            axis=1,
-        )
-        slots.append(gather_slots(kv))
-    handed, arrived = [], []
-    for part in range(PARTS):
-        handed.append(attend(part, scalars, queries, slots[part]))
-        arrived.append(lax.ppermute(handed[part], "section", [(0, 1), (1, 0)]))
+    parts, early_queries = prepare(queries, keys_values)
+    every = range(section_count)
+    first_hop = [(0, 1), (1, 0)]
+    early_kv = lax.ppermute(parts[0], "section", first_hop)
+    late_slots = gather_slots(parts[1], every)
+    early_queries = lax.ppermute(early_queries, "section", first_hop)
+    both = jnp.concatenate([parts[0], early_kv], axis=1)
+    both, late_slots[1] = lax.optimization_barrier((both, late_slots[1]))
+    both_slots = gather_slots(both, every)
+    late = attend(1, scalars, queries, 1, late_slots, 0)
+    arrived_late = lax.ppermute(late, "section", first_hop)
+    own = attend(0, scalars, queries, 0, both_slots, 0)
+    arrived = [attend(0, scalars, early_queries, 0, both_slots, parts[0].shape[1]), arrived_late]
+    handed = [own, late]
     for step in range(2, section_count):
         on_step = section_place == step - 1
         for part in range(PARTS):

time: 61.2 us -> 54.6 us (0.89)
  waiting for transfers between devices: 28.3 us -> 17.3 us
  Pallas kernels: 7.52 us -> 10.7 us
  starting transfers between devices: 22 us -> 24.1 us
  local copies, waits for them, and re-layouts: 1.72 us -> 0.03 us
  other arithmetic: 0.64 us -> 1.58 us
    ppermute x8 -> x9, waiting for transfers between devices: 19.9 us -> 10.5 us  [the longest x6 10.5 us: gather_slots(): slots.append(lax.ppermute(value, ('section', 'ctx'), pairs))]
    ppermute x4, starting transfers between devices: 4.9 us -> 10.1 us  [swapped_sum(): lax.ppermute(value, axis, [(place, place ^ distance) for place in range(c...]
    pallas_call x2 -> x4, Pallas kernels: 4.81 us -> 8.97 us  [the longest x3 6.88 us: attend(): pl.pallas_call(functools.partial(attend_kernel, part, base), out_shape=ja...]
    ppermute x8 -> x9, starting transfers between devices: 17.1 us -> 14 us  [the longest x6 9.46 us: gather_slots(): slots.append(lax.ppermute(value, ('section', 'ctx'), pairs))]
    ppermute x4, waiting for transfers between devices: 8.4 us -> 6.83 us  [swapped_sum(): lax.ppermute(value, axis, [(place, place ^ distance) for place in range(c...]
    slice x1 -> x0, local copies, waits for them, and re-layouts: 1.05 us -> none  [per_device(): keys_values[:, first:first + step_width]]
    pallas_call x1, Pallas kernels: 2.71 us -> 1.69 us  [finish(): pl.pallas_call(functools.partial(finish_kernel, scale), out_shape=(jax.Sh...]
    concatenate x2 -> x1, other arithmetic: 0.02 us -> 0.96 us  [per_device(): both = jnp.concatenate([parts[0], early_kv], axis=1)]
  transfers between devices with their start and end apart: 12 -> 13, of which waited for: 7 -> 8; matrix products, arithmetic and copies ran while one was open for 0% -> 2% of each run, Pallas kernels for 8% -> 13%
where the time goes in v2:
time: 54.6 us; the launch traced here: 54.4 us
  starting transfers between devices  24.1 us (44%)
  waiting for transfers between devices  17.3 us (32%)
  Pallas kernels  10.7 us (20%)
  other arithmetic  1.58 us (3%)
  between operations  0.79 us (1%)
    ppermute x6, waiting for transfers between devices, gather_slots(): slots.append(lax.ppermute(value, ('section', 'ctx'), pairs))  10.5 us
    ppermute x4, starting transfers between devices, swapped_sum(): lax.ppermute(value, axis, [(place, place ^ distance) for place in range(c...  10.1 us
    ppermute x6, starting transfers between devices, gather_slots(): slots.append(lax.ppermute(value, ('section', 'ctx'), pairs))  9.46 us
    pallas_call x3, Pallas kernels, attend(): pl.pallas_call(functools.partial(attend_kernel, part, base), out_shape=ja...  6.88 us
    ppermute x4, waiting for transfers between devices, swapped_sum(): lax.ppermute(value, axis, [(place, place ^ distance) for place in range(c...  6.83 us
    ppermute x1, starting transfers between devices, per_device(): early_kv = lax.ppermute(parts[0], 'section', first_hop)  2.94 us
    pallas_call x1, Pallas kernels, prepare(): pl.pallas_call(prepare_kernel, grid=(1,), out_shape=[jax.ShapeDtypeStruct...  2.09 us
    pallas_call x1, Pallas kernels, finish(): pl.pallas_call(functools.partial(finish_kernel, scale), out_shape=(jax.Sh...  1.69 us
  transfers between devices with their start and end apart: 13, of which 8 were waited for; matrix products, arithmetic and copies ran while one was open for 2% of the time, Pallas kernels for 13%

profile of v2, /device:TPU:0, one launch (start us, length us, event | category | flops | bytes accessed | tf_op | source)
XLA Modules:
  0.0 54.4 jit_solution(4488858901248576645)
XLA Ops:
  0.6 2.1 %prepare.1 = (bf16[128,512]{1,0:T(8,128)(2,1)}, bf16[128,512]{1,0:T(8,128)(2,1)}, bf16[128,2048]{1,0:T(8,128)(2,1)}) custom-call(bf16[128,4096]{1,0:T(8,128)(2,1)} %bitcast.7, bf16[128,1024]{1,0:T(8,128)(2,1)} %bitcast.11), custom_call_target="tpu_custom_call" | custom-call | tf_op jit(solution)/shard_map/prepare/pallas_call | solution.py:93
  2.7 2.9 %collective-permute-start.1 = (bf16[128,512]{1,0:T(8,128)(2,1)}, bf16[128,512]{1,0:T(8,128)(2,1)S(1)}, u32[]{:S(2)}, u32[]{:S(2)}) collective-permute-start(bf16[128,512]{1,0:T(8,128)(2,1)} %get-tuple-element.10), channel_id=1, source_target_pairs={{0,4},{4,0},{1,5},{5,1},{2,6},{6,2},{3,7},{7,3},{8,12},{12,8},{9,1... | collective-permute-start | bytes 393224 | tf_op jit(solution)/shard_map/ppermute | solution.py:199
  5.7 1.6 %collective-permute-start.2 = (bf16[128,512]{1,0:T(8,128)(2,1)}, bf16[128,512]{1,0:T(8,128)(2,1)S(1)}, u32[]{:S(2)}, u32[]{:S(2)}) collective-permute-start(bf16[128,512]{1,0:T(8,128)(2,1)} %get-tuple-element.11.refs_0_), channel_id=1, source_target_pairs={{0,1},{1,0},{2,3},{3,2},{4,5},{5,4},{6,7},{7,6},{8,9},{9,8},{10,11... | collective-permute-start | bytes 393224 | tf_op jit(solution)/shard_map/ppermute | solution.py:186
  7.2 2.6 %collective-permute-start.6 = (bf16[128,512]{1,0:T(8,128)(2,1)}, bf16[128,512]{1,0:T(8,128)(2,1)S(1)}, u32[]{:S(2)}, u32[]{:S(2)}) collective-permute-start(bf16[128,512]{1,0:T(8,128)(2,1)} %get-tuple-element.11.refs_0_), channel_id=1, source_target_pairs={{0,2},{1,3},{2,0},{3,1},{4,6},{5,7},{6,4},{7,5},{8,10},{9,11},{10,... | collective-permute-start | bytes 393224 | tf_op jit(solution)/shard_map/ppermute | solution.py:186
  9.8 0.7 %collective-permute-start.7 = (bf16[128,512]{1,0:T(8,128)(2,1)}, bf16[128,512]{1,0:T(8,128)(2,1)S(1)}, u32[]{:S(2)}, u32[]{:S(2)}) collective-permute-start(bf16[128,512]{1,0:T(8,128)(2,1)} %get-tuple-element.11.refs_0_), channel_id=1, source_target_pairs={{1,2},{2,1},{5,6},{6,5},{9,10},{10,9},{13,14},{14,13},{17,18},{18,... | collective-permute-start | bytes 393224 | tf_op jit(solution)/shard_map/ppermute | solution.py:186
  10.5 0.6 %collective-permute-start = (bf16[128,2048]{1,0:T(8,128)(2,1)}, bf16[128,2048]{1,0:T(8,128)(2,1)S(1)}, u32[]{:S(2)}, u32[]{:S(2)}) collective-permute-start(bf16[128,2048]{1,0:T(8,128)(2,1)} %get-tuple-element.9), channel_id=1, source_target_pairs={{0,4},{4,0},{1,5},{5,1},{2,6},{6,2},{3,7},{7,3},{8,12},{12,8},{9,1... | collective-permute-start | bytes 1572872 | tf_op jit(solution)/shard_map/ppermute | solution.py:201
  11.1 1.0 %pad_maximum_fusion.refs_0_ = bf16[128,1024]{1,0:T(8,128)(2,1)S(1)} fusion(bf16[128,512]{1,0:T(8,128)(2,1)S(1)} %collective-permute-done.1, bf16[128,512]{1,0:T(8,128)(2,1)} %get-tuple-element.10), kind=kLoop, calls=%fused_computation | loop fusion | flops 524288 | bytes 524288 | tf_op jit(solution)/shard_map/concatenate | solution.py:202
  12.5 1.8 %collective-permute-start.3 = (bf16[128,1024]{1,0:T(8,128)(2,1)S(1)}, bf16[128,1024]{1,0:T(8,128)(2,1)S(1)}, u32[]{:S(2)}, u32[]{:S(2)}) collective-permute-start(bf16[128,1024]{1,0:T(8,128)(2,1)S(1)} %pad_maximum_fusion.refs_0_), channel_id=1, source_target_pairs={{0,1},{1,0},{2,3},{3,2},{4,5},{5,4},{6,7},{7,6},{8,9},{9,8},{10,11... | collective-permute-start | bytes 786440 | tf_op jit(solution)/shard_map/ppermute | solution.py:186
  14.3 2.2 %collective-permute-start.4 = (bf16[128,1024]{1,0:T(8,128)(2,1)S(1)}, bf16[128,1024]{1,0:T(8,128)(2,1)S(1)}, u32[]{:S(2)}, u32[]{:S(2)}) collective-permute-start(bf16[128,1024]{1,0:T(8,128)(2,1)S(1)} %pad_maximum_fusion.refs_0_), channel_id=1, source_target_pairs={{0,2},{1,3},{2,0},{3,1},{4,6},{5,7},{6,4},{7,5},{8,10},{9,11},{10,... | collective-permute-start | bytes 786440 | tf_op jit(solution)/shard_map/ppermute | solution.py:186
  16.5 0.7 %collective-permute-start.5 = (bf16[128,1024]{1,0:T(8,128)(2,1)S(1)}, bf16[128,1024]{1,0:T(8,128)(2,1)S(1)}, u32[]{:S(2)}, u32[]{:S(2)}) collective-permute-start(bf16[128,1024]{1,0:T(8,128)(2,1)S(1)} %pad_maximum_fusion.refs_0_), channel_id=1, source_target_pairs={{1,2},{2,1},{5,6},{6,5},{9,10},{10,9},{13,14},{14,13},{17,18},{18,... | collective-permute-start | bytes 786440 | tf_op jit(solution)/shard_map/ppermute | solution.py:186
  17.3 2.3 %attend.4.refs_3_ = bf16[128,2048]{1,0:T(8,128)(2,1)S(1)} custom-call(s32[1]{0:T(128)} %bitcast.2.place_ref, s32[1,4,4,4]{3,2,1,0:T(4,128)S(1)} %copy-done.3, s32[1,2]{1,0:T(1,128)S(1)} %copy-done.4, s32[1,4]{1,0:T(1,128)S(1)} %copy-done.5, bf16[128,4096]{1,0:T(8,128)(2,1)S(1)} %bitcast.8, bf16[128,512]{1,0:T(8,128)(2,1)S(1)} %copy-done.2, ...), custom_call_target="tpu_custom_call" | custom-call | flops 16106127360 | bytes 1572864 | tf_op jit(solution)/shard_map/attend/pallas_call | solution.py:109
  19.6 1.0 %collective-permute-start.8 = (bf16[128,2048]{1,0:T(8,128)(2,1)S(1)}, bf16[128,2048]{1,0:T(8,128)(2,1)S(1)}, u32[]{:S(2)}, u32[]{:S(2)}) collective-permute-start(bf16[128,2048]{1,0:T(8,128)(2,1)S(1)} %attend.4.refs_3_), channel_id=1, source_target_pairs={{0,4},{4,0},{1,5},{5,1},{2,6},{6,2},{3,7},{7,3},{8,12},{12,8},{9,1... | collective-permute-start | bytes 1572872 | tf_op jit(solution)/shard_map/ppermute | solution.py:206
  21.1 9.5 %collective-permute-done.4.refs_2_ = bf16[128,1024]{1,0:T(8,128)(2,1)S(1)} collective-permute-done((bf16[128,1024]{1,0:T(8,128)(2,1)S(1)}, bf16[128,1024]{1,0:T(8,128)(2,1)S(1)}, u32[]{:S(2)}, u32[]{:S(2)}) %collective-permute-start.4) | collective-permute-done | bytes 262176 | tf_op jit(solution)/shard_map/ppermute | solution.py:186
  30.6 2.3 %attend.5.refs_2_ = bf16[128,2048]{1,0:T(8,128)(2,1)S(1)} custom-call(s32[1]{0:T(128)} %bitcast.2.place_ref, s32[1,4,4,4]{3,2,1,0:T(4,128)S(1)} %copy-done.3, s32[1,2]{1,0:T(1,128)S(1)} %copy-done.4, s32[1,4]{1,0:T(1,128)S(1)} %copy-done.5, bf16[128,4096]{1,0:T(8,128)(2,1)S(1)} %bitcast.9, bf16[128,1024]{1,0:T(8,128)(2,1)S(1)} %pad_maximum_fusion.refs_0_, ...), custom_call_target="tpu_custom_call" | custom-call | flops 16106127360 | bytes 1572864 | tf_op jit(solution)/shard_map/attend/pallas_call | solution.py:109
  32.9 2.3 %attend.3.refs_0_ = bf16[128,2048]{1,0:T(8,128)(2,1)S(1)} custom-call(s32[1]{0:T(128)} %bitcast.2.place_ref, s32[1,4,4,4]{3,2,1,0:T(4,128)S(1)} %copy-done.3, s32[1,2]{1,0:T(1,128)S(1)} %copy-done.4, s32[1,4]{1,0:T(1,128)S(1)} %copy-done.5, bf16[128,2048]{1,0:T(8,128)(2,1)S(1)} %collective-permute-done.q_ref, bf16[128,1024]{1,0:T(8,128)(2,1)S(1)} %pad_maximum_fusion.refs_0_, ...), custom_call_target="tpu_custom_call" | custom-call | flops 16106127360 | bytes 1572864 | tf_op jit(solution)/shard_map/attend/pallas_call | solution.py:109
  35.2 1.7 %finish.1 = (bf16[128,4096]{1,0:T(8,128)(2,1)}, f32[32,128]{1,0:T(8,128)S(1)}) custom-call(s32[1]{0:T(128)} %bitcast.last_ref, bf16[128,4096]{1,0:T(8,128)(2,1)S(1)} %bitcast.10, bf16[128,2048]{1,0:T(8,128)(2,1)S(1)} %attend.3.refs_0_, bf16[128,2048]{1,0:T(8,128)(2,1)S(1)} %collective-permute-done.8.refs_1_, bf16[128,2048]{1,0:T(8,128)(2,1)S(1)} %attend.5.refs_2_, ...), custom_call_target="tpu_custom_call" | custom-call | flops 5242880 | bytes 4194304 | tf_op jit(solution)/shard_map/finish/pallas_call | solution.py:151
  36.9 1.2 %collective-permute-done.9 = f32[32,128]{1,0:T(8,128)S(1)} collective-permute-done((f32[32,128]{1,0:T(8,128)S(1)}, f32[32,128]{1,0:T(8,128)S(1)}, u32[]{:S(2)}, u32[]{:S(2)}) %collective-permute-start.9) | collective-permute-done | bytes 16416 | tf_op jit(solution)/shard_map/ppermute | solution.py:171
  38.1 1.5 %collective-permute-start.10 = (f32[32,128]{1,0:T(8,128)S(1)}, f32[32,128]{1,0:T(8,128)S(1)}, u32[]{:S(2)}, u32[]{:S(2)}) collective-permute-start(f32[32,128]{1,0:T(8,128)S(1)} %add.12), channel_id=1, source_target_pairs={{0,16},{8,24},{16,0},{24,8},{1,17},{9,25},{17,1},{25,9},{2,18},{10... | collective-permute-start | bytes 49160 | tf_op jit(solution)/shard_map/ppermute | solution.py:171
  39.6 2.2 %collective-permute-done.10 = f32[32,128]{1,0:T(8,128)S(1)} collective-permute-done((f32[32,128]{1,0:T(8,128)S(1)}, f32[32,128]{1,0:T(8,128)S(1)}, u32[]{:S(2)}, u32[]{:S(2)}) %collective-permute-start.10) | collective-permute-done | bytes 16416 | tf_op jit(solution)/shard_map/ppermute | solution.py:171
  41.8 5.5 %collective-permute-start.11 = (f32[32,128]{1,0:T(8,128)S(1)}, f32[32,128]{1,0:T(8,128)S(1)}, u32[]{:S(2)}, u32[]{:S(2)}) collective-permute-start(f32[32,128]{1,0:T(8,128)S(1)} %add.13), channel_id=1, source_target_pairs={{0,1},{1,0},{2,3},{3,2},{4,5},{5,4},{6,7},{7,6},{8,9},{9,8},{10,11... | collective-permute-start | bytes 49160 | tf_op jit(solution)/shard_map/ppermute | solution.py:171
  47.4 1.7 %collective-permute-done.11 = f32[32,128]{1,0:T(8,128)S(1)} collective-permute-done((f32[32,128]{1,0:T(8,128)S(1)}, f32[32,128]{1,0:T(8,128)S(1)}, u32[]{:S(2)}, u32[]{:S(2)}) %collective-permute-start.11) | collective-permute-done | bytes 16416 | tf_op jit(solution)/shard_map/ppermute | solution.py:171
  49.1 3.0 %collective-permute-start.12 = (f32[32,128]{1,0:T(8,128)S(1)}, f32[32,128]{1,0:T(8,128)S(1)}, u32[]{:S(2)}, u32[]{:S(2)}) collective-permute-start(f32[32,128]{1,0:T(8,128)S(1)} %add.14), channel_id=1, source_target_pairs={{0,2},{1,3},{2,0},{3,1},{4,6},{5,7},{6,4},{7,5},{8,10},{9,11},{10,... | collective-permute-start | bytes 49160 | tf_op jit(solution)/shard_map/ppermute | solution.py:171
  52.1 1.7 %collective-permute-done.12 = f32[32,128]{1,0:T(8,128)S(1)} collective-permute-done((f32[32,128]{1,0:T(8,128)S(1)}, f32[32,128]{1,0:T(8,128)S(1)}, u32[]{:S(2)}, u32[]{:S(2)}) %collective-permute-start.12) | collective-permute-done | bytes 16416 | tf_op jit(solution)/shard_map/ppermute | solution.py:171
  53.8 0.6 %add.15 = f32[32,128]{1,0:T(8,128)} add(f32[32,128]{1,0:T(8,128)S(1)} %add.14, f32[32,128]{1,0:T(8,128)S(1)} %collective-permute-done.12) | non-fusion elementwise | flops 4096 | bytes 49152 | tf_op jit(solution)/shard_map/add | solution.py:171
  (24 shorter events, 1.0 us)
Async XLA Ops:
  0.6 16.6 %copy-start = (bf16[1,1,128,4096]{3,2,1,0:T(8,128)(2,1)S(1)}, bf16[1,1,128,4096]{3,2,1,0:T(8,128)(2,1)}, u32[]{:S(2)}) copy-start(bf16[1,1,128,4096]{3,2,1,0:T(8,128)(2,1)} %param.6) | copy-start | bytes 3145732
  2.7 8.4 %collective-permute-start.1 = (bf16[128,512]{1,0:T(8,128)(2,1)}, bf16[128,512]{1,0:T(8,128)(2,1)S(1)}, u32[]{:S(2)}, u32[]{:S(2)}) collective-permute-start(bf16[128,512]{1,0:T(8,128)(2,1)} %get-tuple-element.10), channel_id=1, source_target_pairs={{0,4},{4,0},{1,5},{5,1},{2,6},{6,2},{3,7},{7,3},{8,12},{12,8},{9,1... | collective-permute-start | bytes 393224 | tf_op jit(solution)/shard_map/ppermute | solution.py:199
  5.7 6.8 %collective-permute-start.2 = (bf16[128,512]{1,0:T(8,128)(2,1)}, bf16[128,512]{1,0:T(8,128)(2,1)S(1)}, u32[]{:S(2)}, u32[]{:S(2)}) collective-permute-start(bf16[128,512]{1,0:T(8,128)(2,1)} %get-tuple-element.11.refs_0_), channel_id=1, source_target_pairs={{0,1},{1,0},{2,3},{3,2},{4,5},{5,4},{6,7},{7,6},{8,9},{9,8},{10,11... | collective-permute-start | bytes 393224 | tf_op jit(solution)/shard_map/ppermute | solution.py:186
  7.2 9.3 %collective-permute-start.6 = (bf16[128,512]{1,0:T(8,128)(2,1)}, bf16[128,512]{1,0:T(8,128)(2,1)S(1)}, u32[]{:S(2)}, u32[]{:S(2)}) collective-permute-start(bf16[128,512]{1,0:T(8,128)(2,1)} %get-tuple-element.11.refs_0_), channel_id=1, source_target_pairs={{0,2},{1,3},{2,0},{3,1},{4,6},{5,7},{6,4},{7,5},{8,10},{9,11},{10,... | collective-permute-start | bytes 393224 | tf_op jit(solution)/shard_map/ppermute | solution.py:186
  9.8 7.4 %collective-permute-start.7 = (bf16[128,512]{1,0:T(8,128)(2,1)}, bf16[128,512]{1,0:T(8,128)(2,1)S(1)}, u32[]{:S(2)}, u32[]{:S(2)}) collective-permute-start(bf16[128,512]{1,0:T(8,128)(2,1)} %get-tuple-element.11.refs_0_), channel_id=1, source_target_pairs={{1,2},{2,1},{5,6},{6,5},{9,10},{10,9},{13,14},{14,13},{17,18},{18,... | collective-permute-start | bytes 393224 | tf_op jit(solution)/shard_map/ppermute | solution.py:186
  10.5 22.4 %collective-permute-start = (bf16[128,2048]{1,0:T(8,128)(2,1)}, bf16[128,2048]{1,0:T(8,128)(2,1)S(1)}, u32[]{:S(2)}, u32[]{:S(2)}) collective-permute-start(bf16[128,2048]{1,0:T(8,128)(2,1)} %get-tuple-element.9), channel_id=1, source_target_pairs={{0,4},{4,0},{1,5},{5,1},{2,6},{6,2},{3,7},{7,3},{8,12},{12,8},{9,1... | collective-permute-start | bytes 1572872 | tf_op jit(solution)/shard_map/ppermute | solution.py:201
  11.1 6.1 %copy-start.2 = (bf16[128,512]{1,0:T(8,128)(2,1)S(1)}, bf16[128,512]{1,0:T(8,128)(2,1)}, u32[]{:S(2)}) copy-start(bf16[128,512]{1,0:T(8,128)(2,1)} %get-tuple-element.11.refs_0_) | copy-start | bytes 393220
  11.1 6.1 %copy-start.3 = (s32[1,4,4,4]{3,2,1,0:T(4,128)S(1)}, s32[1,4,4,4]{3,2,1,0:T(4,128)}, u32[]{:S(2)}) copy-start(s32[1,4,4,4]{3,2,1,0:T(4,128)} %lists_ref.5) | copy-start | bytes 772
  12.1 5.2 %copy-start.4 = (s32[1,2]{1,0:T(1,128)S(1)}, s32[1,2]{1,0:T(1,128)}, u32[]{:S(2)}) copy-start(s32[1,2]{1,0:T(1,128)} %globals_ref.5) | copy-start | bytes 28
  12.1 5.2 %copy-start.5 = (s32[1,4]{1,0:T(1,128)S(1)}, s32[1,4]{1,0:T(1,128)}, u32[]{:S(2)}) copy-start(s32[1,4]{1,0:T(1,128)} %docs_ref.5) | copy-start | bytes 52
  12.5 8.6 %collective-permute-start.3 = (bf16[128,1024]{1,0:T(8,128)(2,1)S(1)}, bf16[128,1024]{1,0:T(8,128)(2,1)S(1)}, u32[]{:S(2)}, u32[]{:S(2)}) collective-permute-start(bf16[128,1024]{1,0:T(8,128)(2,1)S(1)} %pad_maximum_fusion.refs_0_), channel_id=1, source_target_pairs={{0,1},{1,0},{2,3},{3,2},{4,5},{5,4},{6,7},{7,6},{8,9},{9,8},{10,11... | collective-permute-start | bytes 786440 | tf_op jit(solution)/shard_map/ppermute | solution.py:186
  14.3 16.3 %collective-permute-start.4 = (bf16[128,1024]{1,0:T(8,128)(2,1)S(1)}, bf16[128,1024]{1,0:T(8,128)(2,1)S(1)}, u32[]{:S(2)}, u32[]{:S(2)}) collective-permute-start(bf16[128,1024]{1,0:T(8,128)(2,1)S(1)} %pad_maximum_fusion.refs_0_), channel_id=1, source_target_pairs={{0,2},{1,3},{2,0},{3,1},{4,6},{5,7},{6,4},{7,5},{8,10},{9,11},{10,... | collective-permute-start | bytes 786440 | tf_op jit(solution)/shard_map/ppermute | solution.py:186
  16.5 14.0 %collective-permute-start.5 = (bf16[128,1024]{1,0:T(8,128)(2,1)S(1)}, bf16[128,1024]{1,0:T(8,128)(2,1)S(1)}, u32[]{:S(2)}, u32[]{:S(2)}) collective-permute-start(bf16[128,1024]{1,0:T(8,128)(2,1)S(1)} %pad_maximum_fusion.refs_0_), channel_id=1, source_target_pairs={{1,2},{2,1},{5,6},{6,5},{9,10},{10,9},{13,14},{14,13},{17,18},{18,... | collective-permute-start | bytes 786440 | tf_op jit(solution)/shard_map/ppermute | solution.py:186
  19.6 15.6 %collective-permute-start.8 = (bf16[128,2048]{1,0:T(8,128)(2,1)S(1)}, bf16[128,2048]{1,0:T(8,128)(2,1)S(1)}, u32[]{:S(2)}, u32[]{:S(2)}) collective-permute-start(bf16[128,2048]{1,0:T(8,128)(2,1)S(1)} %attend.4.refs_3_), channel_id=1, source_target_pairs={{0,4},{4,0},{1,5},{5,1},{2,6},{6,2},{3,7},{7,3},{8,12},{12,8},{9,1... | collective-permute-start | bytes 1572872 | tf_op jit(solution)/shard_map/ppermute | solution.py:206
  32.9 2.3 %copy-start.1 = (bf16[1,1,128,4096]{3,2,1,0:T(8,128)(2,1)S(1)}, bf16[1,1,128,4096]{3,2,1,0:T(8,128)(2,1)}, u32[]{:S(2)}) copy-start(bf16[1,1,128,4096]{3,2,1,0:T(8,128)(2,1)} %param.11) | copy-start | bytes 3145732
  36.9 1.2 %collective-permute-start.9 = (f32[32,128]{1,0:T(8,128)S(1)}, f32[32,128]{1,0:T(8,128)S(1)}, u32[]{:S(2)}, u32[]{:S(2)}) collective-permute-start(f32[32,128]{1,0:T(8,128)S(1)} %get-tuple-element.15), channel_id=1, source_target_pairs={{0,8},{8,0},{16,24},{24,16},{1,9},{9,1},{17,25},{25,17},{2,10},{10... | collective-permute-start | bytes 49160 | tf_op jit(solution)/shard_map/ppermute | solution.py:171
  38.1 3.7 %collective-permute-start.10 = (f32[32,128]{1,0:T(8,128)S(1)}, f32[32,128]{1,0:T(8,128)S(1)}, u32[]{:S(2)}, u32[]{:S(2)}) collective-permute-start(f32[32,128]{1,0:T(8,128)S(1)} %add.12), channel_id=1, source_target_pairs={{0,16},{8,24},{16,0},{24,8},{1,17},{9,25},{17,1},{25,9},{2,18},{10... | collective-permute-start | bytes 49160 | tf_op jit(solution)/shard_map/ppermute | solution.py:171
  41.8 7.3 %collective-permute-start.11 = (f32[32,128]{1,0:T(8,128)S(1)}, f32[32,128]{1,0:T(8,128)S(1)}, u32[]{:S(2)}, u32[]{:S(2)}) collective-permute-start(f32[32,128]{1,0:T(8,128)S(1)} %add.13), channel_id=1, source_target_pairs={{0,1},{1,0},{2,3},{3,2},{4,5},{5,4},{6,7},{7,6},{8,9},{9,8},{10,11... | collective-permute-start | bytes 49160 | tf_op jit(solution)/shard_map/ppermute | solution.py:171
  49.1 4.7 %collective-permute-start.12 = (f32[32,128]{1,0:T(8,128)S(1)}, f32[32,128]{1,0:T(8,128)S(1)}, u32[]{:S(2)}, u32[]{:S(2)}) collective-permute-start(f32[32,128]{1,0:T(8,128)S(1)} %add.14), channel_id=1, source_target_pairs={{0,2},{1,3},{2,0},{3,1},{4,6},{5,7},{6,4},{7,5},{8,10},{9,11},{10,... | collective-permute-start | bytes 49160 | tf_op jit(solution)/shard_map/ppermute | solution.py:171

commit v3 on v1

--- a/solution.py
+++ b/solution.py
@@ -17,6 +17,7 @@
 PART = 2
 PARTS = KVH // PART
 NEVER = -1e30
+LEVELS = 8
 SCALE = math.log2(math.e) / math.sqrt(HD)
 VMEM = pl.BlockSpec(memory_space=pltpu.VMEM)
 SMEM = pl.BlockSpec(memory_space=pltpu.SMEM)
@@ -29,36 +30,50 @@
     return found
 
 
-def attend_kernel(part, place_ref, lists_ref, globals_ref, docs_ref, q_ref, *refs):
-    kv_refs, out_ref = refs[:-1], refs[-1]
-    rows = q_ref.shape[0]
+def weigh_kernel(place_ref, lists_ref, globals_ref, docs_ref, out_ref):
+    rows, width = out_ref.shape[0] - LEVELS, out_ref.shape[1]
     place = place_ref[0]
     doc_ends, end = [], 0
     for doc in range(docs_ref.shape[1]):
         end = end + docs_ref[0, doc]
         doc_ends.append(end)
     query_doc = count_docs(doc_ends, place * rows + lax.broadcasted_iota(jnp.int32, (rows, 1), 0))
-    blocks, same = [], []
-    for slot in range(len(kv_refs)):
+    for slot in range(width // rows):
         block = place ^ slot
+        columns = pl.ds(slot * rows, rows)
         key_doc = count_docs(doc_ends, block * rows + lax.broadcasted_iota(jnp.int32, (1, rows), 1))
-        blocks.append(block)
-        same.append(query_doc == key_doc)
+        out_ref[pl.ds(0, rows), columns] = jnp.where(query_doc == key_doc, 0.0, NEVER)
+        shared = (jnp.abs(block - place) <= 1).astype(jnp.int32)
+        for entry in range(GLOBALS):
+            shared += (globals_ref[0, entry] == block).astype(jnp.int32)
+        for head in range(KVH):
+            times = shared
+            for entry in range(RAND):
+                times += (lists_ref[0, place, head, entry] == block).astype(jnp.int32)
+            times = jnp.full((1, rows), times, jnp.int32)
+            level = jnp.where(times > 0, jnp.log2(times.astype(jnp.float32)), NEVER)
+            out_ref[pl.ds(rows + head, 1), columns] = level
+
+
+def weigh(scalars, rows, slots):
+    return pl.pallas_call(
+        weigh_kernel,
+        out_shape=jax.ShapeDtypeStruct((rows + LEVELS, slots * rows), jnp.float32),
+        in_specs=[SMEM] * 4,
+        out_specs=VMEM,
+        compiler_params=pltpu.CompilerParams(vmem_limit_bytes=16 << 20),
+        name="weigh",
+    )(*scalars)
+
+
+def attend_kernel(part, base, weights_ref, q_ref, *refs):
+    kv_refs, out_ref = refs[:-1], refs[-1]
+    rows = q_ref.shape[0]
     for index in range(PART):
-        head = part * PART + index
-        biases = []
-        for block, same_doc in zip(blocks, same):
-            times = (jnp.abs(block - place) <= 1).astype(jnp.int32)
-            for slot in range(GLOBALS):
-                times += (globals_ref[0, slot] == block).astype(jnp.int32)
-            for slot in range(RAND):
-                times += (lists_ref[0, place, head, slot] == block).astype(jnp.int32)
-            level = jnp.log2(jnp.full((1, rows), times, jnp.int32).astype(jnp.float32))
-            biases.append(jnp.where(same_doc & (times > 0), level, NEVER))
-        bias = jnp.concatenate(biases, axis=1)
+        bias = weights_ref[pl.ds(0, rows), :] + weights_ref[pl.ds(rows + part * PART + index, 1), :]
         bias = jnp.concatenate([bias, bias], axis=0)
-        keys = jnp.concatenate([ref[:, pl.ds(index * HD, HD)] for ref in kv_refs], axis=0)
-        values = jnp.concatenate([ref[:, pl.ds((PART + index) * HD, HD)] for ref in kv_refs], axis=0)
+        keys = jnp.concatenate([ref[:, pl.ds(base + index * HD, HD)] for ref in kv_refs], axis=0)
+        values = jnp.concatenate([ref[:, pl.ds(base + (PART + index) * HD, HD)] for ref in kv_refs], axis=0)
         values = jnp.concatenate([values, jnp.ones_like(values)], axis=1)
         for pair in range(GROUP // 2):
             first = (index * GROUP + 2 * pair) * HD
@@ -78,26 +93,28 @@
             out_ref[:, pl.ds(first + HD, HD)] = result[rows:]
 
 
-def attend(part, scalars, queries, kv_slots):
+def attend(part, weights, queries, query_part, kv_slots, base=0):
     rows = queries.shape[0]
     width = PART * GROUP * HD
     keys = rows * len(kv_slots)
     return pl.pallas_call(
-        functools.partial(attend_kernel, part),
+        functools.partial(attend_kernel, part, base),
+        grid=(1,),
         out_shape=jax.ShapeDtypeStruct((rows, width), jnp.bfloat16),
-        grid=(1,),
-        in_specs=[SMEM] * 4
-        + [pl.BlockSpec((rows, width), lambda step: (0, part))]
+        in_specs=[
+            VMEM,
+            pl.BlockSpec((rows, width), lambda step: (0, query_part)),
+        ]
         + [VMEM] * len(kv_slots),
         out_specs=VMEM,
         compiler_params=pltpu.CompilerParams(vmem_limit_bytes=40 << 20),
         cost_estimate=pl.CostEstimate(
-            flops=4 * rows * width * keys,
+            flops=120 * rows * width * keys,
             bytes_accessed=4 * rows * width + 4 * keys * PART * HD,
             transcendentals=rows * PART * GROUP * keys,
         ),
         name="attend",
-    )(*scalars, queries, *kv_slots)
+    )(weights, queries, *kv_slots)
 
 
 def finish_kernel(scale, last_ref, cotangent_ref, *refs):
@@ -140,25 +157,46 @@
     )(is_last, cotangent, *arrived, *handed)
 
 
-def swapped_sum(value, axis):
+def swapped_sum(value, axis, distances):
     count = lax.axis_size(axis)
-    distance = 1
-    while distance < count:
+    for distance in distances:
         value = value + lax.ppermute(value, axis, [(place, place ^ distance) for place in range(count)])
-        distance *= 2
     return value
 
 
+def powers(first, end):
+    return [1 << step for step in range(first, (end - 1).bit_length())]
+
+
+def total_share(value):
+    replicas, count = lax.axis_size("dp"), lax.axis_size("ctx")
+    value = swapped_sum(value, "dp", [1])
+    if replicas != 4 or count > 4:
+        return swapped_sum(swapped_sum(value, "dp", powers(1, replicas)), "ctx", powers(0, count))
+    core = lax.axis_index("dp") % 2
+    heard = []
+    for distance in range(count):
+        pairs = []
+        for replica in range(replicas):
+            for place in range(count):
+                across = replica ^ 2 if distance == 0 or replica % 2 else replica
+                pairs.append((replica * count + place, across * count + (place ^ distance)))
+        heard.append(lax.ppermute(value, ("dp", "ctx"), pairs))
+    value = sum(heard[1:], jnp.where(core == 0, value + heard[0], 0.0))
+    return swapped_sum(value, "dp", [1])
+
+
 def gather_slots(value):
-    count = lax.axis_size("ctx")
+    count, replicas = lax.axis_size("ctx"), lax.axis_size("dp")
     slots = [value]
     for slot in range(1, count):
-        pairs = [
-            (place, place ^ slot)
-            for place in range(count)
-            if abs(place - (place ^ slot)) <= count // 2
-        ]
-        slots.append(lax.ppermute(value, "ctx", pairs))
+        pairs = []
+        for replica in range(replicas):
+            for place in range(count):
+                near = abs(place - (place ^ slot)) <= count // 2
+                partner = (replica, place ^ slot) if near else (replica ^ 1, place)
+                pairs.append((replica * count + place, partner[0] * count + partner[1]))
+        slots.append(lax.ppermute(value, ("dp", "ctx"), pairs))
     return slots
 
 
@@ -169,22 +207,33 @@
     section_count = lax.axis_size("section")
     section_place = lax.axis_index("section")
     half = KVH * HD
-    step_width = PART * HD
-    slots = []
+    kv_width = PART * HD
+    parts = []
     for part in range(PARTS):
-        first = part * step_width
-        kv = jnp.concatenate(
-            [
-                keys_values[:, first : first + step_width],
-                keys_values[:, half + first : half + first + step_width],
-            ],
-            axis=1,
+        first = part * kv_width
+        parts.append(
+            jnp.concatenate(
+                [
+                    keys_values[:, first : first + kv_width],
+                    keys_values[:, half + first : half + first + kv_width],
+                ],
+                axis=1,
+            )
         )
-        slots.append(gather_slots(kv))
-    handed, arrived = [], []
-    for part in range(PARTS):
-        handed.append(attend(part, scalars, queries, slots[part]))
-        arrived.append(lax.ppermute(handed[part], "section", [(0, 1), (1, 0)]))
+    weights = weigh(scalars, queries.shape[0], lax.axis_size("ctx"))
+    first_hop = [(0, 1), (1, 0)]
+    early_kv = lax.ppermute(parts[0], "section", first_hop)
+    late_slots = gather_slots(parts[1])
+    early_queries = lax.ppermute(queries[:, : PART * GROUP * HD], "section", first_hop)
+    own_kv, late_slots[1] = lax.optimization_barrier((parts[0], late_slots[1]))
+    own_slots = gather_slots(own_kv)
+    late = attend(1, weights, queries, 1, late_slots)
+    arrived_late = lax.ppermute(late, "section", first_hop)
+    early_kv, own_slots[1] = lax.optimization_barrier((early_kv, own_slots[1]))
+    early_slots = gather_slots(early_kv)
+    own = attend(0, weights, queries, 0, own_slots)
+    arrived = [attend(0, weights, early_queries, 0, early_slots), arrived_late]
+    handed = [own, late]
     for step in range(2, section_count):
         on_step = section_place == step - 1
         for part in range(PARTS):
@@ -193,7 +242,7 @@
             arrived[part] = lax.ppermute(handed[part], "section", [(step - 1, step), (step, step - 1)])
     is_last = (section_place == section_count - 1).astype(jnp.int32).reshape(1)
     stream, share = finish(is_last, cotangent, arrived, handed, 1.0 / lax.axis_size("dp"))
-    gain_grad = swapped_sum(swapped_sum(share, "dp"), "ctx")
+    gain_grad = total_share(share)
     return (stream[None, None], gain_grad.reshape(1, HEADS * HD))
 
 

time: 61.2 us -> 50.2 us (0.82)
  waiting for transfers between devices: 28.3 us -> 15.6 us
  starting transfers between devices: 22 us -> 23.9 us
    ppermute x8 -> x16, waiting for transfers between devices: 19.9 us -> 13.4 us  [the longest x9 11.1 us: gather_slots(): slots.append(lax.ppermute(value, ('dp', 'ctx'), pairs))]
    ppermute x8 -> x16, starting transfers between devices: 17.1 us -> 23.7 us  [the longest x9 14 us: gather_slots(): slots.append(lax.ppermute(value, ('dp', 'ctx'), pairs))]
    ppermute x4 -> x2, waiting for transfers between devices: 8.4 us -> 2.25 us  [swapped_sum(): lax.ppermute(value, axis, [(place, place ^ distance) for place in range(c...]
    ppermute x4 -> x2, starting transfers between devices: 4.9 us -> 0.18 us  [swapped_sum(): lax.ppermute(value, axis, [(place, place ^ distance) for place in range(c...]
    pallas_call x1, Pallas kernels: 2.71 us -> 1.69 us  [finish(): pl.pallas_call(functools.partial(finish_kernel, scale), out_shape=(jax.Sh...]
    pallas_call x2 -> x4, Pallas kernels: 4.81 us -> 5.64 us  [the longest x3 4.84 us: attend(): pl.pallas_call(functools.partial(attend_kernel, part, base), grid=(1,), o...]
  transfers between devices with their start and end apart: 12 -> 18, of which waited for: 7 -> 8; matrix products, arithmetic and copies ran while one was open for 0% -> 0% of each run, Pallas kernels for 8% -> 11%
where the time goes in v3:
time: 50.2 us; the launch traced here: 50 us
  starting transfers between devices  23.9 us (48%)
  waiting for transfers between devices  15.6 us (31%)
  Pallas kernels  7.33 us (15%)
  local copies, waits for them, and re-layouts  1.79 us (4%)
  between operations  0.77 us (2%)
  other arithmetic  0.64 us (1%)
    ppermute x9, starting transfers between devices, gather_slots(): slots.append(lax.ppermute(value, ('dp', 'ctx'), pairs))  14 us
    ppermute x9, waiting for transfers between devices, gather_slots(): slots.append(lax.ppermute(value, ('dp', 'ctx'), pairs))  11.1 us
    ppermute x4, starting transfers between devices, total_share(): heard.append(lax.ppermute(value, ('dp', 'ctx'), pairs))  5.91 us
    pallas_call x3, Pallas kernels, attend(): pl.pallas_call(functools.partial(attend_kernel, part, base), grid=(1,), o...  4.84 us
    ppermute x2, waiting for transfers between devices, swapped_sum(): lax.ppermute(value, axis, [(place, place ^ distance) for place in range(c...  2.25 us
    ppermute x4, waiting for transfers between devices, total_share(): heard.append(lax.ppermute(value, ('dp', 'ctx'), pairs))  2.22 us
    pallas_call x1, Pallas kernels, finish(): pl.pallas_call(functools.partial(finish_kernel, scale), out_shape=(jax.Sh...  1.69 us
    ppermute x1, starting transfers between devices, per_device(): arrived_late = lax.ppermute(late, 'section', first_hop)  1.56 us
  transfers between devices with their start and end apart: 18, of which 8 were waited for; matrix products, arithmetic and copies ran while one was open for 0% of the time, Pallas kernels for 11%

profile of v3, /device:TPU:0, one launch (start us, length us, event | category | flops | bytes accessed | tf_op | source)
XLA Modules:
  0.0 50.0 jit_solution(14855990396004727782)
XLA Ops:
  0.6 1.0 %fusion = (bf16[128,256]{1,0:T(8,128)(2,1)S(1)}, bf16[128,256]{1,0:T(8,128)(2,1)S(1)}, bf16[128,256]{1,0:T(8,128)(2,1)S(1)}, bf16[128,256]{1,0:T(8,128)(2,1)S(1)}) fusion(bf16[128,1024]{1,0:T(8,128)(2,1)} %bitcast.11), kind=kLoop, calls=%fused_computation.3 | loop fusion | bytes 524288 | tf_op jit(solution)/shard_map/slice | solution.py:217
  1.7 3.1 %collective-permute-start.2 = (bf16[128,512]{1,0:T(8,128)(2,1)S(1)}, bf16[128,512]{1,0:T(8,128)(2,1)S(1)}, u32[]{:S(2)}, u32[]{:S(2)}) collective-permute-start(bf16[128,512]{1,0:T(8,128)(2,1)S(1)} %pad_maximum_fusion.1.refs_0_), channel_id=1, source_target_pairs={{0,1},{1,0},{2,3},{3,2},{8,9},{9,8},{10,11},{11,10},{16,17},{17,16... | collective-permute-start | bytes 393224 | tf_op jit(solution)/shard_map/ppermute | solution.py:199
  4.8 2.6 %collective-permute-start.7 = (bf16[128,512]{1,0:T(8,128)(2,1)S(1)}, bf16[128,512]{1,0:T(8,128)(2,1)S(1)}, u32[]{:S(2)}, u32[]{:S(2)}) collective-permute-start(bf16[128,512]{1,0:T(8,128)(2,1)S(1)} %pad_maximum_fusion.1.refs_0_), channel_id=1, source_target_pairs={{0,2},{1,3},{2,0},{3,1},{8,10},{9,11},{10,8},{11,9},{16,18},{17,19... | collective-permute-start | bytes 393224 | tf_op jit(solution)/shard_map/ppermute | solution.py:199
  7.4 1.6 %collective-permute-start.1 = (bf16[128,512]{1,0:T(8,128)(2,1)S(1)}, bf16[128,512]{1,0:T(8,128)(2,1)S(1)}, u32[]{:S(2)}, u32[]{:S(2)}) collective-permute-start(bf16[128,512]{1,0:T(8,128)(2,1)S(1)} %pad_maximum_fusion.refs_0_), channel_id=1, source_target_pairs={{0,4},{4,0},{1,5},{5,1},{2,6},{6,2},{3,7},{7,3},{8,12},{12,8},{9,1... | collective-permute-start | bytes 393224 | tf_op jit(solution)/shard_map/ppermute | solution.py:225
  9.6 0.7 %copy-done.2 = s32[1,4,4,4]{3,2,1,0:T(4,128)S(1)} copy-done((s32[1,4,4,4]{3,2,1,0:T(4,128)S(1)}, s32[1,4,4,4]{3,2,1,0:T(4,128)}, u32[]{:S(2)}) %copy-start.2) | copy-done | bytes 280
  10.3 0.8 %weigh.1.weights_ref = f32[136,512]{1,0:T(8,128)S(1)} custom-call(s32[1]{0:T(128)} %bitcast.2.place_ref, s32[1,4,4,4]{3,2,1,0:T(4,128)S(1)} %copy-done.2, s32[1,2]{1,0:T(1,128)S(1)} %copy-done.3, s32[1,4]{1,0:T(1,128)S(1)} %copy-done.4), custom_call_target="tpu_custom_call" | custom-call | tf_op jit(solution)/shard_map/weigh/pallas_call | solution.py:59
  11.2 5.2 %collective-permute-start.10 = (bf16[128,512]{1,0:T(8,128)(2,1)S(1)}, bf16[128,512]{1,0:T(8,128)(2,1)S(1)}, u32[]{:S(2)}, u32[]{:S(2)}) collective-permute-start(bf16[128,512]{1,0:T(8,128)(2,1)S(1)} %pad_maximum_fusion.refs_0_), channel_id=1, source_target_pairs={{0,2},{1,3},{2,0},{3,1},{8,10},{9,11},{10,8},{11,9},{16,18},{17,19... | collective-permute-start | bytes 393224 | tf_op jit(solution)/shard_map/ppermute | solution.py:199
  16.4 2.4 %collective-permute-done.7.refs_2_ = bf16[128,512]{1,0:T(8,128)(2,1)S(1)} collective-permute-done((bf16[128,512]{1,0:T(8,128)(2,1)S(1)}, bf16[128,512]{1,0:T(8,128)(2,1)S(1)}, u32[]{:S(2)}, u32[]{:S(2)}) %collective-permute-start.7) | collective-permute-done | bytes 131104 | tf_op jit(solution)/shard_map/ppermute | solution.py:199
  18.8 1.6 %attend.4.refs_3_ = bf16[128,2048]{1,0:T(8,128)(2,1)S(1)} custom-call(f32[136,512]{1,0:T(8,128)S(1)} %weigh.1.weights_ref, bf16[128,4096]{1,0:T(8,128)(2,1)S(1)} %bitcast.9, bf16[128,512]{1,0:T(8,128)(2,1)S(1)} %pad_maximum_fusion.1.refs_0_, bf16[128,512]{1,0:T(8,128)(2,1)S(1)} %collective-permute-done.2.refs_1_, ...), custom_call_target="tpu_custom_call" | custom-call | flops 16106127360 | bytes 1572864 | tf_op jit(solution)/shard_map/attend/pallas_call | solution.py:100
  20.4 1.6 %collective-permute-start.9 = (bf16[128,2048]{1,0:T(8,128)(2,1)S(1)}, bf16[128,2048]{1,0:T(8,128)(2,1)S(1)}, u32[]{:S(2)}, u32[]{:S(2)}) collective-permute-start(bf16[128,2048]{1,0:T(8,128)(2,1)S(1)} %attend.4.refs_3_), channel_id=1, source_target_pairs={{0,4},{4,0},{1,5},{5,1},{2,6},{6,2},{3,7},{7,3},{8,12},{12,8},{9,1... | collective-permute-start | bytes 1572872 | tf_op jit(solution)/shard_map/ppermute | solution.py:231
  22.0 3.7 %collective-permute-done.3.refs_1_ = bf16[128,512]{1,0:T(8,128)(2,1)S(1)} collective-permute-done((bf16[128,512]{1,0:T(8,128)(2,1)S(1)}, bf16[128,512]{1,0:T(8,128)(2,1)S(1)}, u32[]{:S(2)}, u32[]{:S(2)}) %collective-permute-start.3) | collective-permute-done | bytes 131104 | tf_op jit(solution)/shard_map/ppermute | solution.py:199
  25.7 0.9 %collective-permute-start.5 = (bf16[128,512]{1,0:T(8,128)(2,1)S(1)}, bf16[128,512]{1,0:T(8,128)(2,1)S(1)}, u32[]{:S(2)}, u32[]{:S(2)}) collective-permute-start(bf16[128,512]{1,0:T(8,128)(2,1)S(1)} %collective-permute-done.1.refs_0_), channel_id=1, source_target_pairs={{0,2},{1,3},{2,0},{3,1},{8,10},{9,11},{10,8},{11,9},{16,18},{17,19... | collective-permute-start | bytes 393224 | tf_op jit(solution)/shard_map/ppermute | solution.py:199
  26.5 2.3 %collective-permute-start.4 = (bf16[128,512]{1,0:T(8,128)(2,1)S(1)}, bf16[128,512]{1,0:T(8,128)(2,1)S(1)}, u32[]{:S(2)}, u32[]{:S(2)}) collective-permute-start(bf16[128,512]{1,0:T(8,128)(2,1)S(1)} %collective-permute-done.1.refs_0_), channel_id=1, source_target_pairs={{0,1},{1,0},{2,3},{3,2},{8,9},{9,8},{10,11},{11,10},{16,17},{17,16... | collective-permute-start | bytes 393224 | tf_op jit(solution)/shard_map/ppermute | solution.py:199
  28.8 1.6 %attend.5.refs_2_ = bf16[128,2048]{1,0:T(8,128)(2,1)S(1)} custom-call(f32[136,512]{1,0:T(8,128)S(1)} %weigh.1.weights_ref, bf16[128,4096]{1,0:T(8,128)(2,1)S(1)} %bitcast.10, bf16[128,512]{1,0:T(8,128)(2,1)S(1)} %pad_maximum_fusion.refs_0_, bf16[128,512]{1,0:T(8,128)(2,1)S(1)} %collective-permute-done.3.refs_1_, ...), custom_call_target="tpu_custom_call" | custom-call | flops 16106127360 | bytes 1572864 | tf_op jit(solution)/shard_map/attend/pallas_call | solution.py:100
  30.4 4.9 %collective-permute-done.5.refs_2_ = bf16[128,512]{1,0:T(8,128)(2,1)S(1)} collective-permute-done((bf16[128,512]{1,0:T(8,128)(2,1)S(1)}, bf16[128,512]{1,0:T(8,128)(2,1)S(1)}, u32[]{:S(2)}, u32[]{:S(2)}) %collective-permute-start.5) | collective-permute-done | bytes 131104 | tf_op jit(solution)/shard_map/ppermute | solution.py:199
  35.5 1.6 %attend.3.refs_0_ = bf16[128,2048]{1,0:T(8,128)(2,1)S(1)} custom-call(f32[136,512]{1,0:T(8,128)S(1)} %weigh.1.weights_ref, bf16[128,2048]{1,0:T(8,128)(2,1)S(1)} %collective-permute-done.q_ref, bf16[128,512]{1,0:T(8,128)(2,1)S(1)} %collective-permute-done.1.refs_0_, bf16[128,512]{1,0:T(8,128)(2,1)S(1)} %collective-permute-done.4.refs_1_, ...), custom_call_target="tpu_custom_call" | custom-call | flops 16106127360 | bytes 1572864 | tf_op jit(solution)/shard_map/attend/pallas_call | solution.py:100
  37.1 1.7 %finish.1 = (bf16[128,4096]{1,0:T(8,128)(2,1)}, f32[32,128]{1,0:T(8,128)S(1)}) custom-call(s32[1]{0:T(128)} %bitcast.last_ref, bf16[128,4096]{1,0:T(8,128)(2,1)S(1)} %bitcast.7, bf16[128,2048]{1,0:T(8,128)(2,1)S(1)} %attend.3.refs_0_, bf16[128,2048]{1,0:T(8,128)(2,1)S(1)} %collective-permute-done.9.refs_1_, bf16[128,2048]{1,0:T(8,128)(2,1)S(1)} %attend.5.refs_2_, ...), custom_call_target="tpu_custom_call" | custom-call | flops 5242880 | bytes 4194304 | tf_op jit(solution)/shard_map/finish/pallas_call | solution.py:144
  38.8 1.2 %collective-permute-done.12 = f32[32,128]{1,0:T(8,128)S(1)} collective-permute-done((f32[32,128]{1,0:T(8,128)S(1)}, f32[32,128]{1,0:T(8,128)S(1)}, u32[]{:S(2)}, u32[]{:S(2)}) %collective-permute-start.12) | collective-permute-done | bytes 16416 | tf_op jit(solution)/shard_map/ppermute | solution.py:163
  40.0 2.2 %collective-permute-start.16 = (f32[32,128]{1,0:T(8,128)S(1)}, f32[32,128]{1,0:T(8,128)S(1)}, u32[]{:S(2)}, u32[]{:S(2)}) collective-permute-start(f32[32,128]{1,0:T(8,128)S(1)} %add.23), channel_id=1, source_target_pairs={{0,3},{1,2},{2,1},{3,0},{8,27},{9,26},{10,25},{11,24},{16,19},{17,... | collective-permute-start | bytes 49160 | tf_op jit(solution)/shard_map/ppermute | solution.py:184
  42.2 2.2 %collective-permute-start.14 = (f32[32,128]{1,0:T(8,128)S(1)}, f32[32,128]{1,0:T(8,128)S(1)}, u32[]{:S(2)}, u32[]{:S(2)}) collective-permute-start(f32[32,128]{1,0:T(8,128)S(1)} %add.23), channel_id=1, source_target_pairs={{0,1},{1,0},{2,3},{3,2},{8,25},{9,24},{10,27},{11,26},{16,17},{17,... | collective-permute-start | bytes 49160 | tf_op jit(solution)/shard_map/ppermute | solution.py:184
  44.4 1.5 %collective-permute-start.13 = (f32[32,128]{1,0:T(8,128)S(1)}, f32[32,128]{1,0:T(8,128)S(1)}, u32[]{:S(2)}, u32[]{:S(2)}) collective-permute-start(f32[32,128]{1,0:T(8,128)S(1)} %add.23), channel_id=1, source_target_pairs={{0,16},{1,17},{2,18},{3,19},{8,24},{9,25},{10,26},{11,27},{16,0},{... | collective-permute-start | bytes 49160 | tf_op jit(solution)/shard_map/ppermute | solution.py:184
  45.9 0.9 %collective-permute-done.15 = f32[32,128]{1,0:T(8,128)S(1)} collective-permute-done((f32[32,128]{1,0:T(8,128)S(1)}, f32[32,128]{1,0:T(8,128)S(1)}, u32[]{:S(2)}, u32[]{:S(2)}) %collective-permute-start.15) | collective-permute-done | bytes 16416 | tf_op jit(solution)/shard_map/ppermute | solution.py:184
  46.8 1.3 %collective-permute-done.13 = f32[32,128]{1,0:T(8,128)S(1)} collective-permute-done((f32[32,128]{1,0:T(8,128)S(1)}, f32[32,128]{1,0:T(8,128)S(1)}, u32[]{:S(2)}, u32[]{:S(2)}) %collective-permute-start.13) | collective-permute-done | bytes 16416 | tf_op jit(solution)/shard_map/ppermute | solution.py:184
  48.3 1.1 %collective-permute-done.17 = f32[32,128]{1,0:T(8,128)S(1)} collective-permute-done((f32[32,128]{1,0:T(8,128)S(1)}, f32[32,128]{1,0:T(8,128)S(1)}, u32[]{:S(2)}, u32[]{:S(2)}) %collective-permute-start.17) | collective-permute-done | bytes 16416 | tf_op jit(solution)/shard_map/ppermute | solution.py:163
  (34 shorter events, 1.8 us)
Async XLA Ops:
  0.6 8.3 %copy-start.1 = (bf16[1,1,128,4096]{3,2,1,0:T(8,128)(2,1)S(1)}, bf16[1,1,128,4096]{3,2,1,0:T(8,128)(2,1)}, u32[]{:S(2)}) copy-start(bf16[1,1,128,4096]{3,2,1,0:T(8,128)(2,1)} %param.6) | copy-start | bytes 3145732
  1.7 9.4 %collective-permute-start.2 = (bf16[128,512]{1,0:T(8,128)(2,1)S(1)}, bf16[128,512]{1,0:T(8,128)(2,1)S(1)}, u32[]{:S(2)}, u32[]{:S(2)}) collective-permute-start(bf16[128,512]{1,0:T(8,128)(2,1)S(1)} %pad_maximum_fusion.1.refs_0_), channel_id=1, source_target_pairs={{0,1},{1,0},{2,3},{3,2},{8,9},{9,8},{10,11},{11,10},{16,17},{17,16... | collective-permute-start | bytes 393224 | tf_op jit(solution)/shard_map/ppermute | solution.py:199
  4.8 6.4 %collective-permute-start.8 = (bf16[128,512]{1,0:T(8,128)(2,1)S(1)}, bf16[128,512]{1,0:T(8,128)(2,1)S(1)}, u32[]{:S(2)}, u32[]{:S(2)}) collective-permute-start(bf16[128,512]{1,0:T(8,128)(2,1)S(1)} %pad_maximum_fusion.1.refs_0_), channel_id=1, source_target_pairs={{0,8},{1,2},{2,1},{3,11},{8,0},{9,10},{10,9},{11,3},{16,24},{17,18... | collective-permute-start | bytes 393224 | tf_op jit(solution)/shard_map/ppermute | solution.py:199
  4.8 14.0 %collective-permute-start.7 = (bf16[128,512]{1,0:T(8,128)(2,1)S(1)}, bf16[128,512]{1,0:T(8,128)(2,1)S(1)}, u32[]{:S(2)}, u32[]{:S(2)}) collective-permute-start(bf16[128,512]{1,0:T(8,128)(2,1)S(1)} %pad_maximum_fusion.1.refs_0_), channel_id=1, source_target_pairs={{0,2},{1,3},{2,0},{3,1},{8,10},{9,11},{10,8},{11,9},{16,18},{17,19... | collective-permute-start | bytes 393224 | tf_op jit(solution)/shard_map/ppermute | solution.py:199
  7.4 13.0 %collective-permute-start.1 = (bf16[128,512]{1,0:T(8,128)(2,1)S(1)}, bf16[128,512]{1,0:T(8,128)(2,1)S(1)}, u32[]{:S(2)}, u32[]{:S(2)}) collective-permute-start(bf16[128,512]{1,0:T(8,128)(2,1)S(1)} %pad_maximum_fusion.refs_0_), channel_id=1, source_target_pairs={{0,4},{4,0},{1,5},{5,1},{2,6},{6,2},{3,7},{7,3},{8,12},{12,8},{9,1... | collective-permute-start | bytes 393224 | tf_op jit(solution)/shard_map/ppermute | solution.py:225
  9.0 26.5 %collective-permute-start = (bf16[128,2048]{1,0:T(8,128)(2,1)S(1)}, bf16[128,2048]{1,0:T(8,128)(2,1)S(1)}, u32[]{:S(2)}, u32[]{:S(2)}) collective-permute-start(bf16[128,2048]{1,0:T(8,128)(2,1)S(1)} %slice.20), channel_id=1, source_target_pairs={{0,4},{4,0},{1,5},{5,1},{2,6},{6,2},{3,7},{7,3},{8,12},{12,8},{9,1... | collective-permute-start | bytes 1572872 | tf_op jit(solution)/shard_map/ppermute | solution.py:227
  9.6 0.7 %copy-start.2 = (s32[1,4,4,4]{3,2,1,0:T(4,128)S(1)}, s32[1,4,4,4]{3,2,1,0:T(4,128)}, u32[]{:S(2)}) copy-start(s32[1,4,4,4]{3,2,1,0:T(4,128)} %lists_ref.1) | copy-start | bytes 772
  9.6 0.7 %copy-start.3 = (s32[1,2]{1,0:T(1,128)S(1)}, s32[1,2]{1,0:T(1,128)}, u32[]{:S(2)}) copy-start(s32[1,2]{1,0:T(1,128)} %globals_ref.1) | copy-start | bytes 28
  9.6 0.7 %copy-start.4 = (s32[1,4]{1,0:T(1,128)S(1)}, s32[1,4]{1,0:T(1,128)}, u32[]{:S(2)}) copy-start(s32[1,4]{1,0:T(1,128)} %docs_ref.1) | copy-start | bytes 52
  11.1 14.5 %collective-permute-start.11 = (bf16[128,512]{1,0:T(8,128)(2,1)S(1)}, bf16[128,512]{1,0:T(8,128)(2,1)S(1)}, u32[]{:S(2)}, u32[]{:S(2)}) collective-permute-start(bf16[128,512]{1,0:T(8,128)(2,1)S(1)} %pad_maximum_fusion.refs_0_), channel_id=1, source_target_pairs={{0,8},{1,2},{2,1},{3,11},{8,0},{9,10},{10,9},{11,3},{16,24},{17,18... | collective-permute-start | bytes 393224 | tf_op jit(solution)/shard_map/ppermute | solution.py:199
  11.2 15.3 %collective-permute-start.10 = (bf16[128,512]{1,0:T(8,128)(2,1)S(1)}, bf16[128,512]{1,0:T(8,128)(2,1)S(1)}, u32[]{:S(2)}, u32[]{:S(2)}) collective-permute-start(bf16[128,512]{1,0:T(8,128)(2,1)S(1)} %pad_maximum_fusion.refs_0_), channel_id=1, source_target_pairs={{0,2},{1,3},{2,0},{3,1},{8,10},{9,11},{10,8},{11,9},{16,18},{17,19... | collective-permute-start | bytes 393224 | tf_op jit(solution)/shard_map/ppermute | solution.py:199
  18.8 6.9 %collective-permute-start.3 = (bf16[128,512]{1,0:T(8,128)(2,1)S(1)}, bf16[128,512]{1,0:T(8,128)(2,1)S(1)}, u32[]{:S(2)}, u32[]{:S(2)}) collective-permute-start(bf16[128,512]{1,0:T(8,128)(2,1)S(1)} %pad_maximum_fusion.refs_0_), channel_id=1, source_target_pairs={{0,1},{1,0},{2,3},{3,2},{8,9},{9,8},{10,11},{11,10},{16,17},{17,16... | collective-permute-start | bytes 393224 | tf_op jit(solution)/shard_map/ppermute | solution.py:199
  20.4 16.7 %collective-permute-start.9 = (bf16[128,2048]{1,0:T(8,128)(2,1)S(1)}, bf16[128,2048]{1,0:T(8,128)(2,1)S(1)}, u32[]{:S(2)}, u32[]{:S(2)}) collective-permute-start(bf16[128,2048]{1,0:T(8,128)(2,1)S(1)} %attend.4.refs_3_), channel_id=1, source_target_pairs={{0,4},{4,0},{1,5},{5,1},{2,6},{6,2},{3,7},{7,3},{8,12},{12,8},{9,1... | collective-permute-start | bytes 1572872 | tf_op jit(solution)/shard_map/ppermute | solution.py:231
  25.7 4.8 %collective-permute-start.6 = (bf16[128,512]{1,0:T(8,128)(2,1)S(1)}, bf16[128,512]{1,0:T(8,128)(2,1)S(1)}, u32[]{:S(2)}, u32[]{:S(2)}) collective-permute-start(bf16[128,512]{1,0:T(8,128)(2,1)S(1)} %collective-permute-done.1.refs_0_), channel_id=1, source_target_pairs={{0,8},{1,2},{2,1},{3,11},{8,0},{9,10},{10,9},{11,3},{16,24},{17,18... | collective-permute-start | bytes 393224 | tf_op jit(solution)/shard_map/ppermute | solution.py:199
  25.7 9.7 %collective-permute-start.5 = (bf16[128,512]{1,0:T(8,128)(2,1)S(1)}, bf16[128,512]{1,0:T(8,128)(2,1)S(1)}, u32[]{:S(2)}, u32[]{:S(2)}) collective-permute-start(bf16[128,512]{1,0:T(8,128)(2,1)S(1)} %collective-permute-done.1.refs_0_), channel_id=1, source_target_pairs={{0,2},{1,3},{2,0},{3,1},{8,10},{9,11},{10,8},{11,9},{16,18},{17,19... | collective-permute-start | bytes 393224 | tf_op jit(solution)/shard_map/ppermute | solution.py:199
  26.5 9.0 %collective-permute-start.4 = (bf16[128,512]{1,0:T(8,128)(2,1)S(1)}, bf16[128,512]{1,0:T(8,128)(2,1)S(1)}, u32[]{:S(2)}, u32[]{:S(2)}) collective-permute-start(bf16[128,512]{1,0:T(8,128)(2,1)S(1)} %collective-permute-done.1.refs_0_), channel_id=1, source_target_pairs={{0,1},{1,0},{2,3},{3,2},{8,9},{9,8},{10,11},{11,10},{16,17},{17,16... | collective-permute-start | bytes 393224 | tf_op jit(solution)/shard_map/ppermute | solution.py:199
  30.4 6.7 %copy-start = (bf16[1,1,128,4096]{3,2,1,0:T(8,128)(2,1)S(1)}, bf16[1,1,128,4096]{3,2,1,0:T(8,128)(2,1)}, u32[]{:S(2)}) copy-start(bf16[1,1,128,4096]{3,2,1,0:T(8,128)(2,1)} %param.11) | copy-start | bytes 3145732
  38.8 1.2 %collective-permute-start.12 = (f32[32,128]{1,0:T(8,128)S(1)}, f32[32,128]{1,0:T(8,128)S(1)}, u32[]{:S(2)}, u32[]{:S(2)}) collective-permute-start(f32[32,128]{1,0:T(8,128)S(1)} %get-tuple-element.13), channel_id=1, source_target_pairs={{0,8},{8,0},{16,24},{24,16},{1,9},{9,1},{17,25},{25,17},{2,10},{10... | collective-permute-start | bytes 49160 | tf_op jit(solution)/shard_map/ppermute | solution.py:163
  40.0 5.9 %collective-permute-start.16 = (f32[32,128]{1,0:T(8,128)S(1)}, f32[32,128]{1,0:T(8,128)S(1)}, u32[]{:S(2)}, u32[]{:S(2)}) collective-permute-start(f32[32,128]{1,0:T(8,128)S(1)} %add.23), channel_id=1, source_target_pairs={{0,3},{1,2},{2,1},{3,0},{8,27},{9,26},{10,25},{11,24},{16,19},{17,... | collective-permute-start | bytes 49160 | tf_op jit(solution)/shard_map/ppermute | solution.py:184
  42.2 4.6 %collective-permute-start.15 = (f32[32,128]{1,0:T(8,128)S(1)}, f32[32,128]{1,0:T(8,128)S(1)}, u32[]{:S(2)}, u32[]{:S(2)}) collective-permute-start(f32[32,128]{1,0:T(8,128)S(1)} %add.23), channel_id=1, source_target_pairs={{0,2},{1,3},{2,0},{3,1},{8,26},{9,27},{10,24},{11,25},{16,18},{17,... | collective-permute-start | bytes 49160 | tf_op jit(solution)/shard_map/ppermute | solution.py:184
  42.2 4.6 %collective-permute-start.14 = (f32[32,128]{1,0:T(8,128)S(1)}, f32[32,128]{1,0:T(8,128)S(1)}, u32[]{:S(2)}, u32[]{:S(2)}) collective-permute-start(f32[32,128]{1,0:T(8,128)S(1)} %add.23), channel_id=1, source_target_pairs={{0,1},{1,0},{2,3},{3,2},{8,25},{9,24},{10,27},{11,26},{16,17},{17,... | collective-permute-start | bytes 49160 | tf_op jit(solution)/shard_map/ppermute | solution.py:184
  44.4 3.7 %collective-permute-start.13 = (f32[32,128]{1,0:T(8,128)S(1)}, f32[32,128]{1,0:T(8,128)S(1)}, u32[]{:S(2)}, u32[]{:S(2)}) collective-permute-start(f32[32,128]{1,0:T(8,128)S(1)} %add.23), channel_id=1, source_target_pairs={{0,16},{1,17},{2,18},{3,19},{8,24},{9,25},{10,26},{11,27},{16,0},{... | collective-permute-start | bytes 49160 | tf_op jit(solution)/shard_map/ppermute | solution.py:184
  48.1 1.2 %collective-permute-start.17 = (f32[32,128]{1,0:T(8,128)S(1)}, f32[32,128]{1,0:T(8,128)S(1)}, u32[]{:S(2)}, u32[]{:S(2)}) collective-permute-start(f32[32,128]{1,0:T(8,128)S(1)} %add_add_fusion), channel_id=1, source_target_pairs={{0,8},{8,0},{16,24},{24,16},{1,9},{9,1},{17,25},{25,17},{2,10},{10... | collective-permute-start | bytes 49160 | tf_op jit(solution)/shard_map/ppermute | solution.py:163

commit v4 on v3

--- a/solution.py
+++ b/solution.py
@@ -14,13 +14,15 @@
 RAND = 4
 GLOBALS = 2
 GROUP = 8
-PART = 2
-PARTS = KVH // PART
+EARLY = 2
+GROUPS = (range(EARLY), range(EARLY, KVH))
+PARTS = len(GROUPS)
 NEVER = -1e30
 LEVELS = 8
 SCALE = math.log2(math.e) / math.sqrt(HD)
 VMEM = pl.BlockSpec(memory_space=pltpu.VMEM)
 SMEM = pl.BlockSpec(memory_space=pltpu.SMEM)
+ANY = pl.BlockSpec(memory_space=pl.ANY)
 
 
 def count_docs(doc_ends, positions):
@@ -66,14 +68,23 @@
     )(*scalars)
 
 
-def attend_kernel(part, base, weights_ref, q_ref, *refs):
+def attend_kernel(heads, key_base, value_base, place_ref, weights_ref, q_ref, *refs):
     kv_refs, out_ref = refs[:-1], refs[-1]
     rows = q_ref.shape[0]
-    for index in range(PART):
-        bias = weights_ref[pl.ds(0, rows), :] + weights_ref[pl.ds(rows + part * PART + index, 1), :]
+    slots = weights_ref.shape[1] // rows
+    at_end = (place_ref[0] == 0) | (place_ref[0] == slots - 1)
+
+    def blocks(column):
+        found = [ref[:, pl.ds(column, HD)] for ref in kv_refs]
+        if len(found) > slots:
+            found[2] = jnp.where(at_end, found[slots], found[2])
+        return jnp.concatenate(found[:slots], axis=0)
+
+    for index, head in enumerate(heads):
+        bias = weights_ref[pl.ds(0, rows), :] + weights_ref[pl.ds(rows + head, 1), :]
         bias = jnp.concatenate([bias, bias], axis=0)
-        keys = jnp.concatenate([ref[:, pl.ds(base + index * HD, HD)] for ref in kv_refs], axis=0)
-        values = jnp.concatenate([ref[:, pl.ds(base + (PART + index) * HD, HD)] for ref in kv_refs], axis=0)
+        keys = blocks(key_base + index * HD)
+        values = blocks(value_base + index * HD)
         values = jnp.concatenate([values, jnp.ones_like(values)], axis=1)
         for pair in range(GROUP // 2):
             first = (index * GROUP + 2 * pair) * HD
@@ -93,50 +104,58 @@
             out_ref[:, pl.ds(first + HD, HD)] = result[rows:]
 
 
-def attend(part, weights, queries, query_part, kv_slots, base=0):
-    rows = queries.shape[0]
-    width = PART * GROUP * HD
-    keys = rows * len(kv_slots)
+def attend(heads, place, weights, queries, kv_slots, key_base, value_base, effort):
+    rows, width = queries.shape
+    keys = weights.shape[1]
     return pl.pallas_call(
-        functools.partial(attend_kernel, part, base),
-        grid=(1,),
+        functools.partial(attend_kernel, heads, key_base, value_base),
         out_shape=jax.ShapeDtypeStruct((rows, width), jnp.bfloat16),
-        in_specs=[
-            VMEM,
-            pl.BlockSpec((rows, width), lambda step: (0, query_part)),
-        ]
-        + [VMEM] * len(kv_slots),
+        in_specs=[SMEM] + [VMEM] * (2 + len(kv_slots)),
         out_specs=VMEM,
-        compiler_params=pltpu.CompilerParams(vmem_limit_bytes=40 << 20),
+        compiler_params=pltpu.CompilerParams(vmem_limit_bytes=16 << 20),
         cost_estimate=pl.CostEstimate(
-            flops=120 * rows * width * keys,
-            bytes_accessed=4 * rows * width + 4 * keys * PART * HD,
-            transcendentals=rows * PART * GROUP * keys,
+            flops=effort * rows * width * keys,
+            bytes_accessed=4 * rows * width + 4 * keys * len(heads) * HD,
+            transcendentals=rows * width * keys // HD,
         ),
         name="attend",
-    )(weights, queries, *kv_slots)
+    )(place, weights, queries, *kv_slots)
 
 
 def finish_kernel(scale, last_ref, cotangent_ref, *refs):
     arrived_refs, handed_refs = refs[:PARTS], refs[PARTS : 2 * PARTS]
-    stream_ref, share_ref = refs[2 * PARTS :]
-    rows, width = handed_refs[0].shape
+    out_ref, share_ref, cotangent, stream, arrived_last, sems = refs[2 * PARTS :]
+    rows, features = stream.shape
+    last_copy = pltpu.make_async_copy(arrived_refs[-1], arrived_last, sems.at[0])
+    last_copy.start()
+    cotangent_copy = pltpu.make_async_copy(cotangent_ref, cotangent, sems.at[1])
+    cotangent_copy.start()
     is_last = last_ref[0] == 1
     squares = jnp.zeros((rows, HD), jnp.float32)
+    done = 0
     for part in range(PARTS):
-        for column in range(0, width, HD):
+        source = arrived_refs[part]
+        if part == PARTS - 1:
+            last_copy.wait()
+            source = arrived_last
+        for column in range(0, source.shape[1], HD):
             handed = handed_refs[part][:, pl.ds(column, HD)].astype(jnp.float32)
-            arrived = arrived_refs[part][:, pl.ds(column, HD)].astype(jnp.float32)
+            arrived = source[:, pl.ds(column, HD)].astype(jnp.float32)
             total = jnp.where(is_last, handed + arrived, handed).astype(jnp.bfloat16)
-            stream_ref[:, pl.ds(part * width + column, HD)] = total
+            stream[:, pl.ds(done + column, HD)] = total
             widened = total.astype(jnp.float32)
             squares += widened * widened
-    mean = jnp.sum(squares, axis=1, keepdims=True) / (PARTS * width)
+        done += source.shape[1]
+    store_copy = pltpu.make_async_copy(stream, out_ref, sems.at[2])
+    store_copy.start()
+    mean = jnp.sum(squares, axis=1, keepdims=True) / features
     inverse = lax.rsqrt(mean + 1e-06) * scale
-    for tile in range(PARTS * width // HD):
+    cotangent_copy.wait()
+    for tile in range(features // HD):
         columns = pl.ds(tile * HD, HD)
-        term = cotangent_ref[:, columns].astype(jnp.float32) * stream_ref[:, columns].astype(jnp.float32)
+        term = cotangent[:, columns].astype(jnp.float32) * stream[:, columns].astype(jnp.float32)
         share_ref[pl.ds(tile, 1), :] = jnp.sum(term * inverse, axis=0, keepdims=True)
+    store_copy.wait()
 
 
 def finish(is_last, cotangent, arrived, handed, scale):
@@ -147,14 +166,41 @@
             jax.ShapeDtypeStruct((rows, features), jnp.bfloat16),
             jax.ShapeDtypeStruct((features // HD, HD), jnp.float32),
         ),
-        in_specs=[SMEM] + [VMEM] * (1 + 2 * PARTS),
-        out_specs=(VMEM, VMEM),
-        compiler_params=pltpu.CompilerParams(vmem_limit_bytes=40 << 20),
+        in_specs=[SMEM, ANY] + [VMEM] * (PARTS - 1) + [ANY] + [VMEM] * PARTS,
+        out_specs=(ANY, VMEM),
+        scratch_shapes=[
+            pltpu.VMEM((rows, features), jnp.bfloat16),
+            pltpu.VMEM((rows, features), jnp.bfloat16),
+            pltpu.VMEM(arrived[-1].shape, jnp.bfloat16),
+            pltpu.SemaphoreType.DMA((3,)),
+        ],
+        compiler_params=pltpu.CompilerParams(vmem_limit_bytes=16 << 20),
         cost_estimate=pl.CostEstimate(
             flops=10 * rows * features, bytes_accessed=8 * rows * features, transcendentals=rows
         ),
         name="finish",
     )(is_last, cotangent, *arrived, *handed)
+
+
+def split_kernel(queries_ref, *out_refs):
+    done = 0
+    for out_ref in out_refs:
+        out_ref[...] = queries_ref[:, pl.ds(done, out_ref.shape[1])]
+        done += out_ref.shape[1]
+
+
+def split(queries):
+    rows = queries.shape[0]
+    return pl.pallas_call(
+        split_kernel,
+        out_shape=[
+            jax.ShapeDtypeStruct((rows, len(heads) * GROUP * HD), jnp.bfloat16) for heads in GROUPS
+        ],
+        in_specs=[VMEM],
+        out_specs=[VMEM] * PARTS,
+        compiler_params=pltpu.CompilerParams(vmem_limit_bytes=16 << 20),
+        name="split",
+    )(queries)
 
 
 def swapped_sum(value, axis, distances):
@@ -186,18 +232,19 @@
     return swapped_sum(value, "dp", [1])
 
 
+def fetch(value, slot):
+    count, replicas = lax.axis_size("ctx"), lax.axis_size("dp")
+    pairs = []
+    for replica in range(replicas):
+        for place in range(count):
+            near = abs(place - (place ^ slot)) <= count // 2
+            partner = (replica, place ^ slot) if near else (replica ^ 1, place)
+            pairs.append((replica * count + place, partner[0] * count + partner[1]))
+    return lax.ppermute(value, ("dp", "ctx"), pairs)
+
+
 def gather_slots(value):
-    count, replicas = lax.axis_size("ctx"), lax.axis_size("dp")
-    slots = [value]
-    for slot in range(1, count):
-        pairs = []
-        for replica in range(replicas):
-            for place in range(count):
-                near = abs(place - (place ^ slot)) <= count // 2
-                partner = (replica, place ^ slot) if near else (replica ^ 1, place)
-                pairs.append((replica * count + place, partner[0] * count + partner[1]))
-        slots.append(lax.ppermute(value, ("dp", "ctx"), pairs))
-    return slots
+    return [value] + [fetch(value, slot) for slot in range(1, lax.axis_size("ctx"))]
 
 
 def per_device(queries, keys_values, random_blocks, global_blocks, doc_lengths, cotangent):
@@ -207,32 +254,35 @@
     section_count = lax.axis_size("section")
     section_place = lax.axis_index("section")
     half = KVH * HD
-    kv_width = PART * HD
-    parts = []
-    for part in range(PARTS):
-        first = part * kv_width
-        parts.append(
-            jnp.concatenate(
-                [
-                    keys_values[:, first : first + kv_width],
-                    keys_values[:, half + first : half + first + kv_width],
-                ],
-                axis=1,
-            )
-        )
+    early_width = EARLY * HD
+    early_heads, late_heads = GROUPS
     weights = weigh(scalars, queries.shape[0], lax.axis_size("ctx"))
     first_hop = [(0, 1), (1, 0)]
-    early_kv = lax.ppermute(parts[0], "section", first_hop)
-    late_slots = gather_slots(parts[1])
-    early_queries = lax.ppermute(queries[:, : PART * GROUP * HD], "section", first_hop)
-    own_kv, late_slots[1] = lax.optimization_barrier((parts[0], late_slots[1]))
-    own_slots = gather_slots(own_kv)
-    late = attend(1, weights, queries, 1, late_slots)
+    kv_parts = []
+    for heads in GROUPS:
+        first, last = heads[0] * HD, (heads[-1] + 1) * HD
+        kv_parts.append(
+            jnp.concatenate([keys_values[:, first:last], keys_values[:, half + first : half + last]], axis=1)
+        )
+    early_kv = lax.ppermute(kv_parts[0], "section", first_hop)
+    late_slots = gather_slots(kv_parts[1])
+    queries = list(split(queries))
+    early_queries = lax.ppermute(queries[0], "section", first_hop)
+    both = jnp.concatenate([kv_parts[0], early_kv], axis=1)
+    late_slots[1], early_kv = lax.optimization_barrier((late_slots[1], early_kv))
+    late = attend(late_heads, place, weights, queries[1], late_slots, 0, half - early_width, 120)
     arrived_late = lax.ppermute(late, "section", first_hop)
-    early_kv, own_slots[1] = lax.optimization_barrier((early_kv, own_slots[1]))
-    early_slots = gather_slots(early_kv)
-    own = attend(0, weights, queries, 0, own_slots)
-    arrived = [attend(0, weights, early_queries, 0, early_slots), arrived_late]
+    if lax.axis_size("ctx") == 4:
+        first, third = fetch(both, 1), fetch(both, 3)
+        third, early_queries = lax.optimization_barrier((third, early_queries))
+        both_slots = [both, first, fetch(first, 3), third, fetch(third, 1)]
+    else:
+        both_slots = gather_slots(both)
+    own = attend(early_heads, place, weights, queries[0], both_slots, 0, early_width, 1)
+    early = attend(
+        early_heads, place, weights, early_queries, both_slots, 2 * early_width, 3 * early_width, 1
+    )
+    arrived = [early, arrived_late]
     handed = [own, late]
     for step in range(2, section_count):
         on_step = section_place == step - 1

time: 50.2 us -> 49 us (0.976)
  starting transfers between devices: 23.9 us -> 17.7 us
  waiting for transfers between devices: 15.6 us -> 19.1 us
  local copies, waits for them, and re-layouts: 1.79 us -> 2.52 us
  Pallas kernels: 7.33 us -> 7.98 us
    ppermute x11 -> x9, starting transfers between devices: 16.2 us -> 11.1 us  [the longest x7 7.55 us: fetch(): return lax.ppermute(value, ('dp', 'ctx'), pairs)]
    ppermute x11 -> x9, waiting for transfers between devices: 11.1 us -> 14.6 us  [the longest x7 11.4 us: fetch(): return lax.ppermute(value, ('dp', 'ctx'), pairs)]
    ppermute x1, starting transfers between devices: 1.56 us -> 0.6 us  [per_device(): arrived_late = lax.ppermute(late, 'section', first_hop)]
    unnamed x10 -> x14, local copies, waits for them, and re-layouts: 0.71 us -> 1.47 us
    pallas_call x1, Pallas kernels: 1.69 us -> 2.28 us  [finish(): pl.pallas_call(functools.partial(finish_kernel, scale), out_shape=(jax.Sh...]
    pallas_call x3 -> x4, Pallas kernels: 4.84 us -> 4.9 us  [the longest x3 4.83 us: attend(): pl.pallas_call(functools.partial(attend_kernel, heads, key_base, value_ba...]
    slice x2 -> x1, local copies, waits for them, and re-layouts: 1.08 us -> 1.05 us  [per_device(): keys_values[:, first:last]]
  transfers between devices with their start and end apart: 18 -> 16, of which waited for: 8 -> 9; matrix products, arithmetic and copies ran while one was open for 0% -> 0% of each run, Pallas kernels for 11% -> 12%
where the time goes in v4:
time: 49 us; the launch traced here: 48.8 us
  waiting for transfers between devices  19.1 us (39%)
  starting transfers between devices  17.7 us (36%)
  Pallas kernels  7.98 us (16%)
  local copies, waits for them, and re-layouts  2.52 us (5%)
  between operations  0.76 us (2%)
  other arithmetic  0.66 us (1%)
    ppermute x7, waiting for transfers between devices, fetch(): return lax.ppermute(value, ('dp', 'ctx'), pairs)  11.4 us
    ppermute x7, starting transfers between devices, fetch(): return lax.ppermute(value, ('dp', 'ctx'), pairs)  7.55 us
    ppermute x4, starting transfers between devices, total_share(): heard.append(lax.ppermute(value, ('dp', 'ctx'), pairs))  5.91 us
    pallas_call x3, Pallas kernels, attend(): pl.pallas_call(functools.partial(attend_kernel, heads, key_base, value_ba...  4.83 us
    ppermute x1, waiting for transfers between devices, per_device(): early_queries = lax.ppermute(queries[0], 'section', first_hop)  3.27 us
    ppermute x1, starting transfers between devices, per_device(): early_kv = lax.ppermute(kv_parts[0], 'section', first_hop)  3 us
    ppermute x2, waiting for transfers between devices, swapped_sum(): lax.ppermute(value, axis, [(place, place ^ distance) for place in range(c...  2.34 us
    pallas_call x1, Pallas kernels, finish(): pl.pallas_call(functools.partial(finish_kernel, scale), out_shape=(jax.Sh...  2.28 us
  transfers between devices with their start and end apart: 16, of which 9 were waited for; matrix products, arithmetic and copies ran while one was open for 0% of the time, Pallas kernels for 12%

profile of v4, /device:TPU:0, one launch (start us, length us, event | category | flops | bytes accessed | tf_op | source)
XLA Modules:
  0.0 48.8 jit_solution(10543831021150732972)
XLA Ops:
  0.6 1.0 %fusion = (bf16[128,256]{1,0:T(8,128)(2,1)S(1)}, bf16[128,256]{1,0:T(8,128)(2,1)S(1)}, bf16[128,256]{1,0:T(8,128)(2,1)S(1)}, bf16[128,256]{1,0:T(8,128)(2,1)S(1)}) fusion(bf16[128,1024]{1,0:T(8,128)(2,1)} %bitcast.9), kind=kLoop, calls=%fused_computation.4 | loop fusion | bytes 524288 | tf_op jit(solution)/shard_map/slice | solution.py:265
  1.7 3.0 %collective-permute-start = (bf16[128,512]{1,0:T(8,128)(2,1)S(1)}, bf16[128,512]{1,0:T(8,128)(2,1)S(1)}, u32[]{:S(2)}, u32[]{:S(2)}) collective-permute-start(bf16[128,512]{1,0:T(8,128)(2,1)S(1)} %pad_maximum_fusion.1), channel_id=1, source_target_pairs={{0,4},{4,0},{1,5},{5,1},{2,6},{6,2},{3,7},{7,3},{8,12},{12,8},{9,1... | collective-permute-start | bytes 393224 | tf_op jit(solution)/shard_map/ppermute | solution.py:267
  4.7 1.6 %collective-permute-start.6 = (bf16[128,512]{1,0:T(8,128)(2,1)S(1)}, bf16[128,512]{1,0:T(8,128)(2,1)S(1)}, u32[]{:S(2)}, u32[]{:S(2)}) collective-permute-start(bf16[128,512]{1,0:T(8,128)(2,1)S(1)} %pad_maximum_fusion.2.refs_0_), channel_id=1, source_target_pairs={{0,1},{1,0},{2,3},{3,2},{8,9},{9,8},{10,11},{11,10},{16,17},{17,16... | collective-permute-start | bytes 393224 | tf_op jit(solution)/shard_map/ppermute | solution.py:243
  6.4 2.6 %collective-permute-start.7 = (bf16[128,512]{1,0:T(8,128)(2,1)S(1)}, bf16[128,512]{1,0:T(8,128)(2,1)S(1)}, u32[]{:S(2)}, u32[]{:S(2)}) collective-permute-start(bf16[128,512]{1,0:T(8,128)(2,1)S(1)} %pad_maximum_fusion.2.refs_0_), channel_id=1, source_target_pairs={{0,2},{1,3},{2,0},{3,1},{8,10},{9,11},{10,8},{11,9},{16,18},{17,19... | collective-permute-start | bytes 393224 | tf_op jit(solution)/shard_map/ppermute | solution.py:243
  9.0 0.8 %copy-done.5 = bf16[128,2048]{1,0:T(8,128)(2,1)} copy-done((bf16[128,2048]{1,0:T(8,128)(2,1)}, bf16[128,2048]{1,0:T(8,128)(2,1)S(1)}, u32[]{:S(2)}) %copy-start.5) | copy-done | bytes 524312
  11.0 0.8 %weigh.1.weights_ref = f32[136,512]{1,0:T(8,128)S(1)} custom-call(s32[1]{0:T(128)} %bitcast.2.place_ref, s32[1,4,4,4]{3,2,1,0:T(4,128)S(1)} %copy-done.2, s32[1,2]{1,0:T(1,128)S(1)} %copy-done.3, s32[1,4]{1,0:T(1,128)S(1)} %copy-done.4), custom_call_target="tpu_custom_call" | custom-call | tf_op jit(solution)/shard_map/weigh/pallas_call | solution.py:61
  12.2 2.2 %collective-permute-start.3 = (bf16[128,1024]{1,0:T(8,128)(2,1)S(1)}, bf16[128,1024]{1,0:T(8,128)(2,1)S(1)}, u32[]{:S(2)}, u32[]{:S(2)}) collective-permute-start(bf16[128,1024]{1,0:T(8,128)(2,1)S(1)} %pad_maximum_fusion.refs_0_), channel_id=1, source_target_pairs={{0,1},{1,0},{2,3},{3,2},{8,9},{9,8},{10,11},{11,10},{16,17},{17,16... | collective-permute-start | bytes 786440 | tf_op jit(solution)/shard_map/ppermute | solution.py:243
  14.4 1.8 %collective-permute-done.7.refs_2_ = bf16[128,512]{1,0:T(8,128)(2,1)S(1)} collective-permute-done((bf16[128,512]{1,0:T(8,128)(2,1)S(1)}, bf16[128,512]{1,0:T(8,128)(2,1)S(1)}, u32[]{:S(2)}, u32[]{:S(2)}) %collective-permute-start.7) | collective-permute-done | bytes 131104 | tf_op jit(solution)/shard_map/ppermute | solution.py:243
  16.3 1.7 %attend.4.refs_3_ = bf16[128,2048]{1,0:T(8,128)(2,1)S(1)} custom-call(s32[1]{0:T(128)} %bitcast.2.place_ref, f32[136,512]{1,0:T(8,128)S(1)} %weigh.1.weights_ref, bf16[128,2048]{1,0:T(8,128)(2,1)S(1)} %copy-done.6, bf16[128,512]{1,0:T(8,128)(2,1)S(1)} %pad_maximum_fusion.2.refs_0_, bf16[128,512]{1,0:T(8,128)(2,1)S(1)} %collective-permute-done.6.refs_1_, ...), custom_call_target="tpu_custom_call" | custom-call | flops 16106127360 | bytes 1572864 | tf_op jit(solution)/shard_map/attend/pallas_call | solution.py:110
  17.9 0.6 %collective-permute-start.9 = (bf16[128,2048]{1,0:T(8,128)(2,1)S(1)}, bf16[128,2048]{1,0:T(8,128)(2,1)}, u32[]{:S(2)}, u32[]{:S(2)}) collective-permute-start(bf16[128,2048]{1,0:T(8,128)(2,1)S(1)} %attend.4.refs_3_), channel_id=1, source_target_pairs={{0,4},{4,0},{1,5},{5,1},{2,6},{6,2},{3,7},{7,3},{8,12},{12,8},{9,1... | collective-permute-start | bytes 1572872 | tf_op jit(solution)/shard_map/ppermute | solution.py:274
  18.5 2.8 %collective-permute-done.3.refs_1_ = bf16[128,1024]{1,0:T(8,128)(2,1)S(1)} collective-permute-done((bf16[128,1024]{1,0:T(8,128)(2,1)S(1)}, bf16[128,1024]{1,0:T(8,128)(2,1)S(1)}, u32[]{:S(2)}, u32[]{:S(2)}) %collective-permute-start.3) | collective-permute-done | bytes 262176 | tf_op jit(solution)/shard_map/ppermute | solution.py:243
  21.3 3.3 %collective-permute-done.2.q_ref = bf16[128,2048]{1,0:T(8,128)(2,1)S(1)} collective-permute-done((bf16[128,2048]{1,0:T(8,128)(2,1)S(1)}, bf16[128,2048]{1,0:T(8,128)(2,1)S(1)}, u32[]{:S(2)}, u32[]{:S(2)}) %collective-permute-start.2) | collective-permute-done | bytes 524320 | tf_op jit(solution)/shard_map/ppermute | solution.py:270
  24.6 0.8 %collective-permute-start.5 = (bf16[128,1024]{1,0:T(8,128)(2,1)S(1)}, bf16[128,1024]{1,0:T(8,128)(2,1)S(1)}, u32[]{:S(2)}, u32[]{:S(2)}) collective-permute-start(bf16[128,1024]{1,0:T(8,128)(2,1)S(1)} %collective-permute-done.1.refs_3_), channel_id=1, source_target_pairs={{0,1},{1,0},{2,3},{3,2},{8,9},{9,8},{10,11},{11,10},{16,17},{17,16... | collective-permute-start | bytes 786440 | tf_op jit(solution)/shard_map/ppermute | solution.py:243
  25.3 6.8 %collective-permute-done.5.refs_4_ = bf16[128,1024]{1,0:T(8,128)(2,1)S(1)} collective-permute-done((bf16[128,1024]{1,0:T(8,128)(2,1)S(1)}, bf16[128,1024]{1,0:T(8,128)(2,1)S(1)}, u32[]{:S(2)}, u32[]{:S(2)}) %collective-permute-start.5) | collective-permute-done | bytes 262176 | tf_op jit(solution)/shard_map/ppermute | solution.py:243
  32.1 1.6 %attend.5.refs_2_ = bf16[128,2048]{1,0:T(8,128)(2,1)S(1)} custom-call(s32[1]{0:T(128)} %bitcast.2.place_ref, f32[136,512]{1,0:T(8,128)S(1)} %weigh.1.weights_ref, bf16[128,2048]{1,0:T(8,128)(2,1)S(1)} %get-tuple-element.9.q_ref, bf16[128,1024]{1,0:T(8,128)(2,1)S(1)} %pad_maximum_fusion.refs_0_, bf16[128,1024]{1,0:T(8,128)(2,1)S(1)} %collective-permute-done.3.refs_1_, ...), custom_call_target="tpu_custom_call" | custom-call | flops 134217728 | bytes 1572864 | tf_op jit(solution)/shard_map/attend/pallas_call | solution.py:110
  33.7 1.6 %attend.3.refs_0_ = bf16[128,2048]{1,0:T(8,128)(2,1)S(1)} custom-call(s32[1]{0:T(128)} %bitcast.2.place_ref, f32[136,512]{1,0:T(8,128)S(1)} %weigh.1.weights_ref, bf16[128,2048]{1,0:T(8,128)(2,1)S(1)} %collective-permute-done.2.q_ref, bf16[128,1024]{1,0:T(8,128)(2,1)S(1)} %pad_maximum_fusion.refs_0_, bf16[128,1024]{1,0:T(8,128)(2,1)S(1)} %collective-permute-done.3.refs_1_, ...), custom_call_target="tpu_custom_call" | custom-call | flops 134217728 | bytes 1572864 | tf_op jit(solution)/shard_map/attend/pallas_call | solution.py:110
  35.5 2.3 %finish.1 = (bf16[128,4096]{1,0:T(8,128)(2,1)}, f32[32,128]{1,0:T(8,128)S(1)}) custom-call(s32[1]{0:T(128)} %bitcast.last_ref, bf16[128,4096]{1,0:T(8,128)(2,1)S(1)} %bitcast.8, bf16[128,2048]{1,0:T(8,128)(2,1)S(1)} %attend.3.refs_0_, bf16[128,2048]{1,0:T(8,128)(2,1)} %collective-permute-done.9.refs_1_, bf16[128,2048]{1,0:T(8,128)(2,1)S(1)} %attend.5.refs_2_, ...), custom_call_target="tpu_custom_call" | custom-call | flops 5242880 | bytes 4194304 | tf_op jit(solution)/shard_map/finish/pallas_call | solution.py:163
  37.9 1.2 %collective-permute-done.10 = f32[32,128]{1,0:T(8,128)S(1)} collective-permute-done((f32[32,128]{1,0:T(8,128)S(1)}, f32[32,128]{1,0:T(8,128)S(1)}, u32[]{:S(2)}, u32[]{:S(2)}) %collective-permute-start.10) | collective-permute-done | bytes 16416 | tf_op jit(solution)/shard_map/ppermute | solution.py:209
  39.1 1.5 %collective-permute-start.11 = (f32[32,128]{1,0:T(8,128)S(1)}, f32[32,128]{1,0:T(8,128)S(1)}, u32[]{:S(2)}, u32[]{:S(2)}) collective-permute-start(f32[32,128]{1,0:T(8,128)S(1)} %add.23), channel_id=1, source_target_pairs={{0,16},{1,17},{2,18},{3,19},{8,24},{9,25},{10,26},{11,27},{16,0},{... | collective-permute-start | bytes 49160 | tf_op jit(solution)/shard_map/ppermute | solution.py:230
  40.7 0.7 %collective-permute-start.13 = (f32[32,128]{1,0:T(8,128)S(1)}, f32[32,128]{1,0:T(8,128)S(1)}, u32[]{:S(2)}, u32[]{:S(2)}) collective-permute-start(f32[32,128]{1,0:T(8,128)S(1)} %add.23), channel_id=1, source_target_pairs={{0,2},{1,3},{2,0},{3,1},{8,26},{9,27},{10,24},{11,25},{16,18},{17,... | collective-permute-start | bytes 49160 | tf_op jit(solution)/shard_map/ppermute | solution.py:230
  41.4 3.6 %collective-permute-start.14 = (f32[32,128]{1,0:T(8,128)S(1)}, f32[32,128]{1,0:T(8,128)S(1)}, u32[]{:S(2)}, u32[]{:S(2)}) collective-permute-start(f32[32,128]{1,0:T(8,128)S(1)} %add.23), channel_id=1, source_target_pairs={{0,3},{1,2},{2,1},{3,0},{8,27},{9,26},{10,25},{11,24},{16,19},{17,... | collective-permute-start | bytes 49160 | tf_op jit(solution)/shard_map/ppermute | solution.py:230
  45.5 1.4 %collective-permute-done.14 = f32[32,128]{1,0:T(8,128)S(1)} collective-permute-done((f32[32,128]{1,0:T(8,128)S(1)}, f32[32,128]{1,0:T(8,128)S(1)}, u32[]{:S(2)}, u32[]{:S(2)}) %collective-permute-start.14) | collective-permute-done | bytes 16416 | tf_op jit(solution)/shard_map/ppermute | solution.py:230
  47.0 1.2 %collective-permute-done.15 = f32[32,128]{1,0:T(8,128)S(1)} collective-permute-done((f32[32,128]{1,0:T(8,128)S(1)}, f32[32,128]{1,0:T(8,128)S(1)}, u32[]{:S(2)}, u32[]{:S(2)}) %collective-permute-start.15) | collective-permute-done | bytes 16416 | tf_op jit(solution)/shard_map/ppermute | solution.py:209
  48.2 0.6 %add.28 = f32[32,128]{1,0:T(8,128)} add(f32[32,128]{1,0:T(8,128)S(1)} %add_add_fusion, f32[32,128]{1,0:T(8,128)S(1)} %collective-permute-done.15) | non-fusion elementwise | flops 4096 | bytes 49152 | tf_op jit(solution)/shard_map/add | solution.py:209
  (35 shorter events, 2.6 us)
Async XLA Ops:
  0.6 8.3 %copy-start = (bf16[1,1,128,4096]{3,2,1,0:T(8,128)(2,1)S(1)}, bf16[1,1,128,4096]{3,2,1,0:T(8,128)(2,1)}, u32[]{:S(2)}) copy-start(bf16[1,1,128,4096]{3,2,1,0:T(8,128)(2,1)} %param.6) | copy-start | bytes 3145732
  1.7 10.1 %collective-permute-start = (bf16[128,512]{1,0:T(8,128)(2,1)S(1)}, bf16[128,512]{1,0:T(8,128)(2,1)S(1)}, u32[]{:S(2)}, u32[]{:S(2)}) collective-permute-start(bf16[128,512]{1,0:T(8,128)(2,1)S(1)} %pad_maximum_fusion.1), channel_id=1, source_target_pairs={{0,4},{4,0},{1,5},{5,1},{2,6},{6,2},{3,7},{7,3},{8,12},{12,8},{9,1... | collective-permute-start | bytes 393224 | tf_op jit(solution)/shard_map/ppermute | solution.py:267
  4.7 7.5 %collective-permute-start.6 = (bf16[128,512]{1,0:T(8,128)(2,1)S(1)}, bf16[128,512]{1,0:T(8,128)(2,1)S(1)}, u32[]{:S(2)}, u32[]{:S(2)}) collective-permute-start(bf16[128,512]{1,0:T(8,128)(2,1)S(1)} %pad_maximum_fusion.2.refs_0_), channel_id=1, source_target_pairs={{0,1},{1,0},{2,3},{3,2},{8,9},{9,8},{10,11},{11,10},{16,17},{17,16... | collective-permute-start | bytes 393224 | tf_op jit(solution)/shard_map/ppermute | solution.py:243
  6.4 9.9 %collective-permute-start.7 = (bf16[128,512]{1,0:T(8,128)(2,1)S(1)}, bf16[128,512]{1,0:T(8,128)(2,1)S(1)}, u32[]{:S(2)}, u32[]{:S(2)}) collective-permute-start(bf16[128,512]{1,0:T(8,128)(2,1)S(1)} %pad_maximum_fusion.2.refs_0_), channel_id=1, source_target_pairs={{0,2},{1,3},{2,0},{3,1},{8,10},{9,11},{10,8},{11,9},{16,18},{17,19... | collective-permute-start | bytes 393224 | tf_op jit(solution)/shard_map/ppermute | solution.py:243
  9.0 7.3 %collective-permute-start.8 = (bf16[128,512]{1,0:T(8,128)(2,1)S(1)}, bf16[128,512]{1,0:T(8,128)(2,1)S(1)}, u32[]{:S(2)}, u32[]{:S(2)}) collective-permute-start(bf16[128,512]{1,0:T(8,128)(2,1)S(1)} %pad_maximum_fusion.2.refs_0_), channel_id=1, source_target_pairs={{0,8},{1,2},{2,1},{3,11},{8,0},{9,10},{10,9},{11,3},{16,24},{17,18... | collective-permute-start | bytes 393224 | tf_op jit(solution)/shard_map/ppermute | solution.py:243
  9.0 0.8 %copy-start.5 = (bf16[128,2048]{1,0:T(8,128)(2,1)}, bf16[128,2048]{1,0:T(8,128)(2,1)S(1)}, u32[]{:S(2)}) copy-start(bf16[128,2048]{1,0:T(8,128)(2,1)S(1)} %get-tuple-element.12.q_ref) | copy-start | bytes 1572868
  9.8 0.7 %copy-start.2 = (s32[1,4,4,4]{3,2,1,0:T(4,128)S(1)}, s32[1,4,4,4]{3,2,1,0:T(4,128)}, u32[]{:S(2)}) copy-start(s32[1,4,4,4]{3,2,1,0:T(4,128)} %lists_ref.1) | copy-start | bytes 772
  9.8 14.7 %collective-permute-start.2 = (bf16[128,2048]{1,0:T(8,128)(2,1)S(1)}, bf16[128,2048]{1,0:T(8,128)(2,1)S(1)}, u32[]{:S(2)}, u32[]{:S(2)}) collective-permute-start(bf16[128,2048]{1,0:T(8,128)(2,1)S(1)} %get-tuple-element.9.q_ref), channel_id=1, source_target_pairs={{0,4},{4,0},{1,5},{5,1},{2,6},{6,2},{3,7},{7,3},{8,12},{12,8},{9,1... | collective-permute-start | bytes 1572872 | tf_op jit(solution)/shard_map/ppermute | solution.py:270
  10.4 0.7 %copy-start.3 = (s32[1,2]{1,0:T(1,128)S(1)}, s32[1,2]{1,0:T(1,128)}, u32[]{:S(2)}) copy-start(s32[1,2]{1,0:T(1,128)} %globals_ref.1) | copy-start | bytes 28
  10.4 0.7 %copy-start.4 = (s32[1,4]{1,0:T(1,128)S(1)}, s32[1,4]{1,0:T(1,128)}, u32[]{:S(2)}) copy-start(s32[1,4]{1,0:T(1,128)} %docs_ref.1) | copy-start | bytes 52
  10.4 5.9 %copy-start.6 = (bf16[128,2048]{1,0:T(8,128)(2,1)S(1)}, bf16[128,2048]{1,0:T(8,128)(2,1)}, u32[]{:S(2)}) copy-start(bf16[128,2048]{1,0:T(8,128)(2,1)} %copy-done.5) | copy-start | bytes 1572868
  11.9 9.4 %collective-permute-start.1 = (bf16[128,1024]{1,0:T(8,128)(2,1)S(1)}, bf16[128,1024]{1,0:T(8,128)(2,1)S(1)}, u32[]{:S(2)}, u32[]{:S(2)}) collective-permute-start(bf16[128,1024]{1,0:T(8,128)(2,1)S(1)} %pad_maximum_fusion.refs_0_), channel_id=1, source_target_pairs={{0,8},{1,2},{2,1},{3,11},{8,0},{9,10},{10,9},{11,3},{16,24},{17,18... | collective-permute-start | bytes 786440 | tf_op jit(solution)/shard_map/ppermute | solution.py:243
  12.2 9.1 %collective-permute-start.3 = (bf16[128,1024]{1,0:T(8,128)(2,1)S(1)}, bf16[128,1024]{1,0:T(8,128)(2,1)S(1)}, u32[]{:S(2)}, u32[]{:S(2)}) collective-permute-start(bf16[128,1024]{1,0:T(8,128)(2,1)S(1)} %pad_maximum_fusion.refs_0_), channel_id=1, source_target_pairs={{0,1},{1,0},{2,3},{3,2},{8,9},{9,8},{10,11},{11,10},{16,17},{17,16... | collective-permute-start | bytes 786440 | tf_op jit(solution)/shard_map/ppermute | solution.py:243
  17.9 17.6 %collective-permute-start.9 = (bf16[128,2048]{1,0:T(8,128)(2,1)S(1)}, bf16[128,2048]{1,0:T(8,128)(2,1)}, u32[]{:S(2)}, u32[]{:S(2)}) collective-permute-start(bf16[128,2048]{1,0:T(8,128)(2,1)S(1)} %attend.4.refs_3_), channel_id=1, source_target_pairs={{0,4},{4,0},{1,5},{5,1},{2,6},{6,2},{3,7},{7,3},{8,12},{12,8},{9,1... | collective-permute-start | bytes 1572872 | tf_op jit(solution)/shard_map/ppermute | solution.py:274
  21.3 4.1 %collective-permute-start.4 = (bf16[128,1024]{1,0:T(8,128)(2,1)S(1)}, bf16[128,1024]{1,0:T(8,128)(2,1)S(1)}, u32[]{:S(2)}, u32[]{:S(2)}) collective-permute-start(bf16[128,1024]{1,0:T(8,128)(2,1)S(1)} %collective-permute-done.3.refs_1_), channel_id=1, source_target_pairs={{0,8},{1,2},{2,1},{3,11},{8,0},{9,10},{10,9},{11,3},{16,24},{17,18... | collective-permute-start | bytes 786440 | tf_op jit(solution)/shard_map/ppermute | solution.py:243
  24.6 7.6 %collective-permute-start.5 = (bf16[128,1024]{1,0:T(8,128)(2,1)S(1)}, bf16[128,1024]{1,0:T(8,128)(2,1)S(1)}, u32[]{:S(2)}, u32[]{:S(2)}) collective-permute-start(bf16[128,1024]{1,0:T(8,128)(2,1)S(1)} %collective-permute-done.1.refs_3_), channel_id=1, source_target_pairs={{0,1},{1,0},{2,3},{3,2},{8,9},{9,8},{10,11},{11,10},{16,17},{17,16... | collective-permute-start | bytes 786440 | tf_op jit(solution)/shard_map/ppermute | solution.py:243
  33.7 1.8 %copy-start.1 = (bf16[1,1,128,4096]{3,2,1,0:T(8,128)(2,1)S(1)}, bf16[1,1,128,4096]{3,2,1,0:T(8,128)(2,1)}, u32[]{:S(2)}) copy-start(bf16[1,1,128,4096]{3,2,1,0:T(8,128)(2,1)} %param.11) | copy-start | bytes 3145732
  37.8 1.2 %collective-permute-start.10 = (f32[32,128]{1,0:T(8,128)S(1)}, f32[32,128]{1,0:T(8,128)S(1)}, u32[]{:S(2)}, u32[]{:S(2)}) collective-permute-start(f32[32,128]{1,0:T(8,128)S(1)} %get-tuple-element.15), channel_id=1, source_target_pairs={{0,8},{8,0},{16,24},{24,16},{1,9},{9,1},{17,25},{25,17},{2,10},{10... | collective-permute-start | bytes 49160 | tf_op jit(solution)/shard_map/ppermute | solution.py:209
  39.1 5.9 %collective-permute-start.11 = (f32[32,128]{1,0:T(8,128)S(1)}, f32[32,128]{1,0:T(8,128)S(1)}, u32[]{:S(2)}, u32[]{:S(2)}) collective-permute-start(f32[32,128]{1,0:T(8,128)S(1)} %add.23), channel_id=1, source_target_pairs={{0,16},{1,17},{2,18},{3,19},{8,24},{9,25},{10,26},{11,27},{16,0},{... | collective-permute-start | bytes 49160 | tf_op jit(solution)/shard_map/ppermute | solution.py:230
  40.6 4.4 %collective-permute-start.12 = (f32[32,128]{1,0:T(8,128)S(1)}, f32[32,128]{1,0:T(8,128)S(1)}, u32[]{:S(2)}, u32[]{:S(2)}) collective-permute-start(f32[32,128]{1,0:T(8,128)S(1)} %add.23), channel_id=1, source_target_pairs={{0,1},{1,0},{2,3},{3,2},{8,25},{9,24},{10,27},{11,26},{16,17},{17,... | collective-permute-start | bytes 49160 | tf_op jit(solution)/shard_map/ppermute | solution.py:230
  40.7 4.8 %collective-permute-start.13 = (f32[32,128]{1,0:T(8,128)S(1)}, f32[32,128]{1,0:T(8,128)S(1)}, u32[]{:S(2)}, u32[]{:S(2)}) collective-permute-start(f32[32,128]{1,0:T(8,128)S(1)} %add.23), channel_id=1, source_target_pairs={{0,2},{1,3},{2,0},{3,1},{8,26},{9,27},{10,24},{11,25},{16,18},{17,... | collective-permute-start | bytes 49160 | tf_op jit(solution)/shard_map/ppermute | solution.py:230
  41.4 5.5 %collective-permute-start.14 = (f32[32,128]{1,0:T(8,128)S(1)}, f32[32,128]{1,0:T(8,128)S(1)}, u32[]{:S(2)}, u32[]{:S(2)}) collective-permute-start(f32[32,128]{1,0:T(8,128)S(1)} %add.23), channel_id=1, source_target_pairs={{0,3},{1,2},{2,1},{3,0},{8,27},{9,26},{10,25},{11,24},{16,19},{17,... | collective-permute-start | bytes 49160 | tf_op jit(solution)/shard_map/ppermute | solution.py:230
  46.9 1.2 %collective-permute-start.15 = (f32[32,128]{1,0:T(8,128)S(1)}, f32[32,128]{1,0:T(8,128)S(1)}, u32[]{:S(2)}, u32[]{:S(2)}) collective-permute-start(f32[32,128]{1,0:T(8,128)S(1)} %add_add_fusion), channel_id=1, source_target_pairs={{0,8},{8,0},{16,24},{24,16},{1,9},{9,1},{17,25},{25,17},{2,10},{10... | collective-permute-start | bytes 49160 | tf_op jit(solution)/shard_map/ppermute | solution.py:209

commit v5 on v4

--- a/solution.py
+++ b/solution.py
@@ -68,9 +68,17 @@
     )(*scalars)
 
 
-def attend_kernel(heads, key_base, value_base, place_ref, weights_ref, q_ref, *refs):
-    kv_refs, out_ref = refs[:-1], refs[-1]
+def attend_kernel(heads, query_base, key_base, value_base, kv_count, place_ref, weights_ref, q_ref, *refs):
+    kv_refs, out_ref, scratch = refs[:kv_count], refs[kv_count], refs[kv_count + 1 :]
     rows = q_ref.shape[0]
+    copies = []
+    if scratch:
+        for index in range(len(heads)):
+            columns = pl.ds(index * GROUP * HD, GROUP * HD)
+            source = q_ref.at[:, pl.ds(query_base + index * GROUP * HD, GROUP * HD)]
+            copies.append(pltpu.make_async_copy(source, scratch[0].at[:, columns], scratch[1].at[index]))
+            copies[-1].start()
+        q_ref, query_base = scratch[0], 0
     slots = weights_ref.shape[1] // rows
     at_end = (place_ref[0] == 0) | (place_ref[0] == slots - 1)
 
@@ -86,10 +94,13 @@
         keys = blocks(key_base + index * HD)
         values = blocks(value_base + index * HD)
         values = jnp.concatenate([values, jnp.ones_like(values)], axis=1)
+        if copies:
+            copies[index].wait()
         for pair in range(GROUP // 2):
             first = (index * GROUP + 2 * pair) * HD
+            source = query_base + first
             query = jnp.concatenate(
-                [q_ref[:, pl.ds(first, HD)], q_ref[:, pl.ds(first + HD, HD)]], axis=0
+                [q_ref[:, pl.ds(source, HD)], q_ref[:, pl.ds(source + HD, HD)]], axis=0
             )
             scores = lax.dot_general(
                 query, keys, (((1,), (1,)), ((), ())), preferred_element_type=jnp.float32
@@ -104,15 +115,21 @@
             out_ref[:, pl.ds(first + HD, HD)] = result[rows:]
 
 
-def attend(heads, place, weights, queries, kv_slots, key_base, value_base, effort):
-    rows, width = queries.shape
+def attend(heads, place, weights, queries, query_base, kv_slots, key_base, value_base, effort, fetched=False):
+    rows, width = queries.shape[0], len(heads) * GROUP * HD
     keys = weights.shape[1]
     return pl.pallas_call(
-        functools.partial(attend_kernel, heads, key_base, value_base),
+        functools.partial(attend_kernel, heads, query_base, key_base, value_base, len(kv_slots)),
         out_shape=jax.ShapeDtypeStruct((rows, width), jnp.bfloat16),
-        in_specs=[SMEM] + [VMEM] * (2 + len(kv_slots)),
+        in_specs=[SMEM, VMEM, ANY if fetched else VMEM] + [VMEM] * len(kv_slots),
         out_specs=VMEM,
-        compiler_params=pltpu.CompilerParams(vmem_limit_bytes=16 << 20),
+        scratch_shapes=[
+            pltpu.VMEM((rows, width), jnp.bfloat16),
+            pltpu.SemaphoreType.DMA((len(heads),)),
+        ]
+        if fetched
+        else [],
+        compiler_params=pltpu.CompilerParams(vmem_limit_bytes=(16 if fetched else 16) << 20),
         cost_estimate=pl.CostEstimate(
             flops=effort * rows * width * keys,
             bytes_accessed=4 * rows * width + 4 * keys * len(heads) * HD,
@@ -182,27 +199,6 @@
     )(is_last, cotangent, *arrived, *handed)
 
 
-def split_kernel(queries_ref, *out_refs):
-    done = 0
-    for out_ref in out_refs:
-        out_ref[...] = queries_ref[:, pl.ds(done, out_ref.shape[1])]
-        done += out_ref.shape[1]
-
-
-def split(queries):
-    rows = queries.shape[0]
-    return pl.pallas_call(
-        split_kernel,
-        out_shape=[
-            jax.ShapeDtypeStruct((rows, len(heads) * GROUP * HD), jnp.bfloat16) for heads in GROUPS
-        ],
-        in_specs=[VMEM],
-        out_specs=[VMEM] * PARTS,
-        compiler_params=pltpu.CompilerParams(vmem_limit_bytes=16 << 20),
-        name="split",
-    )(queries)
-
-
 def swapped_sum(value, axis, distances):
     count = lax.axis_size(axis)
     for distance in distances:
@@ -265,22 +261,25 @@
             jnp.concatenate([keys_values[:, first:last], keys_values[:, half + first : half + last]], axis=1)
         )
     early_kv = lax.ppermute(kv_parts[0], "section", first_hop)
+    part_queries = queries[:, : EARLY * GROUP * HD]
+    early_queries = lax.ppermute(part_queries, "section", first_hop)
     late_slots = gather_slots(kv_parts[1])
-    queries = list(split(queries))
-    early_queries = lax.ppermute(queries[0], "section", first_hop)
     both = jnp.concatenate([kv_parts[0], early_kv], axis=1)
     late_slots[1], early_kv = lax.optimization_barrier((late_slots[1], early_kv))
-    late = attend(late_heads, place, weights, queries[1], late_slots, 0, half - early_width, 120)
+    late_columns = EARLY * GROUP * HD
+    late = attend(
+        late_heads, place, weights, queries, late_columns, late_slots, 0, half - early_width, 120, True
+    )
     arrived_late = lax.ppermute(late, "section", first_hop)
     if lax.axis_size("ctx") == 4:
-        first, third = fetch(both, 1), fetch(both, 3)
-        third, early_queries = lax.optimization_barrier((third, early_queries))
+        first, third = fetch(both, 1), lax.ppermute(both, "ctx", [(1, 2), (2, 1)])
+        first, early_queries = lax.optimization_barrier((first, early_queries))
         both_slots = [both, first, fetch(first, 3), third, fetch(third, 1)]
     else:
         both_slots = gather_slots(both)
-    own = attend(early_heads, place, weights, queries[0], both_slots, 0, early_width, 1)
+    own = attend(early_heads, place, weights, part_queries, 0, both_slots, 0, early_width, 1)
     early = attend(
-        early_heads, place, weights, early_queries, both_slots, 2 * early_width, 3 * early_width, 1
+        early_heads, place, weights, early_queries, 0, both_slots, 2 * early_width, 3 * early_width, 1
     )
     arrived = [early, arrived_late]
     handed = [own, late]

time: 49 us -> 48.3 us (0.986)
  waiting for transfers between devices: 19.1 us -> 15.6 us
  starting transfers between devices: 17.7 us -> 19.7 us
    ppermute x1 -> x2, waiting for transfers between devices: 3.27 us -> 0.01 us  [the longest x1 0.01 us: per_device(): first, third = (fetch(both, 1), lax.ppermute(both, 'ctx', [(1, 2), (2, 1)]))]
    ppermute x7 -> x6, waiting for transfers between devices: 11.4 us -> 9.61 us  [fetch(): return lax.ppermute(value, ('dp', 'ctx'), pairs)]
    ppermute x1, waiting for transfers between devices: 0.2 us -> 1.67 us  [per_device(): arrived_late = lax.ppermute(late, 'section', first_hop)]
    ppermute x7 -> x6, starting transfers between devices: 7.55 us -> 8.75 us  [fetch(): return lax.ppermute(value, ('dp', 'ctx'), pairs)]
    ppermute x1 -> x2, starting transfers between devices: 0.53 us -> 1.27 us  [the longest x1 0.67 us: per_device(): first, third = (fetch(both, 1), lax.ppermute(both, 'ctx', [(1, 2), (2, 1)]))]
    unnamed x14 -> x12, local copies, waits for them, and re-layouts: 1.47 us -> 1.91 us
    pallas_call x4 -> x3, Pallas kernels: 4.9 us -> 5.27 us  [attend(): pl.pallas_call(functools.partial(attend_kernel, heads, query_base, key_ba...]
  transfers between devices with their start and end apart: 16 -> 16, of which waited for: 9 -> 7; matrix products, arithmetic and copies ran while one was open for 0% -> 0% of each run, Pallas kernels for 12% -> 13%
where the time goes in v5:
time: 48.3 us; the launch traced here: 48 us
  starting transfers between devices  19.7 us (41%)
  waiting for transfers between devices  15.6 us (32%)
  Pallas kernels  8.35 us (17%)
  local copies, waits for them, and re-layouts  2.99 us (6%)
  between operations  0.77 us (2%)
  other arithmetic  0.66 us (1%)
    ppermute x6, waiting for transfers between devices, fetch(): return lax.ppermute(value, ('dp', 'ctx'), pairs)  9.61 us
    ppermute x6, starting transfers between devices, fetch(): return lax.ppermute(value, ('dp', 'ctx'), pairs)  8.75 us
    ppermute x4, starting transfers between devices, total_share(): heard.append(lax.ppermute(value, ('dp', 'ctx'), pairs))  5.91 us
    pallas_call x3, Pallas kernels, attend(): pl.pallas_call(functools.partial(attend_kernel, heads, query_base, key_ba...  5.27 us
    ppermute x1, starting transfers between devices, per_device(): early_kv = lax.ppermute(kv_parts[0], 'section', first_hop)  3 us
    ppermute x2, waiting for transfers between devices, swapped_sum(): lax.ppermute(value, axis, [(place, place ^ distance) for place in range(c...  2.34 us
    pallas_call x1, Pallas kernels, finish(): pl.pallas_call(functools.partial(finish_kernel, scale), out_shape=(jax.Sh...  2.28 us
    ppermute x4, waiting for transfers between devices, total_share(): heard.append(lax.ppermute(value, ('dp', 'ctx'), pairs))  1.95 us
  transfers between devices with their start and end apart: 16, of which 7 were waited for; matrix products, arithmetic and copies ran while one was open for 0% of the time, Pallas kernels for 13%

profile of v5, /device:TPU:0, one launch (start us, length us, event | category | flops | bytes accessed | tf_op | source)
XLA Modules:
  0.0 48.0 jit_solution(2419077960197334693)
XLA Ops:
  0.6 1.0 %fusion = (bf16[128,256]{1,0:T(8,128)(2,1)S(1)}, bf16[128,256]{1,0:T(8,128)(2,1)S(1)}, bf16[128,256]{1,0:T(8,128)(2,1)S(1)}, bf16[128,256]{1,0:T(8,128)(2,1)S(1)}) fusion(bf16[128,1024]{1,0:T(8,128)(2,1)} %bitcast.10), kind=kLoop, calls=%fused_computation.4 | loop fusion | bytes 524288 | tf_op jit(solution)/shard_map/slice | solution.py:261
  1.7 3.0 %collective-permute-start = (bf16[128,512]{1,0:T(8,128)(2,1)S(1)}, bf16[128,512]{1,0:T(8,128)(2,1)S(1)}, u32[]{:S(2)}, u32[]{:S(2)}) collective-permute-start(bf16[128,512]{1,0:T(8,128)(2,1)S(1)} %pad_maximum_fusion.1), channel_id=1, source_target_pairs={{0,4},{4,0},{1,5},{5,1},{2,6},{6,2},{3,7},{7,3},{8,12},{12,8},{9,1... | collective-permute-start | bytes 393224 | tf_op jit(solution)/shard_map/ppermute | solution.py:263
  4.7 1.6 %collective-permute-start.6 = (bf16[128,512]{1,0:T(8,128)(2,1)S(1)}, bf16[128,512]{1,0:T(8,128)(2,1)S(1)}, u32[]{:S(2)}, u32[]{:S(2)}) collective-permute-start(bf16[128,512]{1,0:T(8,128)(2,1)S(1)} %pad_maximum_fusion.2.refs_0_), channel_id=1, source_target_pairs={{0,1},{1,0},{2,3},{3,2},{8,9},{9,8},{10,11},{11,10},{16,17},{17,16... | collective-permute-start | bytes 393224 | tf_op jit(solution)/shard_map/ppermute | solution.py:239
  6.4 2.6 %collective-permute-start.7 = (bf16[128,512]{1,0:T(8,128)(2,1)S(1)}, bf16[128,512]{1,0:T(8,128)(2,1)S(1)}, u32[]{:S(2)}, u32[]{:S(2)}) collective-permute-start(bf16[128,512]{1,0:T(8,128)(2,1)S(1)} %pad_maximum_fusion.2.refs_0_), channel_id=1, source_target_pairs={{0,2},{1,3},{2,0},{3,1},{8,10},{9,11},{10,8},{11,9},{16,18},{17,19... | collective-permute-start | bytes 393224 | tf_op jit(solution)/shard_map/ppermute | solution.py:239
  10.3 0.8 %weigh.1.weights_ref = f32[136,512]{1,0:T(8,128)S(1)} custom-call(s32[1]{0:T(128)} %bitcast.2.place_ref, s32[1,4,4,4]{3,2,1,0:T(4,128)S(1)} %copy-done.3, s32[1,2]{1,0:T(1,128)S(1)} %copy-done.4, s32[1,4]{1,0:T(1,128)S(1)} %copy-done.5), custom_call_target="tpu_custom_call" | custom-call | tf_op jit(solution)/shard_map/weigh/pallas_call | solution.py:61
  11.1 1.0 %collective-permute-start.1 = (bf16[128,1024]{1,0:T(8,128)(2,1)S(1)}, bf16[128,1024]{1,0:T(8,128)(2,1)S(1)}, u32[]{:S(2)}, u32[]{:S(2)}) collective-permute-start(bf16[128,1024]{1,0:T(8,128)(2,1)S(1)} %pad_maximum_fusion.refs_0_), channel_id=1, source_target_pairs={{0,1},{1,0},{2,3},{3,2},{8,9},{9,8},{10,11},{11,10},{16,17},{17,16... | collective-permute-start | bytes 786440 | tf_op jit(solution)/shard_map/ppermute | solution.py:239
  12.1 0.7 %collective-permute-start.4 = (bf16[128,1024]{1,0:T(8,128)(2,1)S(1)}, bf16[128,1024]{1,0:T(8,128)(2,1)S(1)}, u32[]{:S(2)}, u32[]{:S(2)}) collective-permute-start(bf16[128,1024]{1,0:T(8,128)(2,1)S(1)} %pad_maximum_fusion.refs_0_), channel_id=1, source_target_pairs={{1,2},{2,1},{5,6},{6,5},{9,10},{10,9},{13,14},{14,13},{17,18},{18,... | collective-permute-start | bytes 786440 | tf_op jit(solution)/shard_map/ppermute | solution.py:275
  12.8 3.5 %collective-permute-done.7.refs_2_ = bf16[128,512]{1,0:T(8,128)(2,1)S(1)} collective-permute-done((bf16[128,512]{1,0:T(8,128)(2,1)S(1)}, bf16[128,512]{1,0:T(8,128)(2,1)S(1)}, u32[]{:S(2)}, u32[]{:S(2)}) %collective-permute-start.7) | collective-permute-done | bytes 131104 | tf_op jit(solution)/shard_map/ppermute | solution.py:239
  16.3 1.2 %copy-done.2 = bf16[1,1,128,4096]{3,2,1,0:T(8,128)(2,1)S(1)} copy-done((bf16[1,1,128,4096]{3,2,1,0:T(8,128)(2,1)S(1)}, bf16[1,1,128,4096]{3,2,1,0:T(8,128)(2,1)}, u32[]{:S(2)}) %copy-start.2) | copy-done | bytes 1048600
  17.5 2.1 %attend.4.refs_3_ = bf16[128,2048]{1,0:T(8,128)(2,1)S(1)} custom-call(s32[1]{0:T(128)} %bitcast.2.place_ref, f32[136,512]{1,0:T(8,128)S(1)} %weigh.1.weights_ref, bf16[128,4096]{1,0:T(8,128)(2,1)S(1)} %bitcast.9, bf16[128,512]{1,0:T(8,128)(2,1)S(1)} %pad_maximum_fusion.2.refs_0_, bf16[128,512]{1,0:T(8,128)(2,1)S(1)} %collective-permute-done.6.refs_1_, ...), custom_call_target="tpu_custom_call" | custom-call | flops 16106127360 | bytes 1572864 | tf_op jit(solution)/shard_map/attend/pallas_call | solution.py:121
  19.6 0.6 %collective-permute-start.9 = (bf16[128,2048]{1,0:T(8,128)(2,1)S(1)}, bf16[128,2048]{1,0:T(8,128)(2,1)}, u32[]{:S(2)}, u32[]{:S(2)}) collective-permute-start(bf16[128,2048]{1,0:T(8,128)(2,1)S(1)} %attend.4.refs_3_), channel_id=1, source_target_pairs={{0,4},{4,0},{1,5},{5,1},{2,6},{6,2},{3,7},{7,3},{8,12},{12,8},{9,1... | collective-permute-start | bytes 1572872 | tf_op jit(solution)/shard_map/ppermute | solution.py:273
  20.2 3.5 %collective-permute-start.5 = (bf16[128,1024]{1,0:T(8,128)(2,1)S(1)}, bf16[128,1024]{1,0:T(8,128)(2,1)S(1)}, u32[]{:S(2)}, u32[]{:S(2)}) collective-permute-start(bf16[128,1024]{1,0:T(8,128)(2,1)S(1)} %collective-permute-done.4.refs_3_), channel_id=1, source_target_pairs={{0,1},{1,0},{2,3},{3,2},{8,9},{9,8},{10,11},{11,10},{16,17},{17,16... | collective-permute-start | bytes 786440 | tf_op jit(solution)/shard_map/ppermute | solution.py:239
  23.8 6.1 %collective-permute-done.5.refs_4_ = bf16[128,1024]{1,0:T(8,128)(2,1)S(1)} collective-permute-done((bf16[128,1024]{1,0:T(8,128)(2,1)S(1)}, bf16[128,1024]{1,0:T(8,128)(2,1)S(1)}, u32[]{:S(2)}, u32[]{:S(2)}) %collective-permute-start.5) | collective-permute-done | bytes 262176 | tf_op jit(solution)/shard_map/ppermute | solution.py:239
  29.9 1.6 %attend.5.refs_2_ = bf16[128,2048]{1,0:T(8,128)(2,1)S(1)} custom-call(s32[1]{0:T(128)} %bitcast.2.place_ref, f32[136,512]{1,0:T(8,128)S(1)} %weigh.1.weights_ref, bf16[128,2048]{1,0:T(8,128)(2,1)S(1)} %slice.22.q_ref, bf16[128,1024]{1,0:T(8,128)(2,1)S(1)} %pad_maximum_fusion.refs_0_, bf16[128,1024]{1,0:T(8,128)(2,1)S(1)} %collective-permute-done.1.refs_1_, ...), custom_call_target="tpu_custom_call" | custom-call | flops 134217728 | bytes 1572864 | tf_op jit(solution)/shard_map/attend/pallas_call | solution.py:121
  31.5 1.6 %attend.3.refs_0_ = bf16[128,2048]{1,0:T(8,128)(2,1)S(1)} custom-call(s32[1]{0:T(128)} %bitcast.2.place_ref, f32[136,512]{1,0:T(8,128)S(1)} %weigh.1.weights_ref, bf16[128,2048]{1,0:T(8,128)(2,1)S(1)} %collective-permute-done.2.q_ref, bf16[128,1024]{1,0:T(8,128)(2,1)S(1)} %pad_maximum_fusion.refs_0_, bf16[128,1024]{1,0:T(8,128)(2,1)S(1)} %collective-permute-done.1.refs_1_, ...), custom_call_target="tpu_custom_call" | custom-call | flops 134217728 | bytes 1572864 | tf_op jit(solution)/shard_map/attend/pallas_call | solution.py:121
  33.1 1.7 %collective-permute-done.9.refs_1_ = bf16[128,2048]{1,0:T(8,128)(2,1)} collective-permute-done((bf16[128,2048]{1,0:T(8,128)(2,1)S(1)}, bf16[128,2048]{1,0:T(8,128)(2,1)}, u32[]{:S(2)}, u32[]{:S(2)}) %collective-permute-start.9) | collective-permute-done | bytes 524320 | tf_op jit(solution)/shard_map/ppermute | solution.py:273
  34.7 2.3 %finish.1 = (bf16[128,4096]{1,0:T(8,128)(2,1)}, f32[32,128]{1,0:T(8,128)S(1)}) custom-call(s32[1]{0:T(128)} %bitcast.last_ref, bf16[128,4096]{1,0:T(8,128)(2,1)S(1)} %bitcast.7, bf16[128,2048]{1,0:T(8,128)(2,1)S(1)} %attend.3.refs_0_, bf16[128,2048]{1,0:T(8,128)(2,1)} %collective-permute-done.9.refs_1_, bf16[128,2048]{1,0:T(8,128)(2,1)S(1)} %attend.5.refs_2_, ...), custom_call_target="tpu_custom_call" | custom-call | flops 5242880 | bytes 4194304 | tf_op jit(solution)/shard_map/finish/pallas_call | solution.py:180
  37.1 1.2 %collective-permute-done.10 = f32[32,128]{1,0:T(8,128)S(1)} collective-permute-done((f32[32,128]{1,0:T(8,128)S(1)}, f32[32,128]{1,0:T(8,128)S(1)}, u32[]{:S(2)}, u32[]{:S(2)}) %collective-permute-start.10) | collective-permute-done | bytes 16416 | tf_op jit(solution)/shard_map/ppermute | solution.py:205
  38.3 1.5 %collective-permute-start.11 = (f32[32,128]{1,0:T(8,128)S(1)}, f32[32,128]{1,0:T(8,128)S(1)}, u32[]{:S(2)}, u32[]{:S(2)}) collective-permute-start(f32[32,128]{1,0:T(8,128)S(1)} %add.23), channel_id=1, source_target_pairs={{0,16},{1,17},{2,18},{3,19},{8,24},{9,25},{10,26},{11,27},{16,0},{... | collective-permute-start | bytes 49160 | tf_op jit(solution)/shard_map/ppermute | solution.py:226
  40.0 0.6 %collective-permute-start.13 = (f32[32,128]{1,0:T(8,128)S(1)}, f32[32,128]{1,0:T(8,128)S(1)}, u32[]{:S(2)}, u32[]{:S(2)}) collective-permute-start(f32[32,128]{1,0:T(8,128)S(1)} %add.23), channel_id=1, source_target_pairs={{0,2},{1,3},{2,0},{3,1},{8,26},{9,27},{10,24},{11,25},{16,18},{17,... | collective-permute-start | bytes 49160 | tf_op jit(solution)/shard_map/ppermute | solution.py:226
  40.6 3.6 %collective-permute-start.14 = (f32[32,128]{1,0:T(8,128)S(1)}, f32[32,128]{1,0:T(8,128)S(1)}, u32[]{:S(2)}, u32[]{:S(2)}) collective-permute-start(f32[32,128]{1,0:T(8,128)S(1)} %add.23), channel_id=1, source_target_pairs={{0,3},{1,2},{2,1},{3,0},{8,27},{9,26},{10,25},{11,24},{16,19},{17,... | collective-permute-start | bytes 49160 | tf_op jit(solution)/shard_map/ppermute | solution.py:226
  44.7 1.4 %collective-permute-done.14 = f32[32,128]{1,0:T(8,128)S(1)} collective-permute-done((f32[32,128]{1,0:T(8,128)S(1)}, f32[32,128]{1,0:T(8,128)S(1)}, u32[]{:S(2)}, u32[]{:S(2)}) %collective-permute-start.14) | collective-permute-done | bytes 16416 | tf_op jit(solution)/shard_map/ppermute | solution.py:226
  46.2 1.2 %collective-permute-done.15 = f32[32,128]{1,0:T(8,128)S(1)} collective-permute-done((f32[32,128]{1,0:T(8,128)S(1)}, f32[32,128]{1,0:T(8,128)S(1)}, u32[]{:S(2)}, u32[]{:S(2)}) %collective-permute-start.15) | collective-permute-done | bytes 16416 | tf_op jit(solution)/shard_map/ppermute | solution.py:205
  47.4 0.6 %add.28 = f32[32,128]{1,0:T(8,128)} add(f32[32,128]{1,0:T(8,128)S(1)} %add_add_fusion, f32[32,128]{1,0:T(8,128)S(1)} %collective-permute-done.15) | non-fusion elementwise | flops 4096 | bytes 49152 | tf_op jit(solution)/shard_map/add | solution.py:205
  (33 shorter events, 2.2 us)
Async XLA Ops:
  0.6 8.3 %copy-start.1 = (bf16[1,1,128,4096]{3,2,1,0:T(8,128)(2,1)S(1)}, bf16[1,1,128,4096]{3,2,1,0:T(8,128)(2,1)}, u32[]{:S(2)}) copy-start(bf16[1,1,128,4096]{3,2,1,0:T(8,128)(2,1)} %param.6) | copy-start | bytes 3145732
  1.7 9.4 %collective-permute-start = (bf16[128,512]{1,0:T(8,128)(2,1)S(1)}, bf16[128,512]{1,0:T(8,128)(2,1)S(1)}, u32[]{:S(2)}, u32[]{:S(2)}) collective-permute-start(bf16[128,512]{1,0:T(8,128)(2,1)S(1)} %pad_maximum_fusion.1), channel_id=1, source_target_pairs={{0,4},{4,0},{1,5},{5,1},{2,6},{6,2},{3,7},{7,3},{8,12},{12,8},{9,1... | collective-permute-start | bytes 393224 | tf_op jit(solution)/shard_map/ppermute | solution.py:263
  4.7 7.4 %collective-permute-start.6 = (bf16[128,512]{1,0:T(8,128)(2,1)S(1)}, bf16[128,512]{1,0:T(8,128)(2,1)S(1)}, u32[]{:S(2)}, u32[]{:S(2)}) collective-permute-start(bf16[128,512]{1,0:T(8,128)(2,1)S(1)} %pad_maximum_fusion.2.refs_0_), channel_id=1, source_target_pairs={{0,1},{1,0},{2,3},{3,2},{8,9},{9,8},{10,11},{11,10},{16,17},{17,16... | collective-permute-start | bytes 393224 | tf_op jit(solution)/shard_map/ppermute | solution.py:239
  6.4 9.9 %collective-permute-start.7 = (bf16[128,512]{1,0:T(8,128)(2,1)S(1)}, bf16[128,512]{1,0:T(8,128)(2,1)S(1)}, u32[]{:S(2)}, u32[]{:S(2)}) collective-permute-start(bf16[128,512]{1,0:T(8,128)(2,1)S(1)} %pad_maximum_fusion.2.refs_0_), channel_id=1, source_target_pairs={{0,2},{1,3},{2,0},{3,1},{8,10},{9,11},{10,8},{11,9},{16,18},{17,19... | collective-permute-start | bytes 393224 | tf_op jit(solution)/shard_map/ppermute | solution.py:239
  9.0 7.3 %collective-permute-start.8 = (bf16[128,512]{1,0:T(8,128)(2,1)S(1)}, bf16[128,512]{1,0:T(8,128)(2,1)S(1)}, u32[]{:S(2)}, u32[]{:S(2)}) collective-permute-start(bf16[128,512]{1,0:T(8,128)(2,1)S(1)} %pad_maximum_fusion.2.refs_0_), channel_id=1, source_target_pairs={{0,8},{1,2},{2,1},{3,11},{8,0},{9,10},{10,9},{11,3},{16,24},{17,18... | collective-permute-start | bytes 393224 | tf_op jit(solution)/shard_map/ppermute | solution.py:239
  9.0 0.7 %copy-start.3 = (s32[1,4,4,4]{3,2,1,0:T(4,128)S(1)}, s32[1,4,4,4]{3,2,1,0:T(4,128)}, u32[]{:S(2)}) copy-start(s32[1,4,4,4]{3,2,1,0:T(4,128)} %lists_ref.1) | copy-start | bytes 772
  9.0 14.8 %collective-permute-start.2 = (bf16[128,2048]{1,0:T(8,128)(2,1)S(1)}, bf16[128,2048]{1,0:T(8,128)(2,1)S(1)}, u32[]{:S(2)}, u32[]{:S(2)}) collective-permute-start(bf16[128,2048]{1,0:T(8,128)(2,1)S(1)} %slice.22.q_ref), channel_id=1, source_target_pairs={{0,4},{4,0},{1,5},{5,1},{2,6},{6,2},{3,7},{7,3},{8,12},{12,8},{9,1... | collective-permute-start | bytes 1572872 | tf_op jit(solution)/shard_map/ppermute | solution.py:265
  9.6 0.7 %copy-start.4 = (s32[1,2]{1,0:T(1,128)S(1)}, s32[1,2]{1,0:T(1,128)}, u32[]{:S(2)}) copy-start(s32[1,2]{1,0:T(1,128)} %globals_ref.1) | copy-start | bytes 28
  9.6 0.7 %copy-start.5 = (s32[1,4]{1,0:T(1,128)S(1)}, s32[1,4]{1,0:T(1,128)}, u32[]{:S(2)}) copy-start(s32[1,4]{1,0:T(1,128)} %docs_ref.1) | copy-start | bytes 52
  11.1 12.7 %collective-permute-start.1 = (bf16[128,1024]{1,0:T(8,128)(2,1)S(1)}, bf16[128,1024]{1,0:T(8,128)(2,1)S(1)}, u32[]{:S(2)}, u32[]{:S(2)}) collective-permute-start(bf16[128,1024]{1,0:T(8,128)(2,1)S(1)} %pad_maximum_fusion.refs_0_), channel_id=1, source_target_pairs={{0,1},{1,0},{2,3},{3,2},{8,9},{9,8},{10,11},{11,10},{16,17},{17,16... | collective-permute-start | bytes 786440 | tf_op jit(solution)/shard_map/ppermute | solution.py:239
  12.1 8.1 %collective-permute-start.4 = (bf16[128,1024]{1,0:T(8,128)(2,1)S(1)}, bf16[128,1024]{1,0:T(8,128)(2,1)S(1)}, u32[]{:S(2)}, u32[]{:S(2)}) collective-permute-start(bf16[128,1024]{1,0:T(8,128)(2,1)S(1)} %pad_maximum_fusion.refs_0_), channel_id=1, source_target_pairs={{1,2},{2,1},{5,6},{6,5},{9,10},{10,9},{13,14},{14,13},{17,18},{18,... | collective-permute-start | bytes 786440 | tf_op jit(solution)/shard_map/ppermute | solution.py:275
  16.3 1.2 %copy-start.2 = (bf16[1,1,128,4096]{3,2,1,0:T(8,128)(2,1)S(1)}, bf16[1,1,128,4096]{3,2,1,0:T(8,128)(2,1)}, u32[]{:S(2)}) copy-start(bf16[1,1,128,4096]{3,2,1,0:T(8,128)(2,1)} %param.6) | copy-start | bytes 3145732
  19.6 15.1 %collective-permute-start.9 = (bf16[128,2048]{1,0:T(8,128)(2,1)S(1)}, bf16[128,2048]{1,0:T(8,128)(2,1)}, u32[]{:S(2)}, u32[]{:S(2)}) collective-permute-start(bf16[128,2048]{1,0:T(8,128)(2,1)S(1)} %attend.4.refs_3_), channel_id=1, source_target_pairs={{0,4},{4,0},{1,5},{5,1},{2,6},{6,2},{3,7},{7,3},{8,12},{12,8},{9,1... | collective-permute-start | bytes 1572872 | tf_op jit(solution)/shard_map/ppermute | solution.py:273
  20.2 9.6 %collective-permute-start.5 = (bf16[128,1024]{1,0:T(8,128)(2,1)S(1)}, bf16[128,1024]{1,0:T(8,128)(2,1)S(1)}, u32[]{:S(2)}, u32[]{:S(2)}) collective-permute-start(bf16[128,1024]{1,0:T(8,128)(2,1)S(1)} %collective-permute-done.4.refs_3_), channel_id=1, source_target_pairs={{0,1},{1,0},{2,3},{3,2},{8,9},{9,8},{10,11},{11,10},{16,17},{17,16... | collective-permute-start | bytes 786440 | tf_op jit(solution)/shard_map/ppermute | solution.py:239
  23.8 6.1 %collective-permute-start.3 = (bf16[128,1024]{1,0:T(8,128)(2,1)S(1)}, bf16[128,1024]{1,0:T(8,128)(2,1)S(1)}, u32[]{:S(2)}, u32[]{:S(2)}) collective-permute-start(bf16[128,1024]{1,0:T(8,128)(2,1)S(1)} %collective-permute-done.1.refs_1_), channel_id=1, source_target_pairs={{0,8},{1,2},{2,1},{3,11},{8,0},{9,10},{10,9},{11,3},{16,24},{17,18... | collective-permute-start | bytes 786440 | tf_op jit(solution)/shard_map/ppermute | solution.py:239
  31.5 3.3 %copy-start = (bf16[1,1,128,4096]{3,2,1,0:T(8,128)(2,1)S(1)}, bf16[1,1,128,4096]{3,2,1,0:T(8,128)(2,1)}, u32[]{:S(2)}) copy-start(bf16[1,1,128,4096]{3,2,1,0:T(8,128)(2,1)} %param.11) | copy-start | bytes 3145732
  37.0 1.2 %collective-permute-start.10 = (f32[32,128]{1,0:T(8,128)S(1)}, f32[32,128]{1,0:T(8,128)S(1)}, u32[]{:S(2)}, u32[]{:S(2)}) collective-permute-start(f32[32,128]{1,0:T(8,128)S(1)} %get-tuple-element.11), channel_id=1, source_target_pairs={{0,8},{8,0},{16,24},{24,16},{1,9},{9,1},{17,25},{25,17},{2,10},{10... | collective-permute-start | bytes 49160 | tf_op jit(solution)/shard_map/ppermute | solution.py:205
  38.3 5.9 %collective-permute-start.11 = (f32[32,128]{1,0:T(8,128)S(1)}, f32[32,128]{1,0:T(8,128)S(1)}, u32[]{:S(2)}, u32[]{:S(2)}) collective-permute-start(f32[32,128]{1,0:T(8,128)S(1)} %add.23), channel_id=1, source_target_pairs={{0,16},{1,17},{2,18},{3,19},{8,24},{9,25},{10,26},{11,27},{16,0},{... | collective-permute-start | bytes 49160 | tf_op jit(solution)/shard_map/ppermute | solution.py:226
  39.8 4.4 %collective-permute-start.12 = (f32[32,128]{1,0:T(8,128)S(1)}, f32[32,128]{1,0:T(8,128)S(1)}, u32[]{:S(2)}, u32[]{:S(2)}) collective-permute-start(f32[32,128]{1,0:T(8,128)S(1)} %add.23), channel_id=1, source_target_pairs={{0,1},{1,0},{2,3},{3,2},{8,25},{9,24},{10,27},{11,26},{16,17},{17,... | collective-permute-start | bytes 49160 | tf_op jit(solution)/shard_map/ppermute | solution.py:226
  40.0 4.7 %collective-permute-start.13 = (f32[32,128]{1,0:T(8,128)S(1)}, f32[32,128]{1,0:T(8,128)S(1)}, u32[]{:S(2)}, u32[]{:S(2)}) collective-permute-start(f32[32,128]{1,0:T(8,128)S(1)} %add.23), channel_id=1, source_target_pairs={{0,2},{1,3},{2,0},{3,1},{8,26},{9,27},{10,24},{11,25},{16,18},{17,... | collective-permute-start | bytes 49160 | tf_op jit(solution)/shard_map/ppermute | solution.py:226
  40.6 5.6 %collective-permute-start.14 = (f32[32,128]{1,0:T(8,128)S(1)}, f32[32,128]{1,0:T(8,128)S(1)}, u32[]{:S(2)}, u32[]{:S(2)}) collective-permute-start(f32[32,128]{1,0:T(8,128)S(1)} %add.23), channel_id=1, source_target_pairs={{0,3},{1,2},{2,1},{3,0},{8,27},{9,26},{10,25},{11,24},{16,19},{17,... | collective-permute-start | bytes 49160 | tf_op jit(solution)/shard_map/ppermute | solution.py:226
  46.2 1.2 %collective-permute-start.15 = (f32[32,128]{1,0:T(8,128)S(1)}, f32[32,128]{1,0:T(8,128)S(1)}, u32[]{:S(2)}, u32[]{:S(2)}) collective-permute-start(f32[32,128]{1,0:T(8,128)S(1)} %add_add_fusion), channel_id=1, source_target_pairs={{0,8},{8,0},{16,24},{24,16},{1,9},{9,1},{17,25},{25,17},{2,10},{10... | collective-permute-start | bytes 49160 | tf_op jit(solution)/shard_map/ppermute | solution.py:205

commit v6 on v5

--- a/solution.py
+++ b/solution.py
@@ -240,7 +240,8 @@
 
 
 def gather_slots(value):
-    return [value] + [fetch(value, slot) for slot in range(1, lax.axis_size("ctx"))]
+    slots = [fetch(value, slot) for slot in range(lax.axis_size("ctx") - 1, 0, -1)]
+    return [value] + slots[::-1]
 
 
 def per_device(queries, keys_values, random_blocks, global_blocks, doc_lengths, cotangent):
@@ -265,7 +266,7 @@
     early_queries = lax.ppermute(part_queries, "section", first_hop)
     late_slots = gather_slots(kv_parts[1])
     both = jnp.concatenate([kv_parts[0], early_kv], axis=1)
-    late_slots[1], early_kv = lax.optimization_barrier((late_slots[1], early_kv))
+    late_slots[-1], early_kv = lax.optimization_barrier((late_slots[-1], early_kv))
     late_columns = EARLY * GROUP * HD
     late = attend(
         late_heads, place, weights, queries, late_columns, late_slots, 0, half - early_width, 120, True

time: 48.3 us -> 48 us (level)
  starting transfers between devices: 19.7 us -> 18.6 us
  waiting for transfers between devices: 15.6 us -> 16.4 us
    ppermute x6, waiting for transfers between devices: 9.61 us -> 7.18 us  [fetch(): return lax.ppermute(value, ('dp', 'ctx'), pairs)]
    ppermute x1, waiting for transfers between devices: 1.67 us -> 3.4 us  [per_device(): arrived_late = lax.ppermute(late, 'section', first_hop)]
    ppermute x6, starting transfers between devices: 8.75 us -> 7.48 us  [fetch(): return lax.ppermute(value, ('dp', 'ctx'), pairs)]
    ppermute x1, waiting for transfers between devices: 0.01 us -> 1.23 us  [per_device(): early_queries = lax.ppermute(part_queries, 'section', first_hop)]
  transfers between devices with their start and end apart: 16 -> 16, of which waited for: 7 -> 8; matrix products, arithmetic and copies ran while one was open for 0% -> 0% of each run, Pallas kernels for 13% -> 13%
where the time goes in v6:
time: 48 us; the launch traced here: 47.7 us
  starting transfers between devices  18.6 us (39%)
  waiting for transfers between devices  16.4 us (34%)
  Pallas kernels  8.36 us (17%)
  local copies, waits for them, and re-layouts  2.99 us (6%)
  between operations  0.78 us (2%)
  other arithmetic  0.66 us (1%)
    ppermute x6, starting transfers between devices, fetch(): return lax.ppermute(value, ('dp', 'ctx'), pairs)  7.48 us
    ppermute x6, waiting for transfers between devices, fetch(): return lax.ppermute(value, ('dp', 'ctx'), pairs)  7.18 us
    ppermute x4, starting transfers between devices, total_share(): heard.append(lax.ppermute(value, ('dp', 'ctx'), pairs))  5.91 us
    pallas_call x3, Pallas kernels, attend(): pl.pallas_call(functools.partial(attend_kernel, heads, query_base, key_ba...  5.27 us
    ppermute x1, waiting for transfers between devices, per_device(): arrived_late = lax.ppermute(late, 'section', first_hop)  3.4 us
    ppermute x1, starting transfers between devices, per_device(): early_kv = lax.ppermute(kv_parts[0], 'section', first_hop)  3 us
    ppermute x2, waiting for transfers between devices, swapped_sum(): lax.ppermute(value, axis, [(place, place ^ distance) for place in range(c...  2.34 us
    pallas_call x1, Pallas kernels, finish(): pl.pallas_call(functools.partial(finish_kernel, scale), out_shape=(jax.Sh...  2.28 us
  transfers between devices with their start and end apart: 16, of which 8 were waited for; matrix products, arithmetic and copies ran while one was open for 0% of the time, Pallas kernels for 13%

profile of v6, /device:TPU:0, one launch (start us, length us, event | category | flops | bytes accessed | tf_op | source)
XLA Modules:
  0.0 47.7 jit_solution(15914213535980517662)
XLA Ops:
  0.6 1.0 %fusion = (bf16[128,256]{1,0:T(8,128)(2,1)S(1)}, bf16[128,256]{1,0:T(8,128)(2,1)S(1)}, bf16[128,256]{1,0:T(8,128)(2,1)S(1)}, bf16[128,256]{1,0:T(8,128)(2,1)S(1)}) fusion(bf16[128,1024]{1,0:T(8,128)(2,1)} %bitcast.10), kind=kLoop, calls=%fused_computation.4 | loop fusion | bytes 524288 | tf_op jit(solution)/shard_map/slice | solution.py:262
  1.7 3.0 %collective-permute-start = (bf16[128,512]{1,0:T(8,128)(2,1)S(1)}, bf16[128,512]{1,0:T(8,128)(2,1)S(1)}, u32[]{:S(2)}, u32[]{:S(2)}) collective-permute-start(bf16[128,512]{1,0:T(8,128)(2,1)S(1)} %pad_maximum_fusion.1), channel_id=1, source_target_pairs={{0,4},{4,0},{1,5},{5,1},{2,6},{6,2},{3,7},{7,3},{8,12},{12,8},{9,1... | collective-permute-start | bytes 393224 | tf_op jit(solution)/shard_map/ppermute | solution.py:264
  4.8 3.1 %collective-permute-start.6 = (bf16[128,512]{1,0:T(8,128)(2,1)S(1)}, bf16[128,512]{1,0:T(8,128)(2,1)S(1)}, u32[]{:S(2)}, u32[]{:S(2)}) collective-permute-start(bf16[128,512]{1,0:T(8,128)(2,1)S(1)} %pad_maximum_fusion.2.refs_0_), channel_id=1, source_target_pairs={{0,1},{1,0},{2,3},{3,2},{8,9},{9,8},{10,11},{11,10},{16,17},{17,16... | collective-permute-start | bytes 393224 | tf_op jit(solution)/shard_map/ppermute | solution.py:239
  7.9 1.1 %collective-permute-start.7 = (bf16[128,512]{1,0:T(8,128)(2,1)S(1)}, bf16[128,512]{1,0:T(8,128)(2,1)S(1)}, u32[]{:S(2)}, u32[]{:S(2)}) collective-permute-start(bf16[128,512]{1,0:T(8,128)(2,1)S(1)} %pad_maximum_fusion.2.refs_0_), channel_id=1, source_target_pairs={{0,2},{1,3},{2,0},{3,1},{8,10},{9,11},{10,8},{11,9},{16,18},{17,19... | collective-permute-start | bytes 393224 | tf_op jit(solution)/shard_map/ppermute | solution.py:239
  10.4 0.8 %weigh.1.weights_ref = f32[136,512]{1,0:T(8,128)S(1)} custom-call(s32[1]{0:T(128)} %bitcast.2.place_ref, s32[1,4,4,4]{3,2,1,0:T(4,128)S(1)} %copy-done.3, s32[1,2]{1,0:T(1,128)S(1)} %copy-done.4, s32[1,4]{1,0:T(1,128)S(1)} %copy-done.5), custom_call_target="tpu_custom_call" | custom-call | tf_op jit(solution)/shard_map/weigh/pallas_call | solution.py:61
  11.2 0.9 %collective-permute-start.1 = (bf16[128,1024]{1,0:T(8,128)(2,1)S(1)}, bf16[128,1024]{1,0:T(8,128)(2,1)S(1)}, u32[]{:S(2)}, u32[]{:S(2)}) collective-permute-start(bf16[128,1024]{1,0:T(8,128)(2,1)S(1)} %pad_maximum_fusion.refs_0_), channel_id=1, source_target_pairs={{0,1},{1,0},{2,3},{3,2},{8,9},{9,8},{10,11},{11,10},{16,17},{17,16... | collective-permute-start | bytes 786440 | tf_op jit(solution)/shard_map/ppermute | solution.py:239
  12.1 0.7 %collective-permute-start.4 = (bf16[128,1024]{1,0:T(8,128)(2,1)S(1)}, bf16[128,1024]{1,0:T(8,128)(2,1)S(1)}, u32[]{:S(2)}, u32[]{:S(2)}) collective-permute-start(bf16[128,1024]{1,0:T(8,128)(2,1)S(1)} %pad_maximum_fusion.refs_0_), channel_id=1, source_target_pairs={{1,2},{2,1},{5,6},{6,5},{9,10},{10,9},{13,14},{14,13},{17,18},{18,... | collective-permute-start | bytes 786440 | tf_op jit(solution)/shard_map/ppermute | solution.py:276
  12.8 3.5 %collective-permute-done.7.refs_2_ = bf16[128,512]{1,0:T(8,128)(2,1)S(1)} collective-permute-done((bf16[128,512]{1,0:T(8,128)(2,1)S(1)}, bf16[128,512]{1,0:T(8,128)(2,1)S(1)}, u32[]{:S(2)}, u32[]{:S(2)}) %collective-permute-start.7) | collective-permute-done | bytes 131104 | tf_op jit(solution)/shard_map/ppermute | solution.py:239
  16.3 1.2 %copy-done.2 = bf16[1,1,128,4096]{3,2,1,0:T(8,128)(2,1)S(1)} copy-done((bf16[1,1,128,4096]{3,2,1,0:T(8,128)(2,1)S(1)}, bf16[1,1,128,4096]{3,2,1,0:T(8,128)(2,1)}, u32[]{:S(2)}) %copy-start.2) | copy-done | bytes 1048600
  17.5 2.1 %attend.4.refs_3_ = bf16[128,2048]{1,0:T(8,128)(2,1)S(1)} custom-call(s32[1]{0:T(128)} %bitcast.2.place_ref, f32[136,512]{1,0:T(8,128)S(1)} %weigh.1.weights_ref, bf16[128,4096]{1,0:T(8,128)(2,1)S(1)} %bitcast.9, bf16[128,512]{1,0:T(8,128)(2,1)S(1)} %pad_maximum_fusion.2.refs_0_, bf16[128,512]{1,0:T(8,128)(2,1)S(1)} %collective-permute-done.6.refs_1_, ...), custom_call_target="tpu_custom_call" | custom-call | flops 16106127360 | bytes 1572864 | tf_op jit(solution)/shard_map/attend/pallas_call | solution.py:121
  19.6 0.8 %collective-permute-start.9 = (bf16[128,2048]{1,0:T(8,128)(2,1)S(1)}, bf16[128,2048]{1,0:T(8,128)(2,1)}, u32[]{:S(2)}, u32[]{:S(2)}) collective-permute-start(bf16[128,2048]{1,0:T(8,128)(2,1)S(1)} %attend.4.refs_3_), channel_id=1, source_target_pairs={{0,4},{4,0},{1,5},{5,1},{2,6},{6,2},{3,7},{7,3},{8,12},{12,8},{9,1... | collective-permute-start | bytes 1572872 | tf_op jit(solution)/shard_map/ppermute | solution.py:274
  20.4 2.3 %collective-permute-start.5 = (bf16[128,1024]{1,0:T(8,128)(2,1)S(1)}, bf16[128,1024]{1,0:T(8,128)(2,1)S(1)}, u32[]{:S(2)}, u32[]{:S(2)}) collective-permute-start(bf16[128,1024]{1,0:T(8,128)(2,1)S(1)} %collective-permute-done.4.refs_3_), channel_id=1, source_target_pairs={{0,1},{1,0},{2,3},{3,2},{8,9},{9,8},{10,11},{11,10},{16,17},{17,16... | collective-permute-start | bytes 786440 | tf_op jit(solution)/shard_map/ppermute | solution.py:239
  22.7 1.2 %collective-permute-done.2.q_ref = bf16[128,2048]{1,0:T(8,128)(2,1)S(1)} collective-permute-done((bf16[128,2048]{1,0:T(8,128)(2,1)S(1)}, bf16[128,2048]{1,0:T(8,128)(2,1)S(1)}, u32[]{:S(2)}, u32[]{:S(2)}) %collective-permute-start.2) | collective-permute-done | bytes 524320 | tf_op jit(solution)/shard_map/ppermute | solution.py:266
  24.0 3.6 %collective-permute-done.5.refs_4_ = bf16[128,1024]{1,0:T(8,128)(2,1)S(1)} collective-permute-done((bf16[128,1024]{1,0:T(8,128)(2,1)S(1)}, bf16[128,1024]{1,0:T(8,128)(2,1)S(1)}, u32[]{:S(2)}, u32[]{:S(2)}) %collective-permute-start.5) | collective-permute-done | bytes 262176 | tf_op jit(solution)/shard_map/ppermute | solution.py:239
  27.6 1.6 %attend.5.refs_2_ = bf16[128,2048]{1,0:T(8,128)(2,1)S(1)} custom-call(s32[1]{0:T(128)} %bitcast.2.place_ref, f32[136,512]{1,0:T(8,128)S(1)} %weigh.1.weights_ref, bf16[128,2048]{1,0:T(8,128)(2,1)S(1)} %slice.22.q_ref, bf16[128,1024]{1,0:T(8,128)(2,1)S(1)} %pad_maximum_fusion.refs_0_, bf16[128,1024]{1,0:T(8,128)(2,1)S(1)} %collective-permute-done.1.refs_1_, ...), custom_call_target="tpu_custom_call" | custom-call | flops 134217728 | bytes 1572864 | tf_op jit(solution)/shard_map/attend/pallas_call | solution.py:121
  29.2 1.6 %attend.3.refs_0_ = bf16[128,2048]{1,0:T(8,128)(2,1)S(1)} custom-call(s32[1]{0:T(128)} %bitcast.2.place_ref, f32[136,512]{1,0:T(8,128)S(1)} %weigh.1.weights_ref, bf16[128,2048]{1,0:T(8,128)(2,1)S(1)} %collective-permute-done.2.q_ref, bf16[128,1024]{1,0:T(8,128)(2,1)S(1)} %pad_maximum_fusion.refs_0_, bf16[128,1024]{1,0:T(8,128)(2,1)S(1)} %collective-permute-done.1.refs_1_, ...), custom_call_target="tpu_custom_call" | custom-call | flops 134217728 | bytes 1572864 | tf_op jit(solution)/shard_map/attend/pallas_call | solution.py:121
  30.8 3.4 %collective-permute-done.9.refs_1_ = bf16[128,2048]{1,0:T(8,128)(2,1)} collective-permute-done((bf16[128,2048]{1,0:T(8,128)(2,1)S(1)}, bf16[128,2048]{1,0:T(8,128)(2,1)}, u32[]{:S(2)}, u32[]{:S(2)}) %collective-permute-start.9) | collective-permute-done | bytes 524320 | tf_op jit(solution)/shard_map/ppermute | solution.py:274
  34.2 2.3 %finish.1 = (bf16[128,4096]{1,0:T(8,128)(2,1)}, f32[32,128]{1,0:T(8,128)S(1)}) custom-call(s32[1]{0:T(128)} %bitcast.last_ref, bf16[128,4096]{1,0:T(8,128)(2,1)S(1)} %bitcast.7, bf16[128,2048]{1,0:T(8,128)(2,1)S(1)} %attend.3.refs_0_, bf16[128,2048]{1,0:T(8,128)(2,1)} %collective-permute-done.9.refs_1_, bf16[128,2048]{1,0:T(8,128)(2,1)S(1)} %attend.5.refs_2_, ...), custom_call_target="tpu_custom_call" | custom-call | flops 5242880 | bytes 4194304 | tf_op jit(solution)/shard_map/finish/pallas_call | solution.py:180
  36.6 1.2 %collective-permute-done.10 = f32[32,128]{1,0:T(8,128)S(1)} collective-permute-done((f32[32,128]{1,0:T(8,128)S(1)}, f32[32,128]{1,0:T(8,128)S(1)}, u32[]{:S(2)}, u32[]{:S(2)}) %collective-permute-start.10) | collective-permute-done | bytes 16416 | tf_op jit(solution)/shard_map/ppermute | solution.py:205
  37.7 1.5 %collective-permute-start.11 = (f32[32,128]{1,0:T(8,128)S(1)}, f32[32,128]{1,0:T(8,128)S(1)}, u32[]{:S(2)}, u32[]{:S(2)}) collective-permute-start(f32[32,128]{1,0:T(8,128)S(1)} %add.23), channel_id=1, source_target_pairs={{0,16},{1,17},{2,18},{3,19},{8,24},{9,25},{10,26},{11,27},{16,0},{... | collective-permute-start | bytes 49160 | tf_op jit(solution)/shard_map/ppermute | solution.py:226
  39.5 0.8 %collective-permute-start.13 = (f32[32,128]{1,0:T(8,128)S(1)}, f32[32,128]{1,0:T(8,128)S(1)}, u32[]{:S(2)}, u32[]{:S(2)}) collective-permute-start(f32[32,128]{1,0:T(8,128)S(1)} %add.23), channel_id=1, source_target_pairs={{0,2},{1,3},{2,0},{3,1},{8,26},{9,27},{10,24},{11,25},{16,18},{17,... | collective-permute-start | bytes 49160 | tf_op jit(solution)/shard_map/ppermute | solution.py:226
  40.3 3.3 %collective-permute-start.14 = (f32[32,128]{1,0:T(8,128)S(1)}, f32[32,128]{1,0:T(8,128)S(1)}, u32[]{:S(2)}, u32[]{:S(2)}) collective-permute-start(f32[32,128]{1,0:T(8,128)S(1)} %add.23), channel_id=1, source_target_pairs={{0,3},{1,2},{2,1},{3,0},{8,27},{9,26},{10,25},{11,24},{16,19},{17,... | collective-permute-start | bytes 49160 | tf_op jit(solution)/shard_map/ppermute | solution.py:226
  44.2 1.7 %collective-permute-done.14 = f32[32,128]{1,0:T(8,128)S(1)} collective-permute-done((f32[32,128]{1,0:T(8,128)S(1)}, f32[32,128]{1,0:T(8,128)S(1)}, u32[]{:S(2)}, u32[]{:S(2)}) %collective-permute-start.14) | collective-permute-done | bytes 16416 | tf_op jit(solution)/shard_map/ppermute | solution.py:226
  46.0 1.2 %collective-permute-done.15 = f32[32,128]{1,0:T(8,128)S(1)} collective-permute-done((f32[32,128]{1,0:T(8,128)S(1)}, f32[32,128]{1,0:T(8,128)S(1)}, u32[]{:S(2)}, u32[]{:S(2)}) %collective-permute-start.15) | collective-permute-done | bytes 16416 | tf_op jit(solution)/shard_map/ppermute | solution.py:205
  (33 shorter events, 3.0 us)
Async XLA Ops:
  0.6 8.4 %copy-start.1 = (bf16[1,1,128,4096]{3,2,1,0:T(8,128)(2,1)S(1)}, bf16[1,1,128,4096]{3,2,1,0:T(8,128)(2,1)}, u32[]{:S(2)}) copy-start(bf16[1,1,128,4096]{3,2,1,0:T(8,128)(2,1)} %param.6) | copy-start | bytes 3145732
  1.7 9.5 %collective-permute-start = (bf16[128,512]{1,0:T(8,128)(2,1)S(1)}, bf16[128,512]{1,0:T(8,128)(2,1)S(1)}, u32[]{:S(2)}, u32[]{:S(2)}) collective-permute-start(bf16[128,512]{1,0:T(8,128)(2,1)S(1)} %pad_maximum_fusion.1), channel_id=1, source_target_pairs={{0,4},{4,0},{1,5},{5,1},{2,6},{6,2},{3,7},{7,3},{8,12},{12,8},{9,1... | collective-permute-start | bytes 393224 | tf_op jit(solution)/shard_map/ppermute | solution.py:264
  4.7 7.4 %collective-permute-start.8 = (bf16[128,512]{1,0:T(8,128)(2,1)S(1)}, bf16[128,512]{1,0:T(8,128)(2,1)S(1)}, u32[]{:S(2)}, u32[]{:S(2)}) collective-permute-start(bf16[128,512]{1,0:T(8,128)(2,1)S(1)} %pad_maximum_fusion.2.refs_0_), channel_id=1, source_target_pairs={{0,8},{1,2},{2,1},{3,11},{8,0},{9,10},{10,9},{11,3},{16,24},{17,18... | collective-permute-start | bytes 393224 | tf_op jit(solution)/shard_map/ppermute | solution.py:239
  4.8 8.0 %collective-permute-start.6 = (bf16[128,512]{1,0:T(8,128)(2,1)S(1)}, bf16[128,512]{1,0:T(8,128)(2,1)S(1)}, u32[]{:S(2)}, u32[]{:S(2)}) collective-permute-start(bf16[128,512]{1,0:T(8,128)(2,1)S(1)} %pad_maximum_fusion.2.refs_0_), channel_id=1, source_target_pairs={{0,1},{1,0},{2,3},{3,2},{8,9},{9,8},{10,11},{11,10},{16,17},{17,16... | collective-permute-start | bytes 393224 | tf_op jit(solution)/shard_map/ppermute | solution.py:239
  7.9 8.4 %collective-permute-start.7 = (bf16[128,512]{1,0:T(8,128)(2,1)S(1)}, bf16[128,512]{1,0:T(8,128)(2,1)S(1)}, u32[]{:S(2)}, u32[]{:S(2)}) collective-permute-start(bf16[128,512]{1,0:T(8,128)(2,1)S(1)} %pad_maximum_fusion.2.refs_0_), channel_id=1, source_target_pairs={{0,2},{1,3},{2,0},{3,1},{8,10},{9,11},{10,8},{11,9},{16,18},{17,19... | collective-permute-start | bytes 393224 | tf_op jit(solution)/shard_map/ppermute | solution.py:239
  9.0 0.7 %copy-start.3 = (s32[1,4,4,4]{3,2,1,0:T(4,128)S(1)}, s32[1,4,4,4]{3,2,1,0:T(4,128)}, u32[]{:S(2)}) copy-start(s32[1,4,4,4]{3,2,1,0:T(4,128)} %lists_ref.1) | copy-start | bytes 772
  9.1 14.9 %collective-permute-start.2 = (bf16[128,2048]{1,0:T(8,128)(2,1)S(1)}, bf16[128,2048]{1,0:T(8,128)(2,1)S(1)}, u32[]{:S(2)}, u32[]{:S(2)}) collective-permute-start(bf16[128,2048]{1,0:T(8,128)(2,1)S(1)} %slice.22.q_ref), channel_id=1, source_target_pairs={{0,4},{4,0},{1,5},{5,1},{2,6},{6,2},{3,7},{7,3},{8,12},{12,8},{9,1... | collective-permute-start | bytes 1572872 | tf_op jit(solution)/shard_map/ppermute | solution.py:266
  9.7 0.7 %copy-start.4 = (s32[1,2]{1,0:T(1,128)S(1)}, s32[1,2]{1,0:T(1,128)}, u32[]{:S(2)}) copy-start(s32[1,2]{1,0:T(1,128)} %globals_ref.1) | copy-start | bytes 28
  9.7 0.7 %copy-start.5 = (s32[1,4]{1,0:T(1,128)S(1)}, s32[1,4]{1,0:T(1,128)}, u32[]{:S(2)}) copy-start(s32[1,4]{1,0:T(1,128)} %docs_ref.1) | copy-start | bytes 52
  11.2 11.5 %collective-permute-start.1 = (bf16[128,1024]{1,0:T(8,128)(2,1)S(1)}, bf16[128,1024]{1,0:T(8,128)(2,1)S(1)}, u32[]{:S(2)}, u32[]{:S(2)}) collective-permute-start(bf16[128,1024]{1,0:T(8,128)(2,1)S(1)} %pad_maximum_fusion.refs_0_), channel_id=1, source_target_pairs={{0,1},{1,0},{2,3},{3,2},{8,9},{9,8},{10,11},{11,10},{16,17},{17,16... | collective-permute-start | bytes 786440 | tf_op jit(solution)/shard_map/ppermute | solution.py:239
  12.1 8.3 %collective-permute-start.4 = (bf16[128,1024]{1,0:T(8,128)(2,1)S(1)}, bf16[128,1024]{1,0:T(8,128)(2,1)S(1)}, u32[]{:S(2)}, u32[]{:S(2)}) collective-permute-start(bf16[128,1024]{1,0:T(8,128)(2,1)S(1)} %pad_maximum_fusion.refs_0_), channel_id=1, source_target_pairs={{1,2},{2,1},{5,6},{6,5},{9,10},{10,9},{13,14},{14,13},{17,18},{18,... | collective-permute-start | bytes 786440 | tf_op jit(solution)/shard_map/ppermute | solution.py:276
  16.3 1.2 %copy-start.2 = (bf16[1,1,128,4096]{3,2,1,0:T(8,128)(2,1)S(1)}, bf16[1,1,128,4096]{3,2,1,0:T(8,128)(2,1)}, u32[]{:S(2)}) copy-start(bf16[1,1,128,4096]{3,2,1,0:T(8,128)(2,1)} %param.6) | copy-start | bytes 3145732
  19.6 14.6 %collective-permute-start.9 = (bf16[128,2048]{1,0:T(8,128)(2,1)S(1)}, bf16[128,2048]{1,0:T(8,128)(2,1)}, u32[]{:S(2)}, u32[]{:S(2)}) collective-permute-start(bf16[128,2048]{1,0:T(8,128)(2,1)S(1)} %attend.4.refs_3_), channel_id=1, source_target_pairs={{0,4},{4,0},{1,5},{5,1},{2,6},{6,2},{3,7},{7,3},{8,12},{12,8},{9,1... | collective-permute-start | bytes 1572872 | tf_op jit(solution)/shard_map/ppermute | solution.py:274
  20.4 7.2 %collective-permute-start.5 = (bf16[128,1024]{1,0:T(8,128)(2,1)S(1)}, bf16[128,1024]{1,0:T(8,128)(2,1)S(1)}, u32[]{:S(2)}, u32[]{:S(2)}) collective-permute-start(bf16[128,1024]{1,0:T(8,128)(2,1)S(1)} %collective-permute-done.4.refs_3_), channel_id=1, source_target_pairs={{0,1},{1,0},{2,3},{3,2},{8,9},{9,8},{10,11},{11,10},{16,17},{17,16... | collective-permute-start | bytes 786440 | tf_op jit(solution)/shard_map/ppermute | solution.py:239
  24.0 3.6 %collective-permute-start.3 = (bf16[128,1024]{1,0:T(8,128)(2,1)S(1)}, bf16[128,1024]{1,0:T(8,128)(2,1)S(1)}, u32[]{:S(2)}, u32[]{:S(2)}) collective-permute-start(bf16[128,1024]{1,0:T(8,128)(2,1)S(1)} %collective-permute-done.1.refs_1_), channel_id=1, source_target_pairs={{0,8},{1,2},{2,1},{3,11},{8,0},{9,10},{10,9},{11,3},{16,24},{17,18... | collective-permute-start | bytes 786440 | tf_op jit(solution)/shard_map/ppermute | solution.py:239
  29.2 5.0 %copy-start = (bf16[1,1,128,4096]{3,2,1,0:T(8,128)(2,1)S(1)}, bf16[1,1,128,4096]{3,2,1,0:T(8,128)(2,1)}, u32[]{:S(2)}) copy-start(bf16[1,1,128,4096]{3,2,1,0:T(8,128)(2,1)} %param.11) | copy-start | bytes 3145732
  36.5 1.2 %collective-permute-start.10 = (f32[32,128]{1,0:T(8,128)S(1)}, f32[32,128]{1,0:T(8,128)S(1)}, u32[]{:S(2)}, u32[]{:S(2)}) collective-permute-start(f32[32,128]{1,0:T(8,128)S(1)} %get-tuple-element.11), channel_id=1, source_target_pairs={{0,8},{8,0},{16,24},{24,16},{1,9},{9,1},{17,25},{25,17},{2,10},{10... | collective-permute-start | bytes 49160 | tf_op jit(solution)/shard_map/ppermute | solution.py:205
  37.7 5.9 %collective-permute-start.11 = (f32[32,128]{1,0:T(8,128)S(1)}, f32[32,128]{1,0:T(8,128)S(1)}, u32[]{:S(2)}, u32[]{:S(2)}) collective-permute-start(f32[32,128]{1,0:T(8,128)S(1)} %add.23), channel_id=1, source_target_pairs={{0,16},{1,17},{2,18},{3,19},{8,24},{9,25},{10,26},{11,27},{16,0},{... | collective-permute-start | bytes 49160 | tf_op jit(solution)/shard_map/ppermute | solution.py:226
  39.3 4.4 %collective-permute-start.12 = (f32[32,128]{1,0:T(8,128)S(1)}, f32[32,128]{1,0:T(8,128)S(1)}, u32[]{:S(2)}, u32[]{:S(2)}) collective-permute-start(f32[32,128]{1,0:T(8,128)S(1)} %add.23), channel_id=1, source_target_pairs={{0,1},{1,0},{2,3},{3,2},{8,25},{9,24},{10,27},{11,26},{16,17},{17,... | collective-permute-start | bytes 49160 | tf_op jit(solution)/shard_map/ppermute | solution.py:226
  39.5 4.7 %collective-permute-start.13 = (f32[32,128]{1,0:T(8,128)S(1)}, f32[32,128]{1,0:T(8,128)S(1)}, u32[]{:S(2)}, u32[]{:S(2)}) collective-permute-start(f32[32,128]{1,0:T(8,128)S(1)} %add.23), channel_id=1, source_target_pairs={{0,2},{1,3},{2,0},{3,1},{8,26},{9,27},{10,24},{11,25},{16,18},{17,... | collective-permute-start | bytes 49160 | tf_op jit(solution)/shard_map/ppermute | solution.py:226
  40.3 5.5 %collective-permute-start.14 = (f32[32,128]{1,0:T(8,128)S(1)}, f32[32,128]{1,0:T(8,128)S(1)}, u32[]{:S(2)}, u32[]{:S(2)}) collective-permute-start(f32[32,128]{1,0:T(8,128)S(1)} %add.23), channel_id=1, source_target_pairs={{0,3},{1,2},{2,1},{3,0},{8,27},{9,26},{10,25},{11,24},{16,19},{17,... | collective-permute-start | bytes 49160 | tf_op jit(solution)/shard_map/ppermute | solution.py:226
  45.9 1.2 %collective-permute-start.15 = (f32[32,128]{1,0:T(8,128)S(1)}, f32[32,128]{1,0:T(8,128)S(1)}, u32[]{:S(2)}, u32[]{:S(2)}) collective-permute-start(f32[32,128]{1,0:T(8,128)S(1)} %add_add_fusion), channel_id=1, source_target_pairs={{0,8},{8,0},{16,24},{24,16},{1,9},{9,1},{17,25},{25,17},{2,10},{10... | collective-permute-start | bytes 49160 | tf_op jit(solution)/shard_map/ppermute | solution.py:205

commit v7 on v6

--- a/solution.py
+++ b/solution.py
@@ -17,6 +17,7 @@
 EARLY = 2
 GROUPS = (range(EARLY), range(EARLY, KVH))
 PARTS = len(GROUPS)
+LAST_COPIES = 2
 NEVER = -1e30
 LEVELS = 8
 SCALE = math.log2(math.e) / math.sqrt(HD)
@@ -141,21 +142,24 @@
 
 def finish_kernel(scale, last_ref, cotangent_ref, *refs):
     arrived_refs, handed_refs = refs[:PARTS], refs[PARTS : 2 * PARTS]
-    out_ref, share_ref, cotangent, stream, arrived_last, sems = refs[2 * PARTS :]
+    out_ref, share_ref, stream, arrived_last, sems = refs[2 * PARTS :]
     rows, features = stream.shape
-    last_copy = pltpu.make_async_copy(arrived_refs[-1], arrived_last, sems.at[0])
-    last_copy.start()
-    cotangent_copy = pltpu.make_async_copy(cotangent_ref, cotangent, sems.at[1])
-    cotangent_copy.start()
+    last_copies = []
+    for index in range(LAST_COPIES):
+        columns = pl.ds(index * (arrived_last.shape[1] // LAST_COPIES), arrived_last.shape[1] // LAST_COPIES)
+        source = arrived_refs[-1].at[:, columns]
+        last_copies.append(pltpu.make_async_copy(source, arrived_last.at[:, columns], sems.at[2 + index]))
+        last_copies[-1].start()
     is_last = last_ref[0] == 1
     squares = jnp.zeros((rows, HD), jnp.float32)
     done = 0
     for part in range(PARTS):
         source = arrived_refs[part]
         if part == PARTS - 1:
-            last_copy.wait()
             source = arrived_last
         for column in range(0, source.shape[1], HD):
+            if part == PARTS - 1 and column % (source.shape[1] // LAST_COPIES) == 0:
+                last_copies[column // (source.shape[1] // LAST_COPIES)].wait()
             handed = handed_refs[part][:, pl.ds(column, HD)].astype(jnp.float32)
             arrived = source[:, pl.ds(column, HD)].astype(jnp.float32)
             total = jnp.where(is_last, handed + arrived, handed).astype(jnp.bfloat16)
@@ -163,14 +167,13 @@
             widened = total.astype(jnp.float32)
             squares += widened * widened
         done += source.shape[1]
-    store_copy = pltpu.make_async_copy(stream, out_ref, sems.at[2])
+    store_copy = pltpu.make_async_copy(stream, out_ref, sems.at[0])
     store_copy.start()
     mean = jnp.sum(squares, axis=1, keepdims=True) / features
     inverse = lax.rsqrt(mean + 1e-06) * scale
-    cotangent_copy.wait()
     for tile in range(features // HD):
         columns = pl.ds(tile * HD, HD)
-        term = cotangent[:, columns].astype(jnp.float32) * stream[:, columns].astype(jnp.float32)
+        term = cotangent_ref[:, columns].astype(jnp.float32) * stream[:, columns].astype(jnp.float32)
         share_ref[pl.ds(tile, 1), :] = jnp.sum(term * inverse, axis=0, keepdims=True)
     store_copy.wait()
 
@@ -183,13 +186,12 @@
             jax.ShapeDtypeStruct((rows, features), jnp.bfloat16),
             jax.ShapeDtypeStruct((features // HD, HD), jnp.float32),
         ),
-        in_specs=[SMEM, ANY] + [VMEM] * (PARTS - 1) + [ANY] + [VMEM] * PARTS,
+        in_specs=[SMEM, VMEM] + [VMEM] * (PARTS - 1) + [ANY] + [VMEM] * PARTS,
         out_specs=(ANY, VMEM),
         scratch_shapes=[
             pltpu.VMEM((rows, features), jnp.bfloat16),
-            pltpu.VMEM((rows, features), jnp.bfloat16),
             pltpu.VMEM(arrived[-1].shape, jnp.bfloat16),
-            pltpu.SemaphoreType.DMA((3,)),
+            pltpu.SemaphoreType.DMA((2 + LAST_COPIES,)),
         ],
         compiler_params=pltpu.CompilerParams(vmem_limit_bytes=16 << 20),
         cost_estimate=pl.CostEstimate(

time: 48 us -> 48 us (level)
  no operation moved by 1% of the time
where the time goes in v7:
time: 48 us; the launch traced here: 47.7 us
  starting transfers between devices  18.6 us (39%)
  waiting for transfers between devices  16.4 us (34%)
  Pallas kernels  8.32 us (17%)
  local copies, waits for them, and re-layouts  2.99 us (6%)
  between operations  0.78 us (2%)
  other arithmetic  0.66 us (1%)
    ppermute x6, starting transfers between devices, fetch(): return lax.ppermute(value, ('dp', 'ctx'), pairs)  7.48 us
    ppermute x6, waiting for transfers between devices, fetch(): return lax.ppermute(value, ('dp', 'ctx'), pairs)  7.18 us
    ppermute x4, starting transfers between devices, total_share(): heard.append(lax.ppermute(value, ('dp', 'ctx'), pairs))  5.91 us
    pallas_call x3, Pallas kernels, attend(): pl.pallas_call(functools.partial(attend_kernel, heads, query_base, key_ba...  5.27 us
    ppermute x1, waiting for transfers between devices, per_device(): arrived_late = lax.ppermute(late, 'section', first_hop)  3.4 us
    ppermute x1, starting transfers between devices, per_device(): early_kv = lax.ppermute(kv_parts[0], 'section', first_hop)  3 us
    ppermute x2, waiting for transfers between devices, swapped_sum(): lax.ppermute(value, axis, [(place, place ^ distance) for place in range(c...  2.34 us
    pallas_call x1, Pallas kernels, finish(): pl.pallas_call(functools.partial(finish_kernel, scale), out_shape=(jax.Sh...  2.24 us
  transfers between devices with their start and end apart: 16, of which 8 were waited for; matrix products, arithmetic and copies ran while one was open for 0% of the time, Pallas kernels for 13%

profile of v7, /device:TPU:0, one launch (start us, length us, event | category | flops | bytes accessed | tf_op | source)
XLA Modules:
  0.0 47.7 jit_solution(3242755517341342875)
XLA Ops:
  0.6 1.0 %fusion = (bf16[128,256]{1,0:T(8,128)(2,1)S(1)}, bf16[128,256]{1,0:T(8,128)(2,1)S(1)}, bf16[128,256]{1,0:T(8,128)(2,1)S(1)}, bf16[128,256]{1,0:T(8,128)(2,1)S(1)}) fusion(bf16[128,1024]{1,0:T(8,128)(2,1)} %bitcast.10), kind=kLoop, calls=%fused_computation.4 | loop fusion | bytes 524288 | tf_op jit(solution)/shard_map/slice | solution.py:264
  1.7 3.0 %collective-permute-start = (bf16[128,512]{1,0:T(8,128)(2,1)S(1)}, bf16[128,512]{1,0:T(8,128)(2,1)S(1)}, u32[]{:S(2)}, u32[]{:S(2)}) collective-permute-start(bf16[128,512]{1,0:T(8,128)(2,1)S(1)} %pad_maximum_fusion.1), channel_id=1, source_target_pairs={{0,4},{4,0},{1,5},{5,1},{2,6},{6,2},{3,7},{7,3},{8,12},{12,8},{9,1... | collective-permute-start | bytes 393224 | tf_op jit(solution)/shard_map/ppermute | solution.py:266
  4.8 3.1 %collective-permute-start.6 = (bf16[128,512]{1,0:T(8,128)(2,1)S(1)}, bf16[128,512]{1,0:T(8,128)(2,1)S(1)}, u32[]{:S(2)}, u32[]{:S(2)}) collective-permute-start(bf16[128,512]{1,0:T(8,128)(2,1)S(1)} %pad_maximum_fusion.2.refs_0_), channel_id=1, source_target_pairs={{0,1},{1,0},{2,3},{3,2},{8,9},{9,8},{10,11},{11,10},{16,17},{17,16... | collective-permute-start | bytes 393224 | tf_op jit(solution)/shard_map/ppermute | solution.py:241
  7.9 1.1 %collective-permute-start.7 = (bf16[128,512]{1,0:T(8,128)(2,1)S(1)}, bf16[128,512]{1,0:T(8,128)(2,1)S(1)}, u32[]{:S(2)}, u32[]{:S(2)}) collective-permute-start(bf16[128,512]{1,0:T(8,128)(2,1)S(1)} %pad_maximum_fusion.2.refs_0_), channel_id=1, source_target_pairs={{0,2},{1,3},{2,0},{3,1},{8,10},{9,11},{10,8},{11,9},{16,18},{17,19... | collective-permute-start | bytes 393224 | tf_op jit(solution)/shard_map/ppermute | solution.py:241
  10.4 0.8 %weigh.1.weights_ref = f32[136,512]{1,0:T(8,128)S(1)} custom-call(s32[1]{0:T(128)} %bitcast.2.place_ref, s32[1,4,4,4]{3,2,1,0:T(4,128)S(1)} %copy-done.3, s32[1,2]{1,0:T(1,128)S(1)} %copy-done.4, s32[1,4]{1,0:T(1,128)S(1)} %copy-done.5), custom_call_target="tpu_custom_call" | custom-call | tf_op jit(solution)/shard_map/weigh/pallas_call | solution.py:62
  11.2 0.9 %collective-permute-start.1 = (bf16[128,1024]{1,0:T(8,128)(2,1)S(1)}, bf16[128,1024]{1,0:T(8,128)(2,1)S(1)}, u32[]{:S(2)}, u32[]{:S(2)}) collective-permute-start(bf16[128,1024]{1,0:T(8,128)(2,1)S(1)} %pad_maximum_fusion.refs_0_), channel_id=1, source_target_pairs={{0,1},{1,0},{2,3},{3,2},{8,9},{9,8},{10,11},{11,10},{16,17},{17,16... | collective-permute-start | bytes 786440 | tf_op jit(solution)/shard_map/ppermute | solution.py:241
  12.1 0.7 %collective-permute-start.4 = (bf16[128,1024]{1,0:T(8,128)(2,1)S(1)}, bf16[128,1024]{1,0:T(8,128)(2,1)S(1)}, u32[]{:S(2)}, u32[]{:S(2)}) collective-permute-start(bf16[128,1024]{1,0:T(8,128)(2,1)S(1)} %pad_maximum_fusion.refs_0_), channel_id=1, source_target_pairs={{1,2},{2,1},{5,6},{6,5},{9,10},{10,9},{13,14},{14,13},{17,18},{18,... | collective-permute-start | bytes 786440 | tf_op jit(solution)/shard_map/ppermute | solution.py:278
  12.8 3.5 %collective-permute-done.7.refs_2_ = bf16[128,512]{1,0:T(8,128)(2,1)S(1)} collective-permute-done((bf16[128,512]{1,0:T(8,128)(2,1)S(1)}, bf16[128,512]{1,0:T(8,128)(2,1)S(1)}, u32[]{:S(2)}, u32[]{:S(2)}) %collective-permute-start.7) | collective-permute-done | bytes 131104 | tf_op jit(solution)/shard_map/ppermute | solution.py:241
  16.3 1.2 %copy-done.2 = bf16[1,1,128,4096]{3,2,1,0:T(8,128)(2,1)S(1)} copy-done((bf16[1,1,128,4096]{3,2,1,0:T(8,128)(2,1)S(1)}, bf16[1,1,128,4096]{3,2,1,0:T(8,128)(2,1)}, u32[]{:S(2)}) %copy-start.2) | copy-done | bytes 1048600
  17.5 2.1 %attend.4.refs_3_ = bf16[128,2048]{1,0:T(8,128)(2,1)S(1)} custom-call(s32[1]{0:T(128)} %bitcast.2.place_ref, f32[136,512]{1,0:T(8,128)S(1)} %weigh.1.weights_ref, bf16[128,4096]{1,0:T(8,128)(2,1)S(1)} %bitcast.9, bf16[128,512]{1,0:T(8,128)(2,1)S(1)} %pad_maximum_fusion.2.refs_0_, bf16[128,512]{1,0:T(8,128)(2,1)S(1)} %collective-permute-done.6.refs_1_, ...), custom_call_target="tpu_custom_call" | custom-call | flops 16106127360 | bytes 1572864 | tf_op jit(solution)/shard_map/attend/pallas_call | solution.py:122
  19.6 0.8 %collective-permute-start.9 = (bf16[128,2048]{1,0:T(8,128)(2,1)S(1)}, bf16[128,2048]{1,0:T(8,128)(2,1)}, u32[]{:S(2)}, u32[]{:S(2)}) collective-permute-start(bf16[128,2048]{1,0:T(8,128)(2,1)S(1)} %attend.4.refs_3_), channel_id=1, source_target_pairs={{0,4},{4,0},{1,5},{5,1},{2,6},{6,2},{3,7},{7,3},{8,12},{12,8},{9,1... | collective-permute-start | bytes 1572872 | tf_op jit(solution)/shard_map/ppermute | solution.py:276
  20.4 2.3 %collective-permute-start.5 = (bf16[128,1024]{1,0:T(8,128)(2,1)S(1)}, bf16[128,1024]{1,0:T(8,128)(2,1)S(1)}, u32[]{:S(2)}, u32[]{:S(2)}) collective-permute-start(bf16[128,1024]{1,0:T(8,128)(2,1)S(1)} %collective-permute-done.4.refs_3_), channel_id=1, source_target_pairs={{0,1},{1,0},{2,3},{3,2},{8,9},{9,8},{10,11},{11,10},{16,17},{17,16... | collective-permute-start | bytes 786440 | tf_op jit(solution)/shard_map/ppermute | solution.py:241
  22.7 1.2 %collective-permute-done.2.q_ref = bf16[128,2048]{1,0:T(8,128)(2,1)S(1)} collective-permute-done((bf16[128,2048]{1,0:T(8,128)(2,1)S(1)}, bf16[128,2048]{1,0:T(8,128)(2,1)S(1)}, u32[]{:S(2)}, u32[]{:S(2)}) %collective-permute-start.2) | collective-permute-done | bytes 524320 | tf_op jit(solution)/shard_map/ppermute | solution.py:268
  24.0 3.6 %collective-permute-done.5.refs_4_ = bf16[128,1024]{1,0:T(8,128)(2,1)S(1)} collective-permute-done((bf16[128,1024]{1,0:T(8,128)(2,1)S(1)}, bf16[128,1024]{1,0:T(8,128)(2,1)S(1)}, u32[]{:S(2)}, u32[]{:S(2)}) %collective-permute-start.5) | collective-permute-done | bytes 262176 | tf_op jit(solution)/shard_map/ppermute | solution.py:241
  27.6 1.6 %attend.5.refs_2_ = bf16[128,2048]{1,0:T(8,128)(2,1)S(1)} custom-call(s32[1]{0:T(128)} %bitcast.2.place_ref, f32[136,512]{1,0:T(8,128)S(1)} %weigh.1.weights_ref, bf16[128,2048]{1,0:T(8,128)(2,1)S(1)} %slice.22.q_ref, bf16[128,1024]{1,0:T(8,128)(2,1)S(1)} %pad_maximum_fusion.refs_0_, bf16[128,1024]{1,0:T(8,128)(2,1)S(1)} %collective-permute-done.1.refs_1_, ...), custom_call_target="tpu_custom_call" | custom-call | flops 134217728 | bytes 1572864 | tf_op jit(solution)/shard_map/attend/pallas_call | solution.py:122
  29.2 1.6 %attend.3.refs_0_ = bf16[128,2048]{1,0:T(8,128)(2,1)S(1)} custom-call(s32[1]{0:T(128)} %bitcast.2.place_ref, f32[136,512]{1,0:T(8,128)S(1)} %weigh.1.weights_ref, bf16[128,2048]{1,0:T(8,128)(2,1)S(1)} %collective-permute-done.2.q_ref, bf16[128,1024]{1,0:T(8,128)(2,1)S(1)} %pad_maximum_fusion.refs_0_, bf16[128,1024]{1,0:T(8,128)(2,1)S(1)} %collective-permute-done.1.refs_1_, ...), custom_call_target="tpu_custom_call" | custom-call | flops 134217728 | bytes 1572864 | tf_op jit(solution)/shard_map/attend/pallas_call | solution.py:122
  30.8 3.4 %collective-permute-done.9.refs_1_ = bf16[128,2048]{1,0:T(8,128)(2,1)} collective-permute-done((bf16[128,2048]{1,0:T(8,128)(2,1)S(1)}, bf16[128,2048]{1,0:T(8,128)(2,1)}, u32[]{:S(2)}, u32[]{:S(2)}) %collective-permute-start.9) | collective-permute-done | bytes 524320 | tf_op jit(solution)/shard_map/ppermute | solution.py:276
  34.2 2.2 %finish.1 = (bf16[128,4096]{1,0:T(8,128)(2,1)}, f32[32,128]{1,0:T(8,128)S(1)}) custom-call(s32[1]{0:T(128)} %bitcast.last_ref, bf16[128,4096]{1,0:T(8,128)(2,1)S(1)} %bitcast.7, bf16[128,2048]{1,0:T(8,128)(2,1)S(1)} %attend.3.refs_0_, bf16[128,2048]{1,0:T(8,128)(2,1)} %collective-permute-done.9.refs_1_, bf16[128,2048]{1,0:T(8,128)(2,1)S(1)} %attend.5.refs_2_, ...), custom_call_target="tpu_custom_call" | custom-call | flops 5242880 | bytes 4194304 | tf_op jit(solution)/shard_map/finish/pallas_call | solution.py:183
  36.5 1.2 %collective-permute-done.10 = f32[32,128]{1,0:T(8,128)S(1)} collective-permute-done((f32[32,128]{1,0:T(8,128)S(1)}, f32[32,128]{1,0:T(8,128)S(1)}, u32[]{:S(2)}, u32[]{:S(2)}) %collective-permute-start.10) | collective-permute-done | bytes 16416 | tf_op jit(solution)/shard_map/ppermute | solution.py:207
  37.7 1.5 %collective-permute-start.11 = (f32[32,128]{1,0:T(8,128)S(1)}, f32[32,128]{1,0:T(8,128)S(1)}, u32[]{:S(2)}, u32[]{:S(2)}) collective-permute-start(f32[32,128]{1,0:T(8,128)S(1)} %add.23), channel_id=1, source_target_pairs={{0,16},{1,17},{2,18},{3,19},{8,24},{9,25},{10,26},{11,27},{16,0},{... | collective-permute-start | bytes 49160 | tf_op jit(solution)/shard_map/ppermute | solution.py:228
  39.5 0.8 %collective-permute-start.13 = (f32[32,128]{1,0:T(8,128)S(1)}, f32[32,128]{1,0:T(8,128)S(1)}, u32[]{:S(2)}, u32[]{:S(2)}) collective-permute-start(f32[32,128]{1,0:T(8,128)S(1)} %add.23), channel_id=1, source_target_pairs={{0,2},{1,3},{2,0},{3,1},{8,26},{9,27},{10,24},{11,25},{16,18},{17,... | collective-permute-start | bytes 49160 | tf_op jit(solution)/shard_map/ppermute | solution.py:228
  40.3 3.3 %collective-permute-start.14 = (f32[32,128]{1,0:T(8,128)S(1)}, f32[32,128]{1,0:T(8,128)S(1)}, u32[]{:S(2)}, u32[]{:S(2)}) collective-permute-start(f32[32,128]{1,0:T(8,128)S(1)} %add.23), channel_id=1, source_target_pairs={{0,3},{1,2},{2,1},{3,0},{8,27},{9,26},{10,25},{11,24},{16,19},{17,... | collective-permute-start | bytes 49160 | tf_op jit(solution)/shard_map/ppermute | solution.py:228
  44.2 1.7 %collective-permute-done.14 = f32[32,128]{1,0:T(8,128)S(1)} collective-permute-done((f32[32,128]{1,0:T(8,128)S(1)}, f32[32,128]{1,0:T(8,128)S(1)}, u32[]{:S(2)}, u32[]{:S(2)}) %collective-permute-start.14) | collective-permute-done | bytes 16416 | tf_op jit(solution)/shard_map/ppermute | solution.py:228
  45.9 1.2 %collective-permute-done.15 = f32[32,128]{1,0:T(8,128)S(1)} collective-permute-done((f32[32,128]{1,0:T(8,128)S(1)}, f32[32,128]{1,0:T(8,128)S(1)}, u32[]{:S(2)}, u32[]{:S(2)}) %collective-permute-start.15) | collective-permute-done | bytes 16416 | tf_op jit(solution)/shard_map/ppermute | solution.py:207
  (33 shorter events, 3.0 us)
Async XLA Ops:
  0.6 8.4 %copy-start.1 = (bf16[1,1,128,4096]{3,2,1,0:T(8,128)(2,1)S(1)}, bf16[1,1,128,4096]{3,2,1,0:T(8,128)(2,1)}, u32[]{:S(2)}) copy-start(bf16[1,1,128,4096]{3,2,1,0:T(8,128)(2,1)} %param.6) | copy-start | bytes 3145732
  1.7 9.5 %collective-permute-start = (bf16[128,512]{1,0:T(8,128)(2,1)S(1)}, bf16[128,512]{1,0:T(8,128)(2,1)S(1)}, u32[]{:S(2)}, u32[]{:S(2)}) collective-permute-start(bf16[128,512]{1,0:T(8,128)(2,1)S(1)} %pad_maximum_fusion.1), channel_id=1, source_target_pairs={{0,4},{4,0},{1,5},{5,1},{2,6},{6,2},{3,7},{7,3},{8,12},{12,8},{9,1... | collective-permute-start | bytes 393224 | tf_op jit(solution)/shard_map/ppermute | solution.py:266
  4.7 7.4 %collective-permute-start.8 = (bf16[128,512]{1,0:T(8,128)(2,1)S(1)}, bf16[128,512]{1,0:T(8,128)(2,1)S(1)}, u32[]{:S(2)}, u32[]{:S(2)}) collective-permute-start(bf16[128,512]{1,0:T(8,128)(2,1)S(1)} %pad_maximum_fusion.2.refs_0_), channel_id=1, source_target_pairs={{0,8},{1,2},{2,1},{3,11},{8,0},{9,10},{10,9},{11,3},{16,24},{17,18... | collective-permute-start | bytes 393224 | tf_op jit(solution)/shard_map/ppermute | solution.py:241
  4.8 8.0 %collective-permute-start.6 = (bf16[128,512]{1,0:T(8,128)(2,1)S(1)}, bf16[128,512]{1,0:T(8,128)(2,1)S(1)}, u32[]{:S(2)}, u32[]{:S(2)}) collective-permute-start(bf16[128,512]{1,0:T(8,128)(2,1)S(1)} %pad_maximum_fusion.2.refs_0_), channel_id=1, source_target_pairs={{0,1},{1,0},{2,3},{3,2},{8,9},{9,8},{10,11},{11,10},{16,17},{17,16... | collective-permute-start | bytes 393224 | tf_op jit(solution)/shard_map/ppermute | solution.py:241
  7.9 8.4 %collective-permute-start.7 = (bf16[128,512]{1,0:T(8,128)(2,1)S(1)}, bf16[128,512]{1,0:T(8,128)(2,1)S(1)}, u32[]{:S(2)}, u32[]{:S(2)}) collective-permute-start(bf16[128,512]{1,0:T(8,128)(2,1)S(1)} %pad_maximum_fusion.2.refs_0_), channel_id=1, source_target_pairs={{0,2},{1,3},{2,0},{3,1},{8,10},{9,11},{10,8},{11,9},{16,18},{17,19... | collective-permute-start | bytes 393224 | tf_op jit(solution)/shard_map/ppermute | solution.py:241
  9.0 0.7 %copy-start.3 = (s32[1,4,4,4]{3,2,1,0:T(4,128)S(1)}, s32[1,4,4,4]{3,2,1,0:T(4,128)}, u32[]{:S(2)}) copy-start(s32[1,4,4,4]{3,2,1,0:T(4,128)} %lists_ref.1) | copy-start | bytes 772
  9.1 14.9 %collective-permute-start.2 = (bf16[128,2048]{1,0:T(8,128)(2,1)S(1)}, bf16[128,2048]{1,0:T(8,128)(2,1)S(1)}, u32[]{:S(2)}, u32[]{:S(2)}) collective-permute-start(bf16[128,2048]{1,0:T(8,128)(2,1)S(1)} %slice.22.q_ref), channel_id=1, source_target_pairs={{0,4},{4,0},{1,5},{5,1},{2,6},{6,2},{3,7},{7,3},{8,12},{12,8},{9,1... | collective-permute-start | bytes 1572872 | tf_op jit(solution)/shard_map/ppermute | solution.py:268
  9.7 0.7 %copy-start.4 = (s32[1,2]{1,0:T(1,128)S(1)}, s32[1,2]{1,0:T(1,128)}, u32[]{:S(2)}) copy-start(s32[1,2]{1,0:T(1,128)} %globals_ref.1) | copy-start | bytes 28
  9.7 0.7 %copy-start.5 = (s32[1,4]{1,0:T(1,128)S(1)}, s32[1,4]{1,0:T(1,128)}, u32[]{:S(2)}) copy-start(s32[1,4]{1,0:T(1,128)} %docs_ref.1) | copy-start | bytes 52
  11.2 11.5 %collective-permute-start.1 = (bf16[128,1024]{1,0:T(8,128)(2,1)S(1)}, bf16[128,1024]{1,0:T(8,128)(2,1)S(1)}, u32[]{:S(2)}, u32[]{:S(2)}) collective-permute-start(bf16[128,1024]{1,0:T(8,128)(2,1)S(1)} %pad_maximum_fusion.refs_0_), channel_id=1, source_target_pairs={{0,1},{1,0},{2,3},{3,2},{8,9},{9,8},{10,11},{11,10},{16,17},{17,16... | collective-permute-start | bytes 786440 | tf_op jit(solution)/shard_map/ppermute | solution.py:241
  12.1 8.3 %collective-permute-start.4 = (bf16[128,1024]{1,0:T(8,128)(2,1)S(1)}, bf16[128,1024]{1,0:T(8,128)(2,1)S(1)}, u32[]{:S(2)}, u32[]{:S(2)}) collective-permute-start(bf16[128,1024]{1,0:T(8,128)(2,1)S(1)} %pad_maximum_fusion.refs_0_), channel_id=1, source_target_pairs={{1,2},{2,1},{5,6},{6,5},{9,10},{10,9},{13,14},{14,13},{17,18},{18,... | collective-permute-start | bytes 786440 | tf_op jit(solution)/shard_map/ppermute | solution.py:278
  16.3 1.2 %copy-start.2 = (bf16[1,1,128,4096]{3,2,1,0:T(8,128)(2,1)S(1)}, bf16[1,1,128,4096]{3,2,1,0:T(8,128)(2,1)}, u32[]{:S(2)}) copy-start(bf16[1,1,128,4096]{3,2,1,0:T(8,128)(2,1)} %param.6) | copy-start | bytes 3145732
  19.6 14.6 %collective-permute-start.9 = (bf16[128,2048]{1,0:T(8,128)(2,1)S(1)}, bf16[128,2048]{1,0:T(8,128)(2,1)}, u32[]{:S(2)}, u32[]{:S(2)}) collective-permute-start(bf16[128,2048]{1,0:T(8,128)(2,1)S(1)} %attend.4.refs_3_), channel_id=1, source_target_pairs={{0,4},{4,0},{1,5},{5,1},{2,6},{6,2},{3,7},{7,3},{8,12},{12,8},{9,1... | collective-permute-start | bytes 1572872 | tf_op jit(solution)/shard_map/ppermute | solution.py:276
  20.4 7.2 %collective-permute-start.5 = (bf16[128,1024]{1,0:T(8,128)(2,1)S(1)}, bf16[128,1024]{1,0:T(8,128)(2,1)S(1)}, u32[]{:S(2)}, u32[]{:S(2)}) collective-permute-start(bf16[128,1024]{1,0:T(8,128)(2,1)S(1)} %collective-permute-done.4.refs_3_), channel_id=1, source_target_pairs={{0,1},{1,0},{2,3},{3,2},{8,9},{9,8},{10,11},{11,10},{16,17},{17,16... | collective-permute-start | bytes 786440 | tf_op jit(solution)/shard_map/ppermute | solution.py:241
  24.0 3.6 %collective-permute-start.3 = (bf16[128,1024]{1,0:T(8,128)(2,1)S(1)}, bf16[128,1024]{1,0:T(8,128)(2,1)S(1)}, u32[]{:S(2)}, u32[]{:S(2)}) collective-permute-start(bf16[128,1024]{1,0:T(8,128)(2,1)S(1)} %collective-permute-done.1.refs_1_), channel_id=1, source_target_pairs={{0,8},{1,2},{2,1},{3,11},{8,0},{9,10},{10,9},{11,3},{16,24},{17,18... | collective-permute-start | bytes 786440 | tf_op jit(solution)/shard_map/ppermute | solution.py:241
  29.2 5.0 %copy-start = (bf16[1,1,128,4096]{3,2,1,0:T(8,128)(2,1)S(1)}, bf16[1,1,128,4096]{3,2,1,0:T(8,128)(2,1)}, u32[]{:S(2)}) copy-start(bf16[1,1,128,4096]{3,2,1,0:T(8,128)(2,1)} %param.11) | copy-start | bytes 3145732
  36.5 1.2 %collective-permute-start.10 = (f32[32,128]{1,0:T(8,128)S(1)}, f32[32,128]{1,0:T(8,128)S(1)}, u32[]{:S(2)}, u32[]{:S(2)}) collective-permute-start(f32[32,128]{1,0:T(8,128)S(1)} %get-tuple-element.11), channel_id=1, source_target_pairs={{0,8},{8,0},{16,24},{24,16},{1,9},{9,1},{17,25},{25,17},{2,10},{10... | collective-permute-start | bytes 49160 | tf_op jit(solution)/shard_map/ppermute | solution.py:207
  37.7 5.9 %collective-permute-start.11 = (f32[32,128]{1,0:T(8,128)S(1)}, f32[32,128]{1,0:T(8,128)S(1)}, u32[]{:S(2)}, u32[]{:S(2)}) collective-permute-start(f32[32,128]{1,0:T(8,128)S(1)} %add.23), channel_id=1, source_target_pairs={{0,16},{1,17},{2,18},{3,19},{8,24},{9,25},{10,26},{11,27},{16,0},{... | collective-permute-start | bytes 49160 | tf_op jit(solution)/shard_map/ppermute | solution.py:228
  39.2 4.4 %collective-permute-start.12 = (f32[32,128]{1,0:T(8,128)S(1)}, f32[32,128]{1,0:T(8,128)S(1)}, u32[]{:S(2)}, u32[]{:S(2)}) collective-permute-start(f32[32,128]{1,0:T(8,128)S(1)} %add.23), channel_id=1, source_target_pairs={{0,1},{1,0},{2,3},{3,2},{8,25},{9,24},{10,27},{11,26},{16,17},{17,... | collective-permute-start | bytes 49160 | tf_op jit(solution)/shard_map/ppermute | solution.py:228
  39.5 4.7 %collective-permute-start.13 = (f32[32,128]{1,0:T(8,128)S(1)}, f32[32,128]{1,0:T(8,128)S(1)}, u32[]{:S(2)}, u32[]{:S(2)}) collective-permute-start(f32[32,128]{1,0:T(8,128)S(1)} %add.23), channel_id=1, source_target_pairs={{0,2},{1,3},{2,0},{3,1},{8,26},{9,27},{10,24},{11,25},{16,18},{17,... | collective-permute-start | bytes 49160 | tf_op jit(solution)/shard_map/ppermute | solution.py:228
  40.3 5.5 %collective-permute-start.14 = (f32[32,128]{1,0:T(8,128)S(1)}, f32[32,128]{1,0:T(8,128)S(1)}, u32[]{:S(2)}, u32[]{:S(2)}) collective-permute-start(f32[32,128]{1,0:T(8,128)S(1)} %add.23), channel_id=1, source_target_pairs={{0,3},{1,2},{2,1},{3,0},{8,27},{9,26},{10,25},{11,24},{16,19},{17,... | collective-permute-start | bytes 49160 | tf_op jit(solution)/shard_map/ppermute | solution.py:228
  45.8 1.2 %collective-permute-start.15 = (f32[32,128]{1,0:T(8,128)S(1)}, f32[32,128]{1,0:T(8,128)S(1)}, u32[]{:S(2)}, u32[]{:S(2)}) collective-permute-start(f32[32,128]{1,0:T(8,128)S(1)} %add_add_fusion), channel_id=1, source_target_pairs={{0,8},{8,0},{16,24},{24,16},{1,9},{9,1},{17,25},{25,17},{2,10},{10... | collective-permute-start | bytes 49160 | tf_op jit(solution)/shard_map/ppermute | solution.py:207
